TPU v7x, 32 devices: a whole 2x2x4 slice. The times are simulated.
32 devices in a mesh: space: 8 (over z, y), dp: 4 (over x, core).
Axes of the slice: x: 2, y: 2, z: 4, core: 2. Of those that a mesh axis runs over, the one named last changes fastest.
Arguments:
- features: bfloat16 [4, 8, 512, 128], P('dp', 'space'), may hold values from -6 to 6
- occupancy: int32 [4, 8, 512], P('dp', 'space'), may hold values from 0 to 1, as said below
- labels: int32 [4, 8, 512], P('dp', 'space'), may hold values from 0 to 2
- rulebook: int32 [4, 8, 27], P('dp', 'space'), may hold values from 0 to 3, as said below
- filter_one: bfloat16 [27, 128, 128], replicated, may hold values from -0.109375 to 0.109375
- filter_two: bfloat16 [27, 128, 128], replicated, may hold values from -0.109375 to 0.109375
- head_weight: bfloat16 [128, 3], replicated, may hold values from -1.5 to 1.5
Outputs:
- grad_filter_one: float32 [27, 128, 128], replicated
- grad_filter_two: float32 [27, 128, 128], replicated
- grad_head: float32 [128, 3], replicated
- mean_loss: float32 [], replicated
- grad_features: bfloat16 [4, 8, 512, 128], P('dp', 'space')
Inputs may be any that keep to these rules, and one draw needn't show every extreme that they name: `rulebook`: values below 1 name a slot of the same device, 1 to 1 a slot of the device one lower along space and only for offsets with z displacement -1, 2 to 2 a slot of the device one higher and only for z displacement +1, 3 no neighbour; the first device has no lower and the last no higher references; offset 13 names the slot itself. Each device fills its slots from slot 0 on; unfilled slots have no neighbours and no occupied voxels. `occupancy`: occupied voxels lie only in filled slots; slot 0 of every device is filled and its first voxel occupied; in each crop some device fills all 1 slots.
All inputs are finite; a program needn't handle non-finite values.
Results may differ from a plain program's by a relative error of at most 0.007.
Values may be sent and summed in bfloat16 or wider, within the bound.
No kernel may reach another device: no remote copies, remote signals or barrier semaphores. Data moves between devices by JAX's collectives and lax.ppermute only.
A program may use at most 64 MiB of HBM per device.

v0:
```python
import jax
import jax.numpy as jnp
from jax import lax
from jax.sharding import PartitionSpec as P

EDGE = 8
VOX = 512


def passed_along(value, axis, by):
    length = lax.axis_size(axis)
    pairs = [(i, i + by) for i in range(length) if 0 <= i + by < length]
    return lax.ppermute(value, axis, pairs)


def blocks_of(values):
    return values.reshape((values.shape[0], EDGE, EDGE, EDGE, values.shape[-1]))


def assemble(local_blocks, below_top, above_bottom, rule_rows):
    slot_count = local_blocks.shape[0]
    shape_full = local_blocks.shape
    layer_shape = (shape_full[1], shape_full[2], 1, shape_full[4])
    dtype_in = local_blocks.dtype
    centre = jnp.concatenate(
        [local_blocks, jnp.zeros((2 * slot_count + 1,) + shape_full[1:], dtype_in)], axis=0
    )
    low_table = jnp.concatenate(
        [
            local_blocks[:, :, :, EDGE - 1 : EDGE],
            below_top,
            jnp.zeros((slot_count + 1,) + layer_shape, dtype_in),
        ],
        axis=0,
    )
    high_table = jnp.concatenate(
        [
            local_blocks[:, :, :, 0:1],
            jnp.zeros((slot_count,) + layer_shape, dtype_in),
            above_bottom,
            jnp.zeros((1,) + layer_shape, dtype_in),
        ],
        axis=0,
    )
    tables = (low_table, centre, high_table)
    bounds = ((EDGE - 1, EDGE), (0, EDGE), (0, 1))
    planes = []
    for step_x in range(3):
        columns = []
        for step_y in range(3):
            pieces = []
            for step_z in range(3):
                table = tables[step_z][
                    :, bounds[step_x][0] : bounds[step_x][1], bounds[step_y][0] : bounds[step_y][1]
                ]
                pieces.append(
                    jnp.take(table, rule_rows[:, (step_x * 3 + step_y) * 3 + step_z], axis=0)
                )
            columns.append(jnp.concatenate(pieces, axis=3))
        planes.append(jnp.concatenate(columns, axis=2))
    return jnp.concatenate(planes, axis=1)


def windows(padded, step_x, step_y, step_z):
    window = padded[:, step_x : step_x + EDGE, step_y : step_y + EDGE, step_z : step_z + EDGE]
    return window.reshape((padded.shape[0] * EDGE**3, padded.shape[-1]))


def forward_conv(padded, weights):
    summed = jnp.zeros((padded.shape[0] * EDGE**3, weights.shape[2]), jnp.float32)
    for offset in range(27):
        window = windows(padded, offset // 9, offset // 3 % 3, offset % 3)
        summed = summed + jnp.dot(window, weights[offset], preferred_element_type=jnp.float32)
    return summed


def transpose_conv(padded, weights):
    summed = jnp.zeros((padded.shape[0] * EDGE**3, weights.shape[1]), jnp.float32)
    for offset in range(27):
        window = windows(padded, 2 - offset // 9, 2 - offset // 3 % 3, 2 - offset % 3)
        summed = summed + jnp.dot(window, weights[offset].T, preferred_element_type=jnp.float32)
    return summed


def filter_grad(padded, cotangent):
    terms = []
    for offset in range(27):
        window = windows(padded, offset // 9, offset // 3 % 3, offset % 3)
        terms.append(
            lax.dot_general(
                window, cotangent, (((0,), (0,)), ((), ())), preferred_element_type=jnp.float32
            )
        )
    return jnp.stack(terms)


def silu_slope(pre_act):
    sigmoid = jax.nn.sigmoid(pre_act)
    return sigmoid * (1.0 + pre_act * (1.0 - sigmoid))


def head_part(act_two, pre_two, occupied, label_ids, head_weight):
    mask_col = occupied.astype(jnp.float32)[:, None]
    logits = jnp.dot(act_two, head_weight, preferred_element_type=jnp.float32)
    classes = jnp.arange(head_weight.shape[1], dtype=jnp.int32)
    onehot = (label_ids[:, None] == classes[None, :]).astype(jnp.float32)
    total_log = jax.nn.logsumexp(logits, axis=1, keepdims=True)
    losses = jnp.sum((total_log - logits) * onehot * mask_col)
    dlogits = (jnp.exp(logits - total_log) - onehot) * mask_col
    head_term = lax.dot_general(
        act_two.astype(jnp.float32),
        dlogits,
        (((0,), (0,)), ((), ())),
        precision=lax.Precision.HIGHEST,
        preferred_element_type=jnp.float32,
    )
    back_two = jnp.dot(
        dlogits,
        head_weight.astype(jnp.float32).T,
        precision=lax.Precision.HIGHEST,
        preferred_element_type=jnp.float32,
    )
    grad_two = (back_two * silu_slope(pre_two) * mask_col).astype(jnp.bfloat16)
    return (grad_two, head_term, losses, jnp.sum(mask_col))


def neighbourhood(values, rule_rows):
    local_blocks = blocks_of(values)
    from_below = passed_along(local_blocks, "space", 1)
    from_above = passed_along(local_blocks, "space", -1)
    below_top = from_below[:, :, :, EDGE - 1 : EDGE]
    above_bottom = from_above[:, :, :, 0:1]
    return assemble(local_blocks, below_top, above_bottom, rule_rows)


def local(features, occupancy, labels, rulebook, filter_one, filter_two, head_weight):
    values = features[0]
    occupied = occupancy[0]
    rule_rows = rulebook[0]
    slot_count, voxels, channels = values.shape
    row_count = slot_count * voxels
    mask_col = occupied.reshape((row_count, 1)).astype(jnp.float32)
    masked_in = values * occupied[:, :, None].astype(jnp.bfloat16)
    pad_in = neighbourhood(masked_in, rule_rows)
    pre_one = forward_conv(pad_in, filter_one) * mask_col
    act_one = jax.nn.silu(pre_one).astype(jnp.bfloat16)
    pad_act = neighbourhood(act_one.reshape(values.shape), rule_rows)
    pre_two = forward_conv(pad_act, filter_two) * mask_col
    act_two = jax.nn.silu(pre_two).astype(jnp.bfloat16)
    grad_two, head_term, losses, counted = head_part(
        act_two, pre_two, occupied.reshape(row_count), labels[0].reshape(row_count), head_weight
    )
    pad_grad_two = neighbourhood(grad_two.reshape(values.shape), rule_rows)
    filter_term_two = filter_grad(pad_act, grad_two)
    back_one = transpose_conv(pad_grad_two, filter_two)
    grad_one = (back_one * silu_slope(pre_one) * mask_col).astype(jnp.bfloat16)
    filter_term_one = filter_grad(pad_in, grad_one)
    pad_grad_one = neighbourhood(grad_one.reshape(values.shape), rule_rows)
    grad_in = (transpose_conv(pad_grad_one, filter_one) * mask_col).astype(jnp.bfloat16)
    sum_one, sum_two, head_sum, loss_sum, count_sum = lax.psum(
        (filter_term_one, filter_term_two, head_term, losses, counted), ("space", "dp")
    )
    scale = 1.0 / VOX
    return (
        sum_one * scale,
        sum_two * scale,
        head_sum * scale,
        loss_sum / count_sum,
        grad_in.reshape(features.shape),
    )


def solution(mesh):
    placed = (
        P("dp", "space", None, None),
        P("dp", "space", None),
        P("dp", "space", None),
        P("dp", "space", None),
        P(),
        P(),
        P(),
    )
    return jax.shard_map(
        local,
        mesh=mesh,
        in_specs=placed,
        out_specs=(P(), P(), P(), P(), P("dp", "space", None, None)),
        check_vma=False,
    )
```

profile of v0, /device:TPU:1, one launch (start us, length us, event | category | flops | bytes accessed | tf_op | source)
XLA Modules:
  0.0 359.8 jit_solution(13847579024420010118)
XLA Ops:
  8.0 1.0 broadcast_multiply_fusion.2
  9.1 1.3 collective-permute-start.1
  10.4 4.6 %collective-permute-start = (bf16[1,8,8,8,128]{4,3,2,1,0:T(8,128)(2,1)S(1)}, bf16[1,8,8,8,128]{4,3,2,1,0:T(8,128)(2,1)S(1)}, u32[]{:S(2)}, u32[]{:S(2)}) collective-permute-start(bf16[1,8,8,8,128]{4,3,2,1,0:T(8,128)(2,1)S(1)} %broadcast_multiply_fusion.2), channel_id=1, source_target_pairs={{0,4},{4,8},{8,12},{12,16},{16,20},{20,24},{24,28},{1,5},{5,9},{9,... | collective-permute-start | bytes 393224 | tf_op jit(solution)/shard_map/ppermute | solution.py:13
  15.1 2.1 fusion.369
  20.9 1.6 fusion.370
  34.0 1.3 convert_reduce_fusion.1
  74.7 1.0 copy-done.1
  80.5 0.9 multiply_convert_fusion.1
  81.4 1.3 collective-permute-start.3
  82.8 4.9 %collective-permute-start.2 = (bf16[1,8,8,8,128]{4,3,2,1,0:T(8,128)(2,1)S(1)}, bf16[1,8,8,8,128]{4,3,2,1,0:T(8,128)(2,1)S(1)}, u32[]{:S(2)}, u32[]{:S(2)}) collective-permute-start(bf16[1,8,8,8,128]{4,3,2,1,0:T(8,128)(2,1)S(1)} %bitcast.1093), channel_id=1, source_target_pairs={{0,4},{4,8},{8,12},{12,16},{16,20},{20,24},{24,28},{1,5},{5,9},{9,... | collective-permute-start | bytes 393224 | tf_op jit(solution)/shard_map/ppermute | solution.py:13
  88.4 3.9 %collective-permute-done.2 = bf16[1,8,8,8,128]{4,3,2,1,0:T(8,128)(2,1)S(1)} collective-permute-done((bf16[1,8,8,8,128]{4,3,2,1,0:T(8,128)(2,1)S(1)}, bf16[1,8,8,8,128]{4,3,2,1,0:T(8,128)(2,1)S(1)}, u32[]{:S(2)}, u32[]{:S(2)}) %collective-permute-start.2) | collective-permute-done | bytes 131104 | tf_op jit(solution)/shard_map/ppermute | solution.py:13
  100.7 1.3 collective-permute-start.5
  102.1 5.4 %collective-permute-start.4 = (bf16[1,8,8,8,128]{4,3,2,1,0:T(8,128)(2,1)S(1)}, bf16[1,8,8,8,128]{4,3,2,1,0:T(8,128)(2,1)}, u32[]{:S(2)}, u32[]{:S(2)}) collective-permute-start(bf16[1,8,8,8,128]{4,3,2,1,0:T(8,128)(2,1)S(1)} %bitcast.1080), channel_id=1, source_target_pairs={{0,4},{4,8},{8,12},{12,16},{16,20},{20,24},{24,28},{1,5},{5,9},{9,... | collective-permute-start | bytes 393224 | tf_op jit(solution)/shard_map/ppermute | solution.py:13
  107.5 0.9 fusion.36
  110.9 0.9 fusion.35
  111.8 0.9 fusion.34
  112.6 0.9 fusion.33
  113.5 0.9 fusion.32
  114.3 0.9 fusion.31
  115.2 0.9 fusion.30
  116.0 0.9 fusion.29
  116.9 0.9 fusion.28
  117.8 0.9 fusion.27
  118.6 0.9 fusion.26
  119.5 0.9 fusion.25
  120.3 0.9 fusion.24
  121.2 0.9 fusion.23
  122.0 0.9 fusion.22
  123.8 0.9 fusion.20
  124.6 0.9 fusion.19
  125.5 0.9 fusion.18
  126.3 0.9 fusion.17
  128.0 0.9 fusion.15
  128.9 0.9 fusion.14
  129.8 0.9 fusion.13
  130.6 0.9 fusion.12
  131.5 0.9 fusion.11
  132.3 0.9 fusion.10
  133.2 41.4 %all-reduce.4 = (f32[128,3]{0,1:T(4,128)S(1)}, f32[]{:T(128)}, f32[]{:T(128)}) all-reduce(f32[128,3]{0,1:T(4,128)S(1)} %fusion.324, f32[]{:T(128)} %multiply_reduce_fusion, f32[]{:T(128)} %convert_reduce_fusion.1), channel_id=1, replica_groups=mesh['space'=8,'dp'=4] {'space','dp'}, use_global_device_ids=true, to_apply=%region_4.13 | all-reduce | flops 386 | bytes 3088 | tf_op jit(solution)/shard_map/psum | solution.py:160
  177.1 0.9 slice.1675
  178.3 0.9 slice.1672
  187.3 1.4 collective-permute-start.7
  189.4 4.8 %collective-permute-start.6 = (bf16[1,8,8,8,128]{4,3,2,1,0:T(8,128)(2,1)S(1)}, bf16[1,8,8,8,128]{4,3,2,1,0:T(8,128)(2,1)}, u32[]{:S(2)}, u32[]{:S(2)}) collective-permute-start(bf16[1,8,8,8,128]{4,3,2,1,0:T(8,128)(2,1)S(1)} %bitcast.1073), channel_id=1, source_target_pairs={{0,4},{4,8},{8,12},{12,16},{16,20},{20,24},{24,28},{1,5},{5,9},{9,... | collective-permute-start | bytes 393224 | tf_op jit(solution)/shard_map/ppermute | solution.py:13
  206.9 0.9 slice.1719
  208.2 0.9 slice.1716
  217.4 130.0 %all-reduce.8.cloned.1.call-done = (f32[27,128,128]{2,1,0:T(8,128)}, f32[27,128,128]{2,1,0:T(8,128)}) async-done(((f32[27,128,128]{2,1,0:T(8,128)}, f32[27,128,128]{2,1,0:T(8,128)}), (f32[27,128,128]{2,1,0:T(8,128)}, f32[27,128,128]{2,1,0:T(8,128)})) %all-reduce.8.cloned.1.call-update) | async-done | bytes 3538960 | tf_op jit(solution)/shard_map/psum | solution.py:160
  347.4 3.0 broadcast_multiply_fusion.1
  350.4 1.4 broadcast_multiply_fusion
  (453 shorter events, 51.5 us)
Async XLA Ops:
  7.2 92.9 %copy-start = (bf16[128,3]{0,1:T(4,128)(2,1)S(1)}, bf16[128,3]{0,1:T(4,128)(2,1)}, u32[]{:S(2)}) copy-start(bf16[128,3]{0,1:T(4,128)(2,1)} %param.29) | copy-start | bytes 2308
  7.2 340.2 %all-reduce.8.cloned.1.call-start = ((), (), s32[]{:S(2)}) async-start(), calls=%async_computation | async-start | bytes 7077888 | tf_op jit(solution)/shard_map/psum | solution.py:160
  9.1 62.8 %collective-permute-start.1 = (bf16[1,8,8,8,128]{4,3,2,1,0:T(8,128)(2,1)S(1)}, bf16[1,8,8,8,128]{4,3,2,1,0:T(8,128)(2,1)S(1)}, u32[]{:S(2)}, u32[]{:S(2)}) collective-permute-start(bf16[1,8,8,8,128]{4,3,2,1,0:T(8,128)(2,1)S(1)} %broadcast_multiply_fusion.2), channel_id=1, source_target_pairs={{4,0},{8,4},{12,8},{16,12},{20,16},{24,20},{28,24},{5,1},{9,5},{13... | collective-permute-start | bytes 393224 | tf_op jit(solution)/shard_map/ppermute | solution.py:13
  10.4 61.9 %collective-permute-start = (bf16[1,8,8,8,128]{4,3,2,1,0:T(8,128)(2,1)S(1)}, bf16[1,8,8,8,128]{4,3,2,1,0:T(8,128)(2,1)S(1)}, u32[]{:S(2)}, u32[]{:S(2)}) collective-permute-start(bf16[1,8,8,8,128]{4,3,2,1,0:T(8,128)(2,1)S(1)} %broadcast_multiply_fusion.2), channel_id=1, source_target_pairs={{0,4},{4,8},{8,12},{12,16},{16,20},{20,24},{24,28},{1,5},{5,9},{9,... | collective-permute-start | bytes 393224 | tf_op jit(solution)/shard_map/ppermute | solution.py:13
  71.8 20.6 %copy-start.49 = (bf16[4]{0:T(256)(128)(2,1)}, bf16[4]{0:T(256)(128)(2,1)S(1)}, u32[]{:S(2)}) copy-start(bf16[4]{0:T(256)(128)(2,1)S(1)} %pad.255.clone) | copy-start | bytes 28
  73.8 2.8 copy-start.9
  73.9 3.0 copy-start.7
  73.9 3.1 copy-start.5
  74.0 3.4 copy-start.45
  74.0 3.6 copy-start.43
  74.0 3.7 %copy-start.41 = (bf16[1,8,8,8,128]{4,3,2,1,0:T(8,128)(2,1)}, bf16[1,8,8,8,128]{4,3,2,1,0:T(8,128)(2,1)S(1)}, u32[]{:S(2)}) copy-start(bf16[1,8,8,8,128]{4,3,2,1,0:T(8,128)(2,1)S(1)} %get-tuple-element.199) | copy-start | bytes 393220
  74.1 4.3 %copy-start.39 = (bf16[1,8,8,8,128]{4,3,2,1,0:T(8,128)(2,1)}, bf16[1,8,8,8,128]{4,3,2,1,0:T(8,128)(2,1)S(1)}, u32[]{:S(2)}) copy-start(bf16[1,8,8,8,128]{4,3,2,1,0:T(8,128)(2,1)S(1)} %get-tuple-element.198) | copy-start | bytes 393220
  74.1 4.5 %copy-start.37 = (bf16[1,8,8,8,128]{4,3,2,1,0:T(8,128)(2,1)}, bf16[1,8,8,8,128]{4,3,2,1,0:T(8,128)(2,1)S(1)}, u32[]{:S(2)}) copy-start(bf16[1,8,8,8,128]{4,3,2,1,0:T(8,128)(2,1)S(1)} %get-tuple-element.197) | copy-start | bytes 393220
  74.1 4.7 %copy-start.35 = (bf16[1,8,8,8,128]{4,3,2,1,0:T(8,128)(2,1)}, bf16[1,8,8,8,128]{4,3,2,1,0:T(8,128)(2,1)S(1)}, u32[]{:S(2)}) copy-start(bf16[1,8,8,8,128]{4,3,2,1,0:T(8,128)(2,1)S(1)} %get-tuple-element.196) | copy-start | bytes 393220
  74.6 4.4 %copy-start.33 = (bf16[1,8,8,8,128]{4,3,2,1,0:T(8,128)(2,1)}, bf16[1,8,8,8,128]{4,3,2,1,0:T(8,128)(2,1)S(1)}, u32[]{:S(2)}) copy-start(bf16[1,8,8,8,128]{4,3,2,1,0:T(8,128)(2,1)S(1)} %get-tuple-element.168) | copy-start | bytes 393220
  74.6 4.6 %copy-start.31 = (bf16[1,8,8,8,128]{4,3,2,1,0:T(8,128)(2,1)}, bf16[1,8,8,8,128]{4,3,2,1,0:T(8,128)(2,1)S(1)}, u32[]{:S(2)}) copy-start(bf16[1,8,8,8,128]{4,3,2,1,0:T(8,128)(2,1)S(1)} %get-tuple-element.167) | copy-start | bytes 393220
  74.6 4.7 %copy-start.29 = (bf16[1,8,8,8,128]{4,3,2,1,0:T(8,128)(2,1)}, bf16[1,8,8,8,128]{4,3,2,1,0:T(8,128)(2,1)S(1)}, u32[]{:S(2)}) copy-start(bf16[1,8,8,8,128]{4,3,2,1,0:T(8,128)(2,1)S(1)} %get-tuple-element.166) | copy-start | bytes 393220
  74.7 4.9 %copy-start.27 = (bf16[1,8,8,8,128]{4,3,2,1,0:T(8,128)(2,1)}, bf16[1,8,8,8,128]{4,3,2,1,0:T(8,128)(2,1)S(1)}, u32[]{:S(2)}) copy-start(bf16[1,8,8,8,128]{4,3,2,1,0:T(8,128)(2,1)S(1)} %get-tuple-element.165) | copy-start | bytes 393220
  74.7 5.1 %copy-start.23 = (bf16[1,8,8,8,128]{4,3,2,1,0:T(8,128)(2,1)}, bf16[1,8,8,8,128]{4,3,2,1,0:T(8,128)(2,1)S(1)}, u32[]{:S(2)}) copy-start(bf16[1,8,8,8,128]{4,3,2,1,0:T(8,128)(2,1)S(1)} %get-tuple-element.164) | copy-start | bytes 393220
  74.7 5.3 %copy-start.19 = (bf16[1,8,8,8,128]{4,3,2,1,0:T(8,128)(2,1)}, bf16[1,8,8,8,128]{4,3,2,1,0:T(8,128)(2,1)S(1)}, u32[]{:S(2)}) copy-start(bf16[1,8,8,8,128]{4,3,2,1,0:T(8,128)(2,1)S(1)} %get-tuple-element.163) | copy-start | bytes 393220
  74.7 5.4 %copy-start.15 = (bf16[1,8,8,8,128]{4,3,2,1,0:T(8,128)(2,1)}, bf16[1,8,8,8,128]{4,3,2,1,0:T(8,128)(2,1)S(1)}, u32[]{:S(2)}) copy-start(bf16[1,8,8,8,128]{4,3,2,1,0:T(8,128)(2,1)S(1)} %get-tuple-element.162) | copy-start | bytes 393220
  74.7 5.6 %copy-start.11 = (bf16[1,8,8,8,128]{4,3,2,1,0:T(8,128)(2,1)}, bf16[1,8,8,8,128]{4,3,2,1,0:T(8,128)(2,1)S(1)}, u32[]{:S(2)}) copy-start(bf16[1,8,8,8,128]{4,3,2,1,0:T(8,128)(2,1)S(1)} %get-tuple-element.161) | copy-start | bytes 393220
  74.7 5.8 %copy-start.47 = (bf16[1,8,8,8,128]{4,3,2,1,0:T(8,128)(2,1)}, bf16[1,8,8,8,128]{4,3,2,1,0:T(8,128)(2,1)S(1)}, u32[]{:S(2)}) copy-start(bf16[1,8,8,8,128]{4,3,2,1,0:T(8,128)(2,1)S(1)} %get-tuple-element.160) | copy-start | bytes 393220
  81.4 6.6 %collective-permute-start.3 = (bf16[1,8,8,8,128]{4,3,2,1,0:T(8,128)(2,1)S(1)}, bf16[1,8,8,8,128]{4,3,2,1,0:T(8,128)(2,1)S(1)}, u32[]{:S(2)}, u32[]{:S(2)}) collective-permute-start(bf16[1,8,8,8,128]{4,3,2,1,0:T(8,128)(2,1)S(1)} %bitcast.1090), channel_id=1, source_target_pairs={{4,0},{8,4},{12,8},{16,12},{20,16},{24,20},{28,24},{5,1},{9,5},{13... | collective-permute-start | bytes 393224 | tf_op jit(solution)/shard_map/ppermute | solution.py:13
  82.8 9.6 %collective-permute-start.2 = (bf16[1,8,8,8,128]{4,3,2,1,0:T(8,128)(2,1)S(1)}, bf16[1,8,8,8,128]{4,3,2,1,0:T(8,128)(2,1)S(1)}, u32[]{:S(2)}, u32[]{:S(2)}) collective-permute-start(bf16[1,8,8,8,128]{4,3,2,1,0:T(8,128)(2,1)S(1)} %bitcast.1093), channel_id=1, source_target_pairs={{0,4},{4,8},{8,12},{12,16},{16,20},{20,24},{24,28},{1,5},{5,9},{9,... | collective-permute-start | bytes 393224 | tf_op jit(solution)/shard_map/ppermute | solution.py:13
  100.7 76.4 %collective-permute-start.5 = (bf16[1,8,8,8,128]{4,3,2,1,0:T(8,128)(2,1)S(1)}, bf16[1,8,8,8,128]{4,3,2,1,0:T(8,128)(2,1)}, u32[]{:S(2)}, u32[]{:S(2)}) collective-permute-start(bf16[1,8,8,8,128]{4,3,2,1,0:T(8,128)(2,1)S(1)} %bitcast.1077), channel_id=1, source_target_pairs={{4,0},{8,4},{12,8},{16,12},{20,16},{24,20},{28,24},{5,1},{9,5},{13... | collective-permute-start | bytes 393224 | tf_op jit(solution)/shard_map/ppermute | solution.py:13
  102.1 76.3 %collective-permute-start.4 = (bf16[1,8,8,8,128]{4,3,2,1,0:T(8,128)(2,1)S(1)}, bf16[1,8,8,8,128]{4,3,2,1,0:T(8,128)(2,1)}, u32[]{:S(2)}, u32[]{:S(2)}) collective-permute-start(bf16[1,8,8,8,128]{4,3,2,1,0:T(8,128)(2,1)S(1)} %bitcast.1080), channel_id=1, source_target_pairs={{0,4},{4,8},{8,12},{12,16},{16,20},{20,24},{24,28},{1,5},{5,9},{9,... | collective-permute-start | bytes 393224 | tf_op jit(solution)/shard_map/ppermute | solution.py:13
  125.5 53.8 %copy-start.50 = (bf16[4]{0:T(256)(128)(2,1)S(1)}, bf16[4]{0:T(256)(128)(2,1)}, u32[]{:S(2)}) copy-start(bf16[4]{0:T(256)(128)(2,1)} %copy-done.49) | copy-start | bytes 28
  130.6 49.8 %copy-start.53 = (bf16[1,1,1,8,128]{4,3,2,1,0:T(8,128)(2,1)S(1)}, bf16[1,1,1,8,128]{4,3,2,1,0:T(8,128)(2,1)}, u32[]{:S(2)}) copy-start(bf16[1,1,1,8,128]{4,3,2,1,0:T(8,128)(2,1)} %fusion.317) | copy-start | bytes 6148
  130.6 49.8 %copy-start.54 = (bf16[1,1,1,8,128]{4,3,2,1,0:T(8,128)(2,1)S(1)}, bf16[1,1,1,8,128]{4,3,2,1,0:T(8,128)(2,1)}, u32[]{:S(2)}) copy-start(bf16[1,1,1,8,128]{4,3,2,1,0:T(8,128)(2,1)} %fusion.316) | copy-start | bytes 6148
  186.6 8.9 %copy-start.26 = (bf16[1,8,8,8,128]{4,3,2,1,0:T(8,128)(2,1)S(1)}, bf16[1,8,8,8,128]{4,3,2,1,0:T(8,128)(2,1)}, u32[]{:S(2)}) copy-start(bf16[1,8,8,8,128]{4,3,2,1,0:T(8,128)(2,1)} %copy-done.25) | copy-start | bytes 393220
  186.6 9.2 %copy-start.22 = (bf16[1,8,8,8,128]{4,3,2,1,0:T(8,128)(2,1)S(1)}, bf16[1,8,8,8,128]{4,3,2,1,0:T(8,128)(2,1)}, u32[]{:S(2)}) copy-start(bf16[1,8,8,8,128]{4,3,2,1,0:T(8,128)(2,1)} %copy-done.21) | copy-start | bytes 393220
  186.8 9.2 %copy-start.18 = (bf16[1,8,8,8,128]{4,3,2,1,0:T(8,128)(2,1)S(1)}, bf16[1,8,8,8,128]{4,3,2,1,0:T(8,128)(2,1)}, u32[]{:S(2)}) copy-start(bf16[1,8,8,8,128]{4,3,2,1,0:T(8,128)(2,1)} %copy-done.17) | copy-start | bytes 393220
  186.8 9.4 %copy-start.14 = (bf16[1,8,8,8,128]{4,3,2,1,0:T(8,128)(2,1)S(1)}, bf16[1,8,8,8,128]{4,3,2,1,0:T(8,128)(2,1)}, u32[]{:S(2)}) copy-start(bf16[1,8,8,8,128]{4,3,2,1,0:T(8,128)(2,1)} %copy-done.13) | copy-start | bytes 393220
  186.8 9.7 %copy-start.10 = (bf16[1,8,8,8,128]{4,3,2,1,0:T(8,128)(2,1)S(1)}, bf16[1,8,8,8,128]{4,3,2,1,0:T(8,128)(2,1)}, u32[]{:S(2)}) copy-start(bf16[1,8,8,8,128]{4,3,2,1,0:T(8,128)(2,1)} %copy-done.9) | copy-start | bytes 393220
  187.0 9.7 %copy-start.8 = (bf16[1,8,8,8,128]{4,3,2,1,0:T(8,128)(2,1)S(1)}, bf16[1,8,8,8,128]{4,3,2,1,0:T(8,128)(2,1)}, u32[]{:S(2)}) copy-start(bf16[1,8,8,8,128]{4,3,2,1,0:T(8,128)(2,1)} %copy-done.7) | copy-start | bytes 393220
  187.0 9.9 %copy-start.6 = (bf16[1,8,8,8,128]{4,3,2,1,0:T(8,128)(2,1)S(1)}, bf16[1,8,8,8,128]{4,3,2,1,0:T(8,128)(2,1)}, u32[]{:S(2)}) copy-start(bf16[1,8,8,8,128]{4,3,2,1,0:T(8,128)(2,1)} %copy-done.5) | copy-start | bytes 393220
  187.3 10.2 %copy-start.46 = (bf16[1,8,8,8,128]{4,3,2,1,0:T(8,128)(2,1)S(1)}, bf16[1,8,8,8,128]{4,3,2,1,0:T(8,128)(2,1)}, u32[]{:S(2)}) copy-start(bf16[1,8,8,8,128]{4,3,2,1,0:T(8,128)(2,1)} %copy-done.45) | copy-start | bytes 393220
  187.3 19.6 %collective-permute-start.7 = (bf16[1,8,8,8,128]{4,3,2,1,0:T(8,128)(2,1)S(1)}, bf16[1,8,8,8,128]{4,3,2,1,0:T(8,128)(2,1)}, u32[]{:S(2)}, u32[]{:S(2)}) collective-permute-start(bf16[1,8,8,8,128]{4,3,2,1,0:T(8,128)(2,1)S(1)} %bitcast.1070), channel_id=1, source_target_pairs={{4,0},{8,4},{12,8},{16,12},{20,16},{24,20},{28,24},{5,1},{9,5},{13... | collective-permute-start | bytes 393224 | tf_op jit(solution)/shard_map/ppermute | solution.py:13
  189.4 8.3 %copy-start.44 = (bf16[1,8,8,8,128]{4,3,2,1,0:T(8,128)(2,1)S(1)}, bf16[1,8,8,8,128]{4,3,2,1,0:T(8,128)(2,1)}, u32[]{:S(2)}) copy-start(bf16[1,8,8,8,128]{4,3,2,1,0:T(8,128)(2,1)} %copy-done.43) | copy-start | bytes 393220
  189.4 18.8 %collective-permute-start.6 = (bf16[1,8,8,8,128]{4,3,2,1,0:T(8,128)(2,1)S(1)}, bf16[1,8,8,8,128]{4,3,2,1,0:T(8,128)(2,1)}, u32[]{:S(2)}, u32[]{:S(2)}) collective-permute-start(bf16[1,8,8,8,128]{4,3,2,1,0:T(8,128)(2,1)S(1)} %bitcast.1073), channel_id=1, source_target_pairs={{0,4},{4,8},{8,12},{12,16},{16,20},{20,24},{24,28},{1,5},{5,9},{9,... | collective-permute-start | bytes 393224 | tf_op jit(solution)/shard_map/ppermute | solution.py:13
  194.8 3.2 copy-start.42
  196.2 2.7 copy-start.40
  196.5 2.7 copy-start.38
  196.7 2.7 copy-start.36
  197.0 2.7 copy-start.34
  201.9 4.9 %copy-start.3 = (f32[27,128,128]{2,1,0:T(8,128)}, f32[27,128,128]{2,1,0:T(8,128)S(1)}, u32[]{:S(2)}) copy-start(f32[27,128,128]{2,1,0:T(8,128)S(1)} %fusion.37) | copy-start | bytes 5308420
  347.4 3.0 copy-start.4
  (19 other events, 39.6 us)
Sparse Core Ops, SparseCore 0:
  207.0 140.3 all-reduce.7
where the time goes:
time: 364 us; the launch traced here: 360 us
  waiting for transfers between devices  134 us (37%)
  between operations  70.5 us (19%)
  matrix products  50.6 us (14%)
  blocking collectives  41.4 us (11%)
  starting transfers between devices  25 us (7%)
  other arithmetic  23.5 us (6%)
  local copies, waits for them, and re-layouts  14.7 us (4%)
    psum x1, waiting for transfers between devices, local(): lax.psum((filter_term_one, filter_term_two, head_term, losses, counted),...  130 us
    psum x1, blocking collectives, local(): lax.psum((filter_term_one, filter_term_two, head_term, losses, counted),...  41.4 us
    dot_general x54, matrix products, filter_grad(): lax.dot_general(window, cotangent, (((0,), (0,)), ((), ())), preferred_el...  29.2 us
    ppermute x8, starting transfers between devices, passed_along(): return lax.ppermute(value, axis, pairs)  25 us
    dot_general x54, matrix products, transpose_conv(): jnp.dot(window, weights[offset].T, preferred_element_type=jnp.float32)  10.8 us
    dot_general x54, matrix products, forward_conv(): jnp.dot(window, weights[offset], preferred_element_type=jnp.float32)  9.91 us
    select_n x95, other arithmetic, assemble(): jnp.take(table, rule_rows[:, (step_x * 3 + step_y) * 3 + step_z], axis=0)  8.77 us
  transfers between devices with their start and end apart: 9, of which 3 were waited for; matrix products, arithmetic and copies ran while one was open for 16% of the time, Pallas kernels for 0%

commit v1 on v0

v1 whole, which is shorter than its diff:
```python
import functools

import jax
import jax.numpy as jnp
from jax import lax
from jax.experimental import pallas as pl
from jax.experimental.pallas import tpu as pltpu
from jax.sharding import Mesh, PartitionSpec as P

EDGE = 8
VOX = 512
LANES = 128
TAPS = 9
SMALL = 8
F32 = jnp.float32
BF16 = jnp.bfloat16
PARAMS = pltpu.CompilerParams(vmem_limit_bytes=40 * 1024 * 1024)
VMEM = pl.BlockSpec(memory_space=pltpu.VMEM)
SMEM = pl.BlockSpec(memory_space=pltpu.SMEM)


def sds(shape, dtype):
    return jax.ShapeDtypeStruct(shape, dtype)


def contract(a, b, dim_a, dim_b):
    return lax.dot_general(a, b, (((dim_a,), (dim_b,)), ((), ())), preferred_element_type=F32)


def spread_layer(layer):
    return jnp.broadcast_to(layer.astype(F32).reshape(64, 1, LANES), (64, EDGE, LANES))


def build_windows(block, recv_a, recv_b, rule_ref, parity_ref, out_ref):
    cells = block.reshape(64, EDGE, LANES)
    even = parity_ref[0] == 0
    got_a, got_b = recv_a.astype(F32), recv_b.astype(F32)
    below = jnp.where(even, got_b, got_a)
    above = jnp.where(even, got_a, got_b)
    depth = lax.broadcasted_iota(jnp.int32, (1, EDGE, LANES), 1)

    def flag(i, j, k, wanted):
        return jnp.where(rule_ref[9 * i + 3 * j + k] == wanted, 1.0, 0.0).astype(F32)

    for k in range(3):
        if k == 1:
            own, other = cells, None
        elif k == 0:
            own, other = pltpu.roll(cells, 1, 1), spread_layer(below)
        else:
            own, other = pltpu.roll(cells, EDGE - 1, 1), spread_layer(above)
        own = own.reshape(EDGE, EDGE, EDGE, LANES)
        if other is not None:
            other = other.reshape(EDGE, EDGE, EDGE, LANES)

        def region(i, j):
            xs = {0: slice(7, 8), 1: slice(0, 8), 2: slice(0, 1)}[i]
            ys = {0: slice(7, 8), 1: slice(0, 8), 2: slice(0, 1)}[j]
            inner = flag(i, j, 1, 0)
            if k == 1:
                return own[xs, ys] * inner
            edge = depth == (0 if k == 0 else EDGE - 1)
            keep = jnp.where(edge, flag(i, j, k, 0), inner)
            take = jnp.where(edge, flag(i, j, k, 1 if k == 0 else 2), 0.0)
            return own[xs, ys] * keep[None] + other[xs, ys] * take[None]

        columns = [jnp.concatenate([region(i, j) for i in range(3)], axis=0).astype(F32) for j in range(3)]
        for j in range(3):
            if j == 0:
                padded = jnp.concatenate([columns[0], columns[1][:, :7]], axis=1)
            elif j == 1:
                padded = columns[1]
            else:
                padded = jnp.concatenate([columns[1][:, 1:], columns[2]], axis=1)
            lane = (3 * j + k) * LANES
            out_ref[:, lane : lane + LANES] = padded.reshape(640, LANES).astype(BF16)


def put_layers(block, parity_ref, send_a_ref, send_b_ref):
    cells = block.reshape(64, EDGE, LANES)
    top, bottom = cells[:, EDGE - 1, :], cells[:, 0, :]
    even = parity_ref[0] == 0
    send_a_ref[...] = jnp.where(even, top, bottom).astype(BF16)
    send_b_ref[...] = jnp.where(even, bottom, top).astype(BF16)


def forward_sum(win_ref, filt_ref):
    total = None
    for i in range(3):
        filt = filt_ref[TAPS * i : TAPS * (i + 1)].reshape(TAPS * LANES, LANES)
        term = jnp.dot(win_ref[64 * i : 64 * i + VOX, :], filt, preferred_element_type=F32)
        total = term if total is None else total + term
    return total


def backward_sum(win_ref, filt_ref):
    total = None
    for i in range(3):
        filt = jnp.concatenate([filt_ref[26 - TAPS * i - t] for t in range(TAPS)], axis=1)
        term = contract(win_ref[64 * i : 64 * i + VOX, :], filt, 1, 1)
        total = term if total is None else total + term
    return total


def filter_terms(win_ref, grad, wide_ref, out_ref):
    wide_ref[...] = jnp.zeros_like(wide_ref)
    for i in range(3):
        wide_ref[64 * i : 64 * i + VOX, LANES * i : LANES * (i + 1)] = grad
    for t in range(TAPS):
        term = contract(win_ref[:, LANES * t : LANES * (t + 1)], wide_ref[...], 0, 0)
        for i in range(3):
            out_ref[TAPS * i + t] = term[:, LANES * i : LANES * (i + 1)].astype(BF16)


def silu_parts(pre):
    sigmoid = 1.0 / (1.0 + jnp.exp(-pre))
    return pre * sigmoid, sigmoid * (1.0 + pre * (1.0 - sigmoid))


def first_kernel(parity, feat, occ, labels, masked, mask, onehot, send_a, send_b):
    rows = lax.broadcasted_iota(jnp.int32, (SMALL, VOX), 0)
    occ_rows = jnp.where(rows == 0, jnp.broadcast_to(occ[...], (SMALL, VOX)), 0).astype(F32).astype(BF16)
    hot_rows = jnp.where(rows == jnp.broadcast_to(labels[...], (SMALL, VOX)), 1.0, 0.0).astype(BF16)
    row = lax.broadcasted_iota(jnp.int32, (SMALL, LANES), 0)
    lane = lax.broadcasted_iota(jnp.int32, (SMALL, LANES), 1)
    first = jnp.where(row == 0, 1.0, 0.0).astype(BF16)
    unit = jnp.where(row == lane, 1.0, 0.0).astype(BF16)
    filled = contract(occ_rows, first, 0, 0)
    mask[...] = filled
    onehot[...] = contract(hot_rows, unit, 0, 0)
    block = feat[...].astype(F32) * filled
    masked[...] = block.astype(BF16)
    put_layers(block, parity, send_a, send_b)


def one_kernel(rule, parity, masked, recv_a, recv_b, filt, mask, win, act, pre, send_a, send_b):
    build_windows(masked[...].astype(F32), recv_a[...], recv_b[...], rule, parity, win)
    total = forward_sum(win, filt) * mask[...]
    pre[...] = total
    acted, _ = silu_parts(total)
    act[...] = acted.astype(BF16)
    put_layers(acted.astype(BF16).astype(F32), parity, send_a, send_b)


def two_kernel(classes, rule, parity, act_one, recv_a, recv_b, filt, mask, onehot, head, win, grad, small, send_a, send_b):
    build_windows(act_one[...].astype(F32), recv_a[...], recv_b[...], rule, parity, win)
    filled = mask[...]
    pre = forward_sum(win, filt) * filled
    acted, slope = silu_parts(pre)
    acted = acted.astype(BF16)
    lane = lax.broadcasted_iota(jnp.int32, (VOX, LANES), 1)
    logits = contract(acted, head[...], 1, 1)
    known = lane < classes
    top = jnp.max(jnp.where(known, logits, -jnp.inf), axis=1, keepdims=True)
    powers = jnp.where(known, jnp.exp(jnp.where(known, logits - top, 0.0)), 0.0)
    total_log = top + jnp.log(jnp.sum(powers, axis=1, keepdims=True))
    hot = onehot[...]
    chances = jnp.where(known, jnp.exp(jnp.where(known, logits - total_log, 0.0)), 0.0)
    dlogits = (chances - hot) * filled
    high = dlogits.astype(BF16)
    low = (dlogits - high.astype(F32)).astype(BF16)
    back = jnp.dot(high, head[...], preferred_element_type=F32) + jnp.dot(low, head[...], preferred_element_type=F32)
    out = (back * slope * filled).astype(BF16)
    grad[...] = out
    put_layers(out.astype(F32), parity, send_a, send_b)
    head_rows = (contract(high, acted, 0, 0) + contract(low, acted, 0, 0))[:SMALL]
    losses = jnp.sum((total_log - logits) * hot * filled, axis=0, keepdims=True)
    counted = jnp.sum(filled, axis=0, keepdims=True)
    tail = jnp.where(lane[:1] < classes, losses, jnp.where(lane[:1] == classes, counted, 0.0))
    row = lax.broadcasted_iota(jnp.int32, (SMALL, LANES), 0)
    values = jnp.where(row < classes, head_rows, jnp.where(row == classes, tail, 0.0))
    small[...] = values


def terms_kernel(win, grad, out, wide):
    filter_terms(win, grad[...], wide, out)


def three_kernel(rule, parity, grad_two, recv_a, recv_b, filt, mask, pre, win_one, grad_one, terms, send_a, send_b, win, wide):
    build_windows(grad_two[...].astype(F32), recv_a[...], recv_b[...], rule, parity, win)
    _, slope = silu_parts(pre[...])
    out = (backward_sum(win, filt) * slope * mask[...]).astype(BF16)
    grad_one[...] = out
    put_layers(out.astype(F32), parity, send_a, send_b)
    filter_terms(win_one, out, wide, terms)


def four_kernel(rule, parity, grad_one, recv_a, recv_b, filt, mask, out, win):
    build_windows(grad_one[...].astype(F32), recv_a[...], recv_b[...], rule, parity, win)
    out[...] = (backward_sum(win, filt) * mask[...]).astype(BF16)


def call(kernel, outs, specs, scratch=(), flops=0):
    return pl.pallas_call(
        kernel,
        out_shape=outs,
        in_specs=specs,
        out_specs=jax.tree.map(lambda _: VMEM, outs),
        scratch_shapes=list(scratch),
        compiler_params=PARAMS,
        cost_estimate=pl.CostEstimate(flops=flops, bytes_accessed=4_000_000, transcendentals=0),
    )


BLOCK = sds((VOX, LANES), BF16)
WIDE_BLOCK = sds((VOX, LANES), F32)
LAYER = sds((64, LANES), BF16)
WINDOWS = sds((640, TAPS * LANES), BF16)
TERMS = sds((27, LANES, LANES), BF16)
WIN_SCRATCH = pltpu.VMEM((640, TAPS * LANES), BF16)
WIDE_SCRATCH = pltpu.VMEM((640, 3 * LANES), BF16)
CONV = 2 * 27 * VOX * LANES * LANES


def swap_layers(send_a, send_b):
    length = lax.axis_size("space")
    pairs_a = [(i, i ^ 1) for i in range(length)]
    pairs_b = [(i, (i + 1) % length if i % 2 else (i - 1) % length) for i in range(length)]
    return lax.ppermute(send_a, "space", pairs_a), lax.ppermute(send_b, "space", pairs_b)


def core_swap(value):
    return lax.ppermute(value, "core", [(0, 1), (1, 0)])


def split_pair(value):
    high = value.astype(BF16)
    return jnp.concatenate([high, (value - high.astype(F32)).astype(BF16)], axis=0)


def join_pair(pair):
    half = pair.shape[0] // 2
    return pair[:half].astype(F32) + pair[half:].astype(F32)


def pair_kernel(rows, peers, mine, other, small_mine, small_other, out):
    small = join_pair(small_mine[...]) + join_pair(small_other[...])
    tail = split_pair(small)
    total = mine[...].reshape(27 * LANES, LANES).astype(F32) + other[...].reshape(27 * LANES, LANES).astype(F32)
    total = total.astype(BF16)
    spare = rows * peers - 27 * LANES
    if spare:
        total = jnp.concatenate([total, jnp.zeros((spare, LANES), BF16)], axis=0)
    for p in range(peers):
        out[p] = jnp.concatenate([total[p * rows : (p + 1) * rows], tail], axis=0)


def sum_kernel(rows, peers, parts, out, small):
    total = parts[0].astype(F32)
    half = SMALL // 2
    for p in range(1, peers):
        total = total + parts[p].astype(F32)
    result = total[:rows].astype(BF16)
    for p in range(peers):
        out[p] = result
    tail = total[rows:]
    small[...] = jnp.concatenate([tail[:half] + tail[half:], jnp.zeros((half, LANES), F32)], axis=0)


def local(classes, features, occupancy, labels, rulebook, filter_one, filter_two, head_weight):
    parity = (lax.axis_index("space") % 2).reshape(1).astype(jnp.int32)
    rule = rulebook.reshape(27)
    head = jnp.zeros((LANES, LANES), BF16).at[:classes].set(head_weight.T)
    masked, mask, onehot, a, b = call(
        first_kernel, (BLOCK, WIDE_BLOCK, WIDE_BLOCK, LAYER, LAYER), [SMEM] + [VMEM] * 3
    )(parity, features.reshape(VOX, LANES), occupancy.reshape(1, VOX), labels.reshape(1, VOX))
    a, b = swap_layers(a, b)
    win_one, act_one, pre_one, c, d = call(
        one_kernel, (WINDOWS, BLOCK, WIDE_BLOCK, LAYER, LAYER), [SMEM] * 2 + [VMEM] * 5, flops=CONV
    )(rule, parity, masked, a, b, filter_one, mask)
    c, d = swap_layers(c, d)
    win_two, grad_two, small, e, f = call(
        functools.partial(two_kernel, classes),
        (WINDOWS, BLOCK, sds((SMALL, LANES), F32), LAYER, LAYER),
        [SMEM] * 2 + [VMEM] * 7,
        flops=CONV,
    )(rule, parity, act_one, c, d, filter_two, mask, onehot, head)
    e, f = swap_layers(e, f)
    terms_two = call(terms_kernel, TERMS, [VMEM] * 2, [WIDE_SCRATCH], flops=CONV)(win_two, grad_two)
    grad_one, terms_one, g, h = call(
        three_kernel, (BLOCK, TERMS, LAYER, LAYER), [SMEM] * 2 + [VMEM] * 7, [WIN_SCRATCH, WIDE_SCRATCH], flops=2 * CONV
    )(rule, parity, grad_two, e, f, filter_two, mask, pre_one, win_one)
    g, h = swap_layers(g, h)
    grad_in = call(four_kernel, BLOCK, [SMEM] * 2 + [VMEM] * 5, [WIN_SCRATCH], flops=CONV)(
        rule, parity, grad_one, g, h, filter_one, mask
    )

    core = lax.axis_index("core")
    peers = lax.axis_size("space") * lax.axis_size("x")
    rows = -(-27 * LANES // (peers * SMALL)) * SMALL
    small_pair = split_pair(small[: SMALL // 2])
    mine = jnp.where(core == 0, terms_one, terms_two)
    away = jnp.where(core == 0, terms_two, terms_one)
    other, small_other = core_swap(away), core_swap(small_pair)
    chunks = call(
        functools.partial(pair_kernel, rows, peers), sds((peers, rows + SMALL, LANES), BF16), [VMEM] * 4
    )(mine, other, small_pair, small_other)
    parts = lax.all_to_all(chunks, ("space", "x"), 0, 0, tiled=True)
    copies, sums = call(
        functools.partial(sum_kernel, rows, peers),
        (sds((peers, rows, LANES), BF16), sds((SMALL, LANES), F32)),
        [VMEM],
    )(parts)
    whole = lax.all_to_all(copies, ("space", "x"), 0, 0, tiled=True)
    whole = whole.reshape(peers * rows, LANES)[: 27 * LANES].reshape(27, LANES, LANES)
    whole_other = core_swap(whole)
    scale = 1.0 / VOX
    sum_one = jnp.where(core == 0, whole, whole_other).astype(F32) * scale
    sum_two = jnp.where(core == 0, whole_other, whole).astype(F32) * scale
    return (
        sum_one,
        sum_two,
        sums[:classes].T * scale,
        jnp.sum(sums[classes, :classes]) / sums[classes, classes],
        grad_in.reshape(features.shape),
    )


def solution(mesh):
    shape = mesh.devices.shape
    inner = Mesh(mesh.devices.reshape(shape[0], shape[1] // 2, 2), ("space", "x", "core"))
    parts = ("x", "core")
    placed = (
        P(parts, "space", None, None),
        P(parts, "space", None),
        P(parts, "space", None),
        P(parts, "space", None),
        P(),
        P(),
        P(),
    )

    def whole(features, occupancy, labels, rulebook, filter_one, filter_two, head_weight):
        step = jax.shard_map(
            functools.partial(local, head_weight.shape[1]),
            mesh=inner,
            in_specs=placed,
            out_specs=(P(), P(), P(), P(), P(parts, "space", None, None)),
            check_vma=False,
        )
        return step(features, occupancy, labels, rulebook, filter_one, filter_two, head_weight)

    return whole
```

time: 364 us -> 111 us (0.30)
  waiting for transfers between devices: 134 us -> 10 us
  between operations: 70.5 us -> 3.25 us
  matrix products: 50.6 us -> 0 us
  other arithmetic: 23.5 us -> 3.59 us
  blocking collectives: 41.4 us -> 53.6 us
  Pallas kernels: 0 us -> 12 us
  local copies, waits for them, and re-layouts: 14.7 us -> 4.69 us
    psum x1 -> x0, waiting for transfers between devices: 130 us -> none  [local(): lax.psum((filter_term_one, filter_term_two, head_term, losses, counted),...]
    all_to_all x0 -> x2, blocking collectives: none -> 53.6 us  [the longest x1 27.7 us: local(): parts = lax.all_to_all(chunks, ('space', 'x'), 0, 0, tiled=True)]
    dot_general x165 -> x0, matrix products: 50.6 us -> none  [the longest x54 29.2 us: filter_grad(): lax.dot_general(window, cotangent, (((0,), (0,)), ((), ())), preferred_el...]
    psum x1 -> x0, blocking collectives: 41.4 us -> none  [local(): lax.psum((filter_term_one, filter_term_two, head_term, losses, counted),...]
    slice x66 -> x1, local copies, waits for them, and re-layouts: 12.8 us -> 0.58 us  [local(): sums[classes, classes]]
    pallas_call x0 -> x8, Pallas kernels: none -> 12 us  [the longest x1 3.37 us: local(): call(three_kernel, (BLOCK, TERMS, LAYER, LAYER), [SMEM] * 2 + [VMEM] * 7,...]
    select_n x96 -> x1, other arithmetic: 8.78 us -> 0.12 us  [local(): away = jnp.where(core == 0, terms_two, terms_one)]
    ppermute x8 -> x11, waiting for transfers between devices: 4.05 us -> 10 us  [the longest x4 8.06 us: swap_layers(): lax.ppermute(send_b, 'space', pairs_b)]
  transfers between devices with their start and end apart: 9 -> 11, of which waited for: 3 -> 5; matrix products, arithmetic and copies ran while one was open for 16% -> 2% of each run, Pallas kernels for 0% -> 3%
where the time goes in v1:
time: 111 us; the launch traced here: 109 us
  blocking collectives  53.6 us (48%)
  starting transfers between devices  22.1 us (20%)
  Pallas kernels  12 us (11%)
  waiting for transfers between devices  10 us (9%)
  local copies, waits for them, and re-layouts  4.69 us (4%)
  other arithmetic  3.59 us (3%)
  between operations  3.25 us (3%)
    all_to_all x1, blocking collectives, local(): parts = lax.all_to_all(chunks, ('space', 'x'), 0, 0, tiled=True)  27.7 us
    all_to_all x1, blocking collectives, local(): whole = lax.all_to_all(copies, ('space', 'x'), 0, 0, tiled=True)  26 us
    ppermute x4, starting transfers between devices, swap_layers(): lax.ppermute(send_b, 'space', pairs_b)  12 us
    ppermute x4, waiting for transfers between devices, swap_layers(): lax.ppermute(send_b, 'space', pairs_b)  8.06 us
    ppermute x3, starting transfers between devices, core_swap(): return lax.ppermute(value, 'core', [(0, 1), (1, 0)])  7.22 us
    unnamed x18, local copies, waits for them, and re-layouts  4.1 us
    pallas_call x1, Pallas kernels, local(): call(three_kernel, (BLOCK, TERMS, LAYER, LAYER), [SMEM] * 2 + [VMEM] * 7,...  3.37 us
    ppermute x4, starting transfers between devices, swap_layers(): lax.ppermute(send_a, 'space', pairs_a)  2.8 us
  transfers between devices with their start and end apart: 11, of which 5 were waited for; matrix products, arithmetic and copies ran while one was open for 2% of the time, Pallas kernels for 3%

profile of v1, /device:TPU:1, one launch (start us, length us, event | category | flops | bytes accessed | tf_op | source)
XLA Modules:
  0.0 109.2 jit_solution(10402968002954161840)
XLA Ops:
  0.6 0.0 copy-start.7
  0.6 0.0 copy-start.8
  0.7 0.0 copy-start
  0.7 0.9 copy-done
  1.6 0.7 copy-done.1
  2.3 0.7 copy-done.2
  2.9 0.3 shard_map.110
  3.2 2.1 %collective-permute-start = (bf16[64,128]{1,0:T(8,128)(2,1)S(1)}, bf16[64,128]{1,0:T(8,128)(2,1)S(1)}, u32[]{:S(2)}, u32[]{:S(2)}) collective-permute-start(bf16[64,128]{1,0:T(8,128)(2,1)S(1)} %get-tuple-element.39), channel_id=1, source_target_pairs={{0,4},{4,0},{8,12},{12,8},{16,20},{20,16},{24,28},{28,24},{1,5},{5... | collective-permute-start | bytes 49160 | tf_op jit(solution)/shard_map/ppermute | solution.py:219
  5.4 3.3 %collective-permute-start.1 = (bf16[64,128]{1,0:T(8,128)(2,1)S(1)}, bf16[64,128]{1,0:T(8,128)(2,1)S(1)}, u32[]{:S(2)}, u32[]{:S(2)}) collective-permute-start(bf16[64,128]{1,0:T(8,128)(2,1)S(1)} %get-tuple-element.40), channel_id=1, source_target_pairs={{0,28},{4,8},{8,4},{12,16},{16,12},{20,24},{24,20},{28,0},{1,29},{... | collective-permute-start | bytes 49160 | tf_op jit(solution)/shard_map/ppermute | solution.py:219
  8.6 0.0 collective-permute-done.recv_a
  8.7 2.0 %collective-permute-done.1.recv_b = bf16[64,128]{1,0:T(8,128)(2,1)S(1)} collective-permute-done((bf16[64,128]{1,0:T(8,128)(2,1)S(1)}, bf16[64,128]{1,0:T(8,128)(2,1)S(1)}, u32[]{:S(2)}, u32[]{:S(2)}) %collective-permute-start.1) | collective-permute-done | bytes 16416 | tf_op jit(solution)/shard_map/ppermute | solution.py:219
  10.7 1.2 %copy-done.4 = bf16[27,128,128]{2,1,0:T(8,128)(2,1)S(1)} copy-done((bf16[27,128,128]{2,1,0:T(8,128)(2,1)S(1)}, bf16[27,128,128]{2,1,0:T(8,128)(2,1)}, u32[]{:S(2)}) %copy-start.4) | copy-done | bytes 884760
  11.8 0.7 copy-done.6
  12.5 1.9 %shard_map.111 = (bf16[640,1152]{1,0:T(8,128)(2,1)S(1)}, bf16[512,128]{1,0:T(8,128)(2,1)S(1)}, f32[512,128]{1,0:T(8,128)S(1)}, bf16[64,128]{1,0:T(8,128)(2,1)S(1)}, bf16[64,128]{1,0:T(8,128)(2,1)S(1)}) custom-call(s32[27]{0:T(128)S(1)} %bitcast.14, s32[1]{0:T(128)} %bitcast.1.parity, bf16[512,128]{1,0:T(8,128)(2,1)S(1)} %get-tuple-element.38.masked, ...), custom_call_target="tpu_custom_call" | custom-call | flops 452984832 | bytes 4000000 | tf_op jit(solution)/shard_map/pallas_call | solution.py:268
  14.4 0.1 collective-permute-start.2
  14.5 3.3 %collective-permute-start.3 = (bf16[64,128]{1,0:T(8,128)(2,1)S(1)}, bf16[64,128]{1,0:T(8,128)(2,1)S(1)}, u32[]{:S(2)}, u32[]{:S(2)}) collective-permute-start(bf16[64,128]{1,0:T(8,128)(2,1)S(1)} %get-tuple-element.44), channel_id=1, source_target_pairs={{0,28},{4,8},{8,4},{12,16},{16,12},{20,24},{24,20},{28,0},{1,29},{... | collective-permute-start | bytes 49160 | tf_op jit(solution)/shard_map/ppermute | solution.py:219
  17.8 0.0 copy-done.8
  17.8 0.0 collective-permute-done.2.recv_a
  17.8 2.0 %collective-permute-done.3.recv_b = bf16[64,128]{1,0:T(8,128)(2,1)S(1)} collective-permute-done((bf16[64,128]{1,0:T(8,128)(2,1)S(1)}, bf16[64,128]{1,0:T(8,128)(2,1)S(1)}, u32[]{:S(2)}, u32[]{:S(2)}) %collective-permute-start.3) | collective-permute-done | bytes 16416 | tf_op jit(solution)/shard_map/ppermute | solution.py:219
  19.8 0.0 copy-done.7
  19.8 0.0 copy-done.3
  19.8 2.5 %shard_map.112 = (bf16[640,1152]{1,0:T(8,128)(2,1)S(1)}, bf16[512,128]{1,0:T(8,128)(2,1)S(1)}, f32[8,128]{1,0:T(8,128)S(1)}, bf16[64,128]{1,0:T(8,128)(2,1)S(1)}, bf16[64,128]{1,0:T(8,128)(2,1)S(1)}) custom-call(s32[27]{0:T(128)S(1)} %bitcast.15, s32[1]{0:T(128)} %bitcast.1.parity, bf16[512,128]{1,0:T(8,128)(2,1)S(1)} %get-tuple-element.42.act_one, ...), custom_call_target="tpu_custom_call" | custom-call | flops 452984832 | bytes 4000000 | tf_op jit(solution)/shard_map/pallas_call | solution.py:272
  22.4 0.1 collective-permute-start.4
  22.4 3.3 %collective-permute-start.5 = (bf16[64,128]{1,0:T(8,128)(2,1)S(1)}, bf16[64,128]{1,0:T(8,128)(2,1)S(1)}, u32[]{:S(2)}, u32[]{:S(2)}) collective-permute-start(bf16[64,128]{1,0:T(8,128)(2,1)S(1)} %get-tuple-element.48), channel_id=1, source_target_pairs={{0,28},{4,8},{8,4},{12,16},{16,12},{20,24},{24,20},{28,0},{1,29},{... | collective-permute-start | bytes 49160 | tf_op jit(solution)/shard_map/ppermute | solution.py:219
  25.8 1.1 %shard_map.114 = bf16[27,128,128]{2,1,0:T(8,128)(2,1)S(1)} custom-call(bf16[640,1152]{1,0:T(8,128)(2,1)S(1)} %get-tuple-element.52.win, bf16[512,128]{1,0:T(8,128)(2,1)S(1)} %get-tuple-element.46.grad_two.grad), custom_call_target="tpu_custom_call" | custom-call | flops 452984832 | bytes 4000000 | tf_op jit(solution)/shard_map/pallas_call | solution.py:279
  26.9 0.0 collective-permute-done.4.recv_a
  26.9 0.9 collective-permute-done.5.recv_b
  27.8 3.4 %shard_map.113 = (bf16[512,128]{1,0:T(8,128)(2,1)S(1)}, bf16[27,128,128]{2,1,0:T(8,128)(2,1)S(1)}, bf16[64,128]{1,0:T(8,128)(2,1)S(1)}, bf16[64,128]{1,0:T(8,128)(2,1)S(1)}) custom-call(s32[27]{0:T(128)S(1)} %bitcast.16, s32[1]{0:T(128)} %bitcast.1.parity, bf16[512,128]{1,0:T(8,128)(2,1)S(1)} %get-tuple-element.46.grad_two.grad, ...), custom_call_target="tpu_custom_call" | custom-call | flops 905969664 | bytes 4000000 | tf_op jit(solution)/shard_map/pallas_call | solution.py:280
  31.2 0.1 broadcast_select_fusion
  31.3 4.5 %collective-permute-start.6 = (bf16[27,128,128]{2,1,0:T(8,128)(2,1)S(1)}, bf16[27,128,128]{2,1,0:T(8,128)(2,1)S(1)}, u32[]{:S(2)}, u32[]{:S(2)}) collective-permute-start(bf16[27,128,128]{2,1,0:T(8,128)(2,1)S(1)} %get-tuple-element.63), channel_id=1, source_target_pairs={{0,1},{1,0},{2,3},{3,2},{4,5},{5,4},{6,7},{7,6},{8,9},{9,8},{10,11... | collective-permute-start | bytes 2654216 | tf_op jit(solution)/shard_map/ppermute | solution.py:223
  35.9 0.1 collective-permute-start.7
  36.0 1.9 %collective-permute-done.7.small_other = bf16[8,128]{1,0:T(8,128)(2,1)S(1)} collective-permute-done((bf16[8,128]{1,0:T(8,128)(2,1)S(1)}, bf16[8,128]{1,0:T(8,128)(2,1)S(1)}, u32[]{:S(2)}, u32[]{:S(2)}) %collective-permute-start.7) | collective-permute-done | bytes 2080 | tf_op jit(solution)/shard_map/ppermute | solution.py:223
  37.9 0.0 collective-permute-done.6.other
  37.9 0.3 shard_map.115
  38.2 27.7 %all_to_all.10.parts = bf16[16,224,128]{2,1,0:T(8,128)(2,1)S(1)} all-to-all(bf16[16,224,128]{2,1,0:T(8,128)(2,1)S(1)} %shard_map.115), channel_id=1, replica_groups=mesh['space'=8,'x'=2,'core'=2] {'space','x'}, dimensions={0} | all-to-all | bytes 1835008 | tf_op jit(solution)/shard_map/all_to_all | solution.py:298
  65.8 0.1 shard_map.116
  66.0 26.0 %all_to_all.11 = bf16[16,216,128]{2,1,0:T(8,128)(2,1)S(1)} all-to-all(bf16[16,216,128]{2,1,0:T(8,128)(2,1)S(1)} %get-tuple-element.54), channel_id=1, replica_groups=mesh['space'=8,'x'=2,'core'=2] {'space','x'}, dimensions={0} | all-to-all | bytes 1769472 | tf_op jit(solution)/shard_map/all_to_all | solution.py:304
  91.9 2.6 %collective-permute-start.8 = (bf16[27,128,128]{2,1,0:T(8,128)(2,1)S(1)}, bf16[27,128,128]{2,1,0:T(8,128)(2,1)S(1)}, u32[]{:S(2)}, u32[]{:S(2)}) collective-permute-start(bf16[27,128,128]{2,1,0:T(8,128)(2,1)S(1)} %bitcast.18), channel_id=1, source_target_pairs={{0,1},{1,0},{2,3},{3,2},{4,5},{5,4},{6,7},{7,6},{8,9},{9,8},{10,11... | collective-permute-start | bytes 2654216 | tf_op jit(solution)/shard_map/ppermute | solution.py:223
  94.5 0.5 collective-permute-start.9
  95.1 2.1 %collective-permute-start.10 = (bf16[64,128]{1,0:T(8,128)(2,1)S(1)}, bf16[64,128]{1,0:T(8,128)(2,1)S(1)}, u32[]{:S(2)}, u32[]{:S(2)}) collective-permute-start(bf16[64,128]{1,0:T(8,128)(2,1)S(1)} %get-tuple-element.58), channel_id=1, source_target_pairs={{0,28},{4,8},{8,4},{12,16},{16,12},{20,24},{24,20},{28,0},{1,29},{... | collective-permute-start | bytes 49160 | tf_op jit(solution)/shard_map/ppermute | solution.py:219
  97.2 0.0 collective-permute-done.9.recv_a
  97.2 3.2 %collective-permute-done.10.recv_b = bf16[64,128]{1,0:T(8,128)(2,1)S(1)} collective-permute-done((bf16[64,128]{1,0:T(8,128)(2,1)S(1)}, bf16[64,128]{1,0:T(8,128)(2,1)S(1)}, u32[]{:S(2)}, u32[]{:S(2)}) %collective-permute-start.10) | collective-permute-done | bytes 16416 | tf_op jit(solution)/shard_map/ppermute | solution.py:219
  100.3 2.3 %shard_map.117 = bf16[512,128]{1,0:T(8,128)(2,1)} custom-call(s32[27]{0:T(128)S(1)} %bitcast.17, s32[1]{0:T(128)} %bitcast.1.parity, bf16[512,128]{1,0:T(8,128)(2,1)S(1)} %get-tuple-element.56.grad_one, bf16[64,128]{1,0:T(8,128)(2,1)S(1)} %collective-permute-done.9.recv_a, bf16[64,128]{1,0:T(8,128)(2,1)S(1)} %collective-permute-done.10.recv_b, ...), custom_call_target="tpu_custom_call" | custom-call | flops 452984832 | bytes 4000000 | tf_op jit(solution)/shard_map/pallas_call | solution.py:284
  102.7 0.6 slice.31
  103.3 0.6 slice_reduce_fusion
  105.2 0.6 multiply_bitcast_fusion
  105.8 0.0 collective-permute-done.8
  105.8 2.3 %convert_multiply_fusion = (f32[27,128,128]{2,1,0:T(8,128)}, f32[27,128,128]{2,1,0:T(8,128)}) fusion(bf16[27,128,128]{2,1,0:T(8,128)(2,1)S(1)} %collective-permute-done.8, bf16[27,128,128]{2,1,0:T(8,128)(2,1)S(1)} %bitcast.19, pred[]{:T(512)S(6)} %eq.4), kind=kLoop, calls=%fused_computation | loop fusion | flops 2654208 | bytes 5308417 | tf_op jit(solution)/shard_map/mul | solution.py:309
  (10 shorter events, 0.0 us)
Async XLA Ops:
  0.6 19.2 %copy-start.7 = (s32[1,1,27]{2,1,0:T(1,128)S(1)}, s32[1,1,27]{2,1,0:T(1,128)}, u32[]{:S(2)}) copy-start(s32[1,1,27]{2,1,0:T(1,128)} %param.12) | copy-start | bytes 328
  0.6 17.1 %copy-start.8 = (bf16[128,3]{0,1:T(4,128)(2,1)S(1)}, bf16[128,3]{0,1:T(4,128)(2,1)}, u32[]{:S(2)}) copy-start(bf16[128,3]{0,1:T(4,128)(2,1)} %param.15) | copy-start | bytes 2308
  0.7 0.9 copy-start
  1.6 0.7 copy-start.1
  2.3 0.7 copy-start.2
  2.9 16.9 %copy-start.3 = (bf16[27,128,128]{2,1,0:T(8,128)(2,1)S(1)}, bf16[27,128,128]{2,1,0:T(8,128)(2,1)}, u32[]{:S(2)}) copy-start(bf16[27,128,128]{2,1,0:T(8,128)(2,1)} %filt.6) | copy-start | bytes 2654212
  3.2 5.4 %collective-permute-start = (bf16[64,128]{1,0:T(8,128)(2,1)S(1)}, bf16[64,128]{1,0:T(8,128)(2,1)S(1)}, u32[]{:S(2)}, u32[]{:S(2)}) collective-permute-start(bf16[64,128]{1,0:T(8,128)(2,1)S(1)} %get-tuple-element.39), channel_id=1, source_target_pairs={{0,4},{4,0},{8,12},{12,8},{16,20},{20,16},{24,28},{28,24},{1,5},{5... | collective-permute-start | bytes 49160 | tf_op jit(solution)/shard_map/ppermute | solution.py:219
  5.4 5.3 %collective-permute-start.1 = (bf16[64,128]{1,0:T(8,128)(2,1)S(1)}, bf16[64,128]{1,0:T(8,128)(2,1)S(1)}, u32[]{:S(2)}, u32[]{:S(2)}) collective-permute-start(bf16[64,128]{1,0:T(8,128)(2,1)S(1)} %get-tuple-element.40), channel_id=1, source_target_pairs={{0,28},{4,8},{8,4},{12,16},{16,12},{20,24},{24,20},{28,0},{1,29},{... | collective-permute-start | bytes 49160 | tf_op jit(solution)/shard_map/ppermute | solution.py:219
  10.7 1.2 %copy-start.4 = (bf16[27,128,128]{2,1,0:T(8,128)(2,1)S(1)}, bf16[27,128,128]{2,1,0:T(8,128)(2,1)}, u32[]{:S(2)}) copy-start(bf16[27,128,128]{2,1,0:T(8,128)(2,1)} %filt.7) | copy-start | bytes 2654212
  11.8 0.7 copy-start.6
  14.4 3.4 %collective-permute-start.2 = (bf16[64,128]{1,0:T(8,128)(2,1)S(1)}, bf16[64,128]{1,0:T(8,128)(2,1)S(1)}, u32[]{:S(2)}, u32[]{:S(2)}) collective-permute-start(bf16[64,128]{1,0:T(8,128)(2,1)S(1)} %get-tuple-element.43), channel_id=1, source_target_pairs={{0,4},{4,0},{8,12},{12,8},{16,20},{20,16},{24,28},{28,24},{1,5},{5... | collective-permute-start | bytes 49160 | tf_op jit(solution)/shard_map/ppermute | solution.py:219
  14.5 5.4 %collective-permute-start.3 = (bf16[64,128]{1,0:T(8,128)(2,1)S(1)}, bf16[64,128]{1,0:T(8,128)(2,1)S(1)}, u32[]{:S(2)}, u32[]{:S(2)}) collective-permute-start(bf16[64,128]{1,0:T(8,128)(2,1)S(1)} %get-tuple-element.44), channel_id=1, source_target_pairs={{0,28},{4,8},{8,4},{12,16},{16,12},{20,24},{24,20},{28,0},{1,29},{... | collective-permute-start | bytes 49160 | tf_op jit(solution)/shard_map/ppermute | solution.py:219
  22.4 4.5 %collective-permute-start.4 = (bf16[64,128]{1,0:T(8,128)(2,1)S(1)}, bf16[64,128]{1,0:T(8,128)(2,1)S(1)}, u32[]{:S(2)}, u32[]{:S(2)}) collective-permute-start(bf16[64,128]{1,0:T(8,128)(2,1)S(1)} %get-tuple-element.47), channel_id=1, source_target_pairs={{0,4},{4,0},{8,12},{12,8},{16,20},{20,16},{24,28},{28,24},{1,5},{5... | collective-permute-start | bytes 49160 | tf_op jit(solution)/shard_map/ppermute | solution.py:219
  22.4 5.4 %collective-permute-start.5 = (bf16[64,128]{1,0:T(8,128)(2,1)S(1)}, bf16[64,128]{1,0:T(8,128)(2,1)S(1)}, u32[]{:S(2)}, u32[]{:S(2)}) collective-permute-start(bf16[64,128]{1,0:T(8,128)(2,1)S(1)} %get-tuple-element.48), channel_id=1, source_target_pairs={{0,28},{4,8},{8,4},{12,16},{16,12},{20,24},{24,20},{28,0},{1,29},{... | collective-permute-start | bytes 49160 | tf_op jit(solution)/shard_map/ppermute | solution.py:219
  31.3 6.6 %collective-permute-start.6 = (bf16[27,128,128]{2,1,0:T(8,128)(2,1)S(1)}, bf16[27,128,128]{2,1,0:T(8,128)(2,1)S(1)}, u32[]{:S(2)}, u32[]{:S(2)}) collective-permute-start(bf16[27,128,128]{2,1,0:T(8,128)(2,1)S(1)} %get-tuple-element.63), channel_id=1, source_target_pairs={{0,1},{1,0},{2,3},{3,2},{4,5},{5,4},{6,7},{7,6},{8,9},{9,8},{10,11... | collective-permute-start | bytes 2654216 | tf_op jit(solution)/shard_map/ppermute | solution.py:223
  35.9 2.0 %collective-permute-start.7 = (bf16[8,128]{1,0:T(8,128)(2,1)S(1)}, bf16[8,128]{1,0:T(8,128)(2,1)S(1)}, u32[]{:S(2)}, u32[]{:S(2)}) collective-permute-start(bf16[8,128]{1,0:T(8,128)(2,1)S(1)} %pad_maximum_fusion.small_mine), channel_id=1, source_target_pairs={{0,1},{1,0},{2,3},{3,2},{4,5},{5,4},{6,7},{7,6},{8,9},{9,8},{10,11... | collective-permute-start | bytes 6152 | tf_op jit(solution)/shard_map/ppermute | solution.py:223
  65.8 34.5 %copy-start.5 = (bf16[27,128,128]{2,1,0:T(8,128)(2,1)S(1)}, bf16[27,128,128]{2,1,0:T(8,128)(2,1)}, u32[]{:S(2)}) copy-start(bf16[27,128,128]{2,1,0:T(8,128)(2,1)} %filt.7) | copy-start | bytes 2654212
  91.9 13.8 %collective-permute-start.8 = (bf16[27,128,128]{2,1,0:T(8,128)(2,1)S(1)}, bf16[27,128,128]{2,1,0:T(8,128)(2,1)S(1)}, u32[]{:S(2)}, u32[]{:S(2)}) collective-permute-start(bf16[27,128,128]{2,1,0:T(8,128)(2,1)S(1)} %bitcast.18), channel_id=1, source_target_pairs={{0,1},{1,0},{2,3},{3,2},{4,5},{5,4},{6,7},{7,6},{8,9},{9,8},{10,11... | collective-permute-start | bytes 2654216 | tf_op jit(solution)/shard_map/ppermute | solution.py:223
  94.5 2.6 %collective-permute-start.9 = (bf16[64,128]{1,0:T(8,128)(2,1)S(1)}, bf16[64,128]{1,0:T(8,128)(2,1)S(1)}, u32[]{:S(2)}, u32[]{:S(2)}) collective-permute-start(bf16[64,128]{1,0:T(8,128)(2,1)S(1)} %get-tuple-element.57), channel_id=1, source_target_pairs={{0,4},{4,0},{8,12},{12,8},{16,20},{20,16},{24,28},{28,24},{1,5},{5... | collective-permute-start | bytes 49160 | tf_op jit(solution)/shard_map/ppermute | solution.py:219
  95.1 5.3 %collective-permute-start.10 = (bf16[64,128]{1,0:T(8,128)(2,1)S(1)}, bf16[64,128]{1,0:T(8,128)(2,1)S(1)}, u32[]{:S(2)}, u32[]{:S(2)}) collective-permute-start(bf16[64,128]{1,0:T(8,128)(2,1)S(1)} %get-tuple-element.58), channel_id=1, source_target_pairs={{0,28},{4,8},{8,4},{12,16},{16,12},{20,24},{24,20},{28,0},{1,29},{... | collective-permute-start | bytes 49160 | tf_op jit(solution)/shard_map/ppermute | solution.py:219

commit v2 on v1

--- a/solution.py
+++ b/solution.py
@@ -12,10 +12,12 @@
 LANES = 128
 TAPS = 9
 SMALL = 8
+SPACE = ("far", "near")
 F32 = jnp.float32
 BF16 = jnp.bfloat16
 PARAMS = pltpu.CompilerParams(vmem_limit_bytes=40 * 1024 * 1024)
 VMEM = pl.BlockSpec(memory_space=pltpu.VMEM)
+ANY = pl.BlockSpec(memory_space=pl.ANY)
 SMEM = pl.BlockSpec(memory_space=pltpu.SMEM)
 
 
@@ -213,10 +215,14 @@
 
 
 def swap_layers(send_a, send_b):
-    length = lax.axis_size("space")
+    length = lax.axis_size(SPACE)
     pairs_a = [(i, i ^ 1) for i in range(length)]
     pairs_b = [(i, (i + 1) % length if i % 2 else (i - 1) % length) for i in range(length)]
-    return lax.ppermute(send_a, "space", pairs_a), lax.ppermute(send_b, "space", pairs_b)
+    return lax.ppermute(send_a, SPACE, pairs_a), lax.ppermute(send_b, SPACE, pairs_b)
+
+
+def far_swap(value):
+    return lax.ppermute(value, "far", [(0, 1), (1, 0)])
 
 
 def core_swap(value):
@@ -224,41 +230,54 @@
 
 
 def split_pair(value):
-    high = value.astype(BF16)
-    return jnp.concatenate([high, (value - high.astype(F32)).astype(BF16)], axis=0)
+    high = value.astype(BF16).astype(F32)
+    return jnp.concatenate([high, value - high], axis=0)
 
 
 def join_pair(pair):
-    half = pair.shape[0] // 2
-    return pair[:half].astype(F32) + pair[half:].astype(F32)
+    return pair[: SMALL // 2] + pair[SMALL // 2 : SMALL]
 
 
 def pair_kernel(rows, peers, mine, other, small_mine, small_other, out):
-    small = join_pair(small_mine[...]) + join_pair(small_other[...])
-    tail = split_pair(small)
+    small = join_pair(small_mine[...].astype(F32)) + join_pair(small_other[...].astype(F32))
+    tail = jnp.concatenate([split_pair(small), jnp.zeros((SMALL, LANES), F32)], axis=0)
     total = mine[...].reshape(27 * LANES, LANES).astype(F32) + other[...].reshape(27 * LANES, LANES).astype(F32)
-    total = total.astype(BF16)
     spare = rows * peers - 27 * LANES
     if spare:
-        total = jnp.concatenate([total, jnp.zeros((spare, LANES), BF16)], axis=0)
+        total = jnp.concatenate([total, jnp.zeros((spare, LANES), F32)], axis=0)
     for p in range(peers):
-        out[p] = jnp.concatenate([total[p * rows : (p + 1) * rows], tail], axis=0)
-
-
-def sum_kernel(rows, peers, parts, out, small):
+        out[p] = jnp.concatenate([total[p * rows : (p + 1) * rows], tail], axis=0).astype(BF16)
+
+
+def half_kernel(rows, peers, far, parts, later_a, later_b, keep, away):
     total = parts[0].astype(F32)
-    half = SMALL // 2
     for p in range(1, peers):
         total = total + parts[p].astype(F32)
-    result = total[:rows].astype(BF16)
+    half = rows // 2
+    near_part, far_part = total[:half], total[half:rows]
+    tail = split_pair(join_pair(total[rows : rows + SMALL])).astype(BF16).astype(F32)
+    low = far[0] == 0
+    keep[...] = jnp.concatenate([jnp.where(low, near_part, far_part), tail], axis=0)
+    away[...] = jnp.concatenate([jnp.where(low, far_part, near_part), tail], axis=0).astype(BF16)
+
+
+def whole_kernel(half, keep, recv, out, small):
+    got = recv[...].astype(F32)
+    out[...] = (keep[:half] + got[:half]).astype(BF16)
+    tail = join_pair(keep[half:]) + join_pair(got[half:])
+    small[...] = jnp.concatenate([tail, jnp.zeros_like(tail)], axis=0)
+
+
+def copies_kernel(peers, far, mine, other, later, out):
+    low = far[0] == 0
+    a, b = mine[...].astype(F32), other[...].astype(F32)
+    both = jnp.concatenate([jnp.where(low, a, b), jnp.where(low, b, a)], axis=0).astype(BF16)
     for p in range(peers):
-        out[p] = result
-    tail = total[rows:]
-    small[...] = jnp.concatenate([tail[:half] + tail[half:], jnp.zeros((half, LANES), F32)], axis=0)
+        out[p] = both
 
 
 def local(classes, features, occupancy, labels, rulebook, filter_one, filter_two, head_weight):
-    parity = (lax.axis_index("space") % 2).reshape(1).astype(jnp.int32)
+    parity = (lax.axis_index(SPACE) % 2).reshape(1).astype(jnp.int32)
     rule = rulebook.reshape(27)
     head = jnp.zeros((LANES, LANES), BF16).at[:classes].set(head_weight.T)
     masked, mask, onehot, a, b = call(
@@ -286,22 +305,30 @@
     )
 
     core = lax.axis_index("core")
-    peers = lax.axis_size("space") * lax.axis_size("x")
-    rows = -(-27 * LANES // (peers * SMALL)) * SMALL
-    small_pair = split_pair(small[: SMALL // 2])
+    far = lax.axis_index("far").reshape(1).astype(jnp.int32)
+    peers = lax.axis_size("near") * lax.axis_size("x")
+    half = -(-27 * LANES // (2 * peers * SMALL)) * SMALL
+    rows = 2 * half
+    small_pair = split_pair(small[: SMALL // 2]).astype(BF16)
     mine = jnp.where(core == 0, terms_one, terms_two)
     away = jnp.where(core == 0, terms_two, terms_one)
     other, small_other = core_swap(away), core_swap(small_pair)
     chunks = call(
-        functools.partial(pair_kernel, rows, peers), sds((peers, rows + SMALL, LANES), BF16), [VMEM] * 4
+        functools.partial(pair_kernel, rows, peers), sds((peers, rows + 2 * SMALL, LANES), BF16), [VMEM] * 4
     )(mine, other, small_pair, small_other)
-    parts = lax.all_to_all(chunks, ("space", "x"), 0, 0, tiled=True)
-    copies, sums = call(
-        functools.partial(sum_kernel, rows, peers),
-        (sds((peers, rows, LANES), BF16), sds((SMALL, LANES), F32)),
-        [VMEM],
-    )(parts)
-    whole = lax.all_to_all(copies, ("space", "x"), 0, 0, tiled=True)
+    parts = lax.all_to_all(chunks, ("near", "x"), 0, 0, tiled=True)
+    keep, away = call(
+        functools.partial(half_kernel, rows, peers),
+        (sds((half + SMALL, LANES), F32), sds((half + SMALL, LANES), BF16)),
+        [SMEM, VMEM, ANY, ANY],
+    )(far, parts, g, h)
+    reduced, sums = call(
+        functools.partial(whole_kernel, half), (sds((half, LANES), BF16), sds((SMALL, LANES), F32)), [VMEM] * 2
+    )(keep, far_swap(away))
+    copies = call(
+        functools.partial(copies_kernel, peers), sds((peers, rows, LANES), BF16), [SMEM, VMEM, VMEM, ANY]
+    )(far, reduced, far_swap(reduced), grad_in)
+    whole = lax.all_to_all(copies, ("near", "x"), 0, 0, tiled=True)
     whole = whole.reshape(peers * rows, LANES)[: 27 * LANES].reshape(27, LANES, LANES)
     whole_other = core_swap(whole)
     scale = 1.0 / VOX
@@ -318,13 +345,13 @@
 
 def solution(mesh):
     shape = mesh.devices.shape
-    inner = Mesh(mesh.devices.reshape(shape[0], shape[1] // 2, 2), ("space", "x", "core"))
+    inner = Mesh(mesh.devices.reshape(2, shape[0] // 2, shape[1] // 2, 2), ("far", "near", "x", "core"))
     parts = ("x", "core")
     placed = (
-        P(parts, "space", None, None),
-        P(parts, "space", None),
-        P(parts, "space", None),
-        P(parts, "space", None),
+        P(parts, SPACE, None, None),
+        P(parts, SPACE, None),
+        P(parts, SPACE, None),
+        P(parts, SPACE, None),
         P(),
         P(),
         P(),
@@ -335,7 +362,7 @@
             functools.partial(local, head_weight.shape[1]),
             mesh=inner,
             in_specs=placed,
-            out_specs=(P(), P(), P(), P(), P(parts, "space", None, None)),
+            out_specs=(P(), P(), P(), P(), P(parts, SPACE, None, None)),
             check_vma=False,
         )
         return step(features, occupancy, labels, rulebook, filter_one, filter_two, head_weight)

time: 111 us -> 93.1 us (0.84); the launches traced: 109 us -> 92.8 us
  blocking collectives: 53.6 us -> 14.5 us
  waiting for transfers between devices: 10 us -> 22.9 us
  starting transfers between devices: 22.1 us -> 28.9 us
  local copies, waits for them, and re-layouts: 4.69 us -> 6.7 us
    all_to_all x2 -> x1, blocking collectives: 53.6 us -> 14.5 us  [local(): whole = lax.all_to_all(copies, ('near', 'x'), 0, 0, tiled=True)]
    ppermute x8 -> x10, waiting for transfers between devices: 8.07 us -> 21 us  [the longest x4 14.7 us: swap_layers(): lax.ppermute(send_b, SPACE, pairs_b)]
    all_to_all x0 -> x1, starting transfers between devices: none -> 3.68 us  [local(): parts = lax.all_to_all(chunks, ('near', 'x'), 0, 0, tiled=True)]
    unnamed x18 -> x24, local copies, waits for them, and re-layouts: 4.1 us -> 6.11 us
    ppermute x8 -> x10, starting transfers between devices: 14.8 us -> 16.8 us  [the longest x4 13 us: swap_layers(): lax.ppermute(send_b, SPACE, pairs_b)]
    ppermute x3, starting transfers between devices: 7.22 us -> 8.43 us  [core_swap(): return lax.ppermute(value, 'core', [(0, 1), (1, 0)])]
  transfers between devices with their start and end apart: 11 -> 14, of which waited for: 5 -> 8; matrix products, arithmetic and copies ran while one was open for 2% -> 2% of each run, Pallas kernels for 3% -> 4%
where the time goes in v2:
time: 93.1 us; the launch traced here: 92.8 us
  starting transfers between devices  28.9 us (31%)
  waiting for transfers between devices  22.9 us (25%)
  blocking collectives  14.5 us (16%)
  Pallas kernels  12.9 us (14%)
  local copies, waits for them, and re-layouts  6.7 us (7%)
  other arithmetic  3.59 us (4%)
  between operations  3.29 us (4%)
    ppermute x4, waiting for transfers between devices, swap_layers(): lax.ppermute(send_b, SPACE, pairs_b)  14.7 us
    all_to_all x1, blocking collectives, local(): whole = lax.all_to_all(copies, ('near', 'x'), 0, 0, tiled=True)  14.5 us
    ppermute x4, starting transfers between devices, swap_layers(): lax.ppermute(send_b, SPACE, pairs_b)  13 us
    ppermute x3, starting transfers between devices, core_swap(): return lax.ppermute(value, 'core', [(0, 1), (1, 0)])  8.43 us
    unnamed x24, local copies, waits for them, and re-layouts  6.11 us
    ppermute x2, waiting for transfers between devices, far_swap(): return lax.ppermute(value, 'far', [(0, 1), (1, 0)])  6.02 us
    all_to_all x1, starting transfers between devices, local(): parts = lax.all_to_all(chunks, ('near', 'x'), 0, 0, tiled=True)  3.68 us
    ppermute x4, starting transfers between devices, swap_layers(): lax.ppermute(send_a, SPACE, pairs_a)  3.57 us
  transfers between devices with their start and end apart: 14, of which 8 were waited for; matrix products, arithmetic and copies ran while one was open for 2% of the time, Pallas kernels for 4%

profile of v2, /device:TPU:1, one launch (start us, length us, event | category | flops | bytes accessed | tf_op | source)
XLA Modules:
  0.0 92.8 jit_solution(6742907110180838041)
XLA Ops:
  0.6 0.0 copy-start.8
  0.7 0.9 copy-done
  1.6 0.7 copy-done.2
  2.3 0.7 copy-done.3
  2.9 0.3 shard_map.110
  3.3 2.1 %collective-permute-start = (bf16[64,128]{1,0:T(8,128)(2,1)S(1)}, bf16[64,128]{1,0:T(8,128)(2,1)S(1)}, u32[]{:S(2)}, u32[]{:S(2)}) collective-permute-start(bf16[64,128]{1,0:T(8,128)(2,1)S(1)} %get-tuple-element.41), channel_id=1, source_target_pairs={{0,4},{4,0},{8,12},{12,8},{16,20},{20,16},{24,28},{28,24},{1,5},{5... | collective-permute-start | bytes 49160 | tf_op jit(solution)/shard_map/ppermute | solution.py:221
  5.4 3.3 %collective-permute-start.1 = (bf16[64,128]{1,0:T(8,128)(2,1)S(1)}, bf16[64,128]{1,0:T(8,128)(2,1)S(1)}, u32[]{:S(2)}, u32[]{:S(2)}) collective-permute-start(bf16[64,128]{1,0:T(8,128)(2,1)S(1)} %get-tuple-element.42), channel_id=1, source_target_pairs={{0,28},{4,8},{8,4},{12,16},{16,12},{20,24},{24,20},{28,0},{1,29},{... | collective-permute-start | bytes 49160 | tf_op jit(solution)/shard_map/ppermute | solution.py:221
  8.7 0.0 collective-permute-done.recv_a
  8.7 2.0 %collective-permute-done.1.recv_b = bf16[64,128]{1,0:T(8,128)(2,1)S(1)} collective-permute-done((bf16[64,128]{1,0:T(8,128)(2,1)S(1)}, bf16[64,128]{1,0:T(8,128)(2,1)S(1)}, u32[]{:S(2)}, u32[]{:S(2)}) %collective-permute-start.1) | collective-permute-done | bytes 16416 | tf_op jit(solution)/shard_map/ppermute | solution.py:221
  10.7 1.2 %copy-done.5 = bf16[27,128,128]{2,1,0:T(8,128)(2,1)S(1)} copy-done((bf16[27,128,128]{2,1,0:T(8,128)(2,1)S(1)}, bf16[27,128,128]{2,1,0:T(8,128)(2,1)}, u32[]{:S(2)}) %copy-start.5) | copy-done | bytes 884760
  11.8 0.7 copy-done.7
  12.5 1.9 %shard_map.111 = (bf16[640,1152]{1,0:T(8,128)(2,1)S(1)}, bf16[512,128]{1,0:T(8,128)(2,1)S(1)}, f32[512,128]{1,0:T(8,128)S(1)}, bf16[64,128]{1,0:T(8,128)(2,1)S(1)}, bf16[64,128]{1,0:T(8,128)(2,1)S(1)}) custom-call(s32[27]{0:T(128)S(1)} %bitcast.16, s32[1]{0:T(128)} %bitcast.2.parity, bf16[512,128]{1,0:T(8,128)(2,1)S(1)} %get-tuple-element.40.masked, ...), custom_call_target="tpu_custom_call" | custom-call | flops 452984832 | bytes 4000000 | tf_op jit(solution)/shard_map/pallas_call | solution.py:287
  14.4 0.0 copy-start.9
  14.4 1.1 %copy-done.9 = bf16[640,1152]{1,0:T(8,128)(2,1)} copy-done((bf16[640,1152]{1,0:T(8,128)(2,1)}, bf16[640,1152]{1,0:T(8,128)(2,1)S(1)}, u32[]{:S(2)}) %copy-start.9) | copy-done | bytes 1474584
  15.5 0.0 collective-permute-start.2
  15.5 3.3 %collective-permute-start.3 = (bf16[64,128]{1,0:T(8,128)(2,1)S(1)}, bf16[64,128]{1,0:T(8,128)(2,1)S(1)}, u32[]{:S(2)}, u32[]{:S(2)}) collective-permute-start(bf16[64,128]{1,0:T(8,128)(2,1)S(1)} %get-tuple-element.46), channel_id=1, source_target_pairs={{0,28},{4,8},{8,4},{12,16},{16,12},{20,24},{24,20},{28,0},{1,29},{... | collective-permute-start | bytes 49160 | tf_op jit(solution)/shard_map/ppermute | solution.py:221
  18.8 2.0 %collective-permute-done.3.recv_b = bf16[64,128]{1,0:T(8,128)(2,1)S(1)} collective-permute-done((bf16[64,128]{1,0:T(8,128)(2,1)S(1)}, bf16[64,128]{1,0:T(8,128)(2,1)S(1)}, u32[]{:S(2)}, u32[]{:S(2)}) %collective-permute-start.3) | collective-permute-done | bytes 16416 | tf_op jit(solution)/shard_map/ppermute | solution.py:221
  20.8 2.5 %shard_map.112 = (bf16[640,1152]{1,0:T(8,128)(2,1)S(1)}, bf16[512,128]{1,0:T(8,128)(2,1)S(1)}, f32[8,128]{1,0:T(8,128)S(1)}, bf16[64,128]{1,0:T(8,128)(2,1)S(1)}, bf16[64,128]{1,0:T(8,128)(2,1)S(1)}) custom-call(s32[27]{0:T(128)S(1)} %bitcast.17, s32[1]{0:T(128)} %bitcast.2.parity, bf16[512,128]{1,0:T(8,128)(2,1)S(1)} %get-tuple-element.44.act_one, ...), custom_call_target="tpu_custom_call" | custom-call | flops 452984832 | bytes 4000000 | tf_op jit(solution)/shard_map/pallas_call | solution.py:291
  23.4 0.1 collective-permute-start.4
  23.5 3.3 %collective-permute-start.5 = (bf16[64,128]{1,0:T(8,128)(2,1)S(1)}, bf16[64,128]{1,0:T(8,128)(2,1)S(1)}, u32[]{:S(2)}, u32[]{:S(2)}) collective-permute-start(bf16[64,128]{1,0:T(8,128)(2,1)S(1)} %get-tuple-element.50), channel_id=1, source_target_pairs={{0,28},{4,8},{8,4},{12,16},{16,12},{20,24},{24,20},{28,0},{1,29},{... | collective-permute-start | bytes 49160 | tf_op jit(solution)/shard_map/ppermute | solution.py:221
  26.8 1.1 %shard_map.114 = bf16[27,128,128]{2,1,0:T(8,128)(2,1)S(1)} custom-call(bf16[640,1152]{1,0:T(8,128)(2,1)S(1)} %get-tuple-element.54.win, bf16[512,128]{1,0:T(8,128)(2,1)S(1)} %get-tuple-element.48.grad_two.grad), custom_call_target="tpu_custom_call" | custom-call | flops 452984832 | bytes 4000000 | tf_op jit(solution)/shard_map/pallas_call | solution.py:298
  27.9 0.9 collective-permute-done.5.recv_b
  28.8 3.4 %shard_map.113 = (bf16[512,128]{1,0:T(8,128)(2,1)S(1)}, bf16[27,128,128]{2,1,0:T(8,128)(2,1)S(1)}, bf16[64,128]{1,0:T(8,128)(2,1)S(1)}, bf16[64,128]{1,0:T(8,128)(2,1)S(1)}) custom-call(s32[27]{0:T(128)S(1)} %bitcast.18, s32[1]{0:T(128)} %bitcast.2.parity, bf16[512,128]{1,0:T(8,128)(2,1)S(1)} %get-tuple-element.48.grad_two.grad, ...), custom_call_target="tpu_custom_call" | custom-call | flops 905969664 | bytes 4000000 | tf_op jit(solution)/shard_map/pallas_call | solution.py:299
  32.2 0.1 broadcast_select_fusion
  32.3 4.6 %collective-permute-start.6 = (bf16[27,128,128]{2,1,0:T(8,128)(2,1)S(1)}, bf16[27,128,128]{2,1,0:T(8,128)(2,1)S(1)}, u32[]{:S(2)}, u32[]{:S(2)}) collective-permute-start(bf16[27,128,128]{2,1,0:T(8,128)(2,1)S(1)} %get-tuple-element.67), channel_id=1, source_target_pairs={{0,1},{1,0},{2,3},{3,2},{4,5},{5,4},{6,7},{7,6},{8,9},{9,8},{10,11... | collective-permute-start | bytes 2654216 | tf_op jit(solution)/shard_map/ppermute | solution.py:229
  36.9 0.1 collective-permute-start.7
  37.0 1.9 %collective-permute-done.7.small_other = bf16[8,128]{1,0:T(8,128)(2,1)S(1)} collective-permute-done((bf16[8,128]{1,0:T(8,128)(2,1)S(1)}, bf16[8,128]{1,0:T(8,128)(2,1)S(1)}, u32[]{:S(2)}, u32[]{:S(2)}) %collective-permute-start.7) | collective-permute-done | bytes 2080 | tf_op jit(solution)/shard_map/ppermute | solution.py:229
  38.9 1.1 %shard_map.115 = bf16[8,448,128]{2,1,0:T(8,128)(2,1)} custom-call(bf16[27,128,128]{2,1,0:T(8,128)(2,1)S(1)} %get-tuple-element.68.mine, bf16[27,128,128]{2,1,0:T(8,128)(2,1)S(1)} %collective-permute-done.6.other, bf16[8,128]{1,0:T(8,128)(2,1)S(1)} %pad_maximum_fusion.small_mine, bf16[8,128]{1,0:T(8,128)(2,1)S(1)} %collective-permute-done.7.small_other), custom_call_target="tpu_custom_call" | custom-call | bytes 4000000 | tf_op jit(solution)/shard_map/pallas_call | solution.py:316
  40.1 3.7 %all-to-all-start = ((bf16[8,448,128]{2,1,0:T(8,128)(2,1)}), bf16[8,448,128]{2,1,0:T(8,128)(2,1)S(1)}, u32[]{:S(2)}, u32[]{:S(2)}) async-start(bf16[8,448,128]{2,1,0:T(8,128)(2,1)} %shard_map.115), calls=%async_computation | async-start | bytes 1835008 | tf_op jit(solution)/shard_map/all_to_all | solution.py:319
  43.8 1.4 %collective-permute-start.8 = (bf16[64,128]{1,0:T(8,128)(2,1)S(1)}, bf16[64,128]{1,0:T(8,128)(2,1)S(1)}, u32[]{:S(2)}, u32[]{:S(2)}) collective-permute-start(bf16[64,128]{1,0:T(8,128)(2,1)S(1)} %get-tuple-element.56), channel_id=1, source_target_pairs={{0,4},{4,0},{8,12},{12,8},{16,20},{20,16},{24,28},{28,24},{1,5},{5... | collective-permute-start | bytes 49160 | tf_op jit(solution)/shard_map/ppermute | solution.py:221
  45.1 3.2 %collective-permute-start.9 = (bf16[64,128]{1,0:T(8,128)(2,1)S(1)}, bf16[64,128]{1,0:T(8,128)(2,1)S(1)}, u32[]{:S(2)}, u32[]{:S(2)}) collective-permute-start(bf16[64,128]{1,0:T(8,128)(2,1)S(1)} %get-tuple-element.57), channel_id=1, source_target_pairs={{0,28},{4,8},{8,4},{12,16},{16,12},{20,24},{24,20},{28,0},{1,29},{... | collective-permute-start | bytes 49160 | tf_op jit(solution)/shard_map/ppermute | solution.py:221
  48.3 0.3 collective-permute-done.8.later_a.recv_a
  48.6 9.7 %collective-permute-done.9.later_b.recv_b = bf16[64,128]{1,0:T(8,128)(2,1)S(1)} collective-permute-done((bf16[64,128]{1,0:T(8,128)(2,1)S(1)}, bf16[64,128]{1,0:T(8,128)(2,1)S(1)}, u32[]{:S(2)}, u32[]{:S(2)}) %collective-permute-start.9) | collective-permute-done | bytes 16416 | tf_op jit(solution)/shard_map/ppermute | solution.py:221
  58.3 0.0 all-to-all-done.parts
  58.3 0.1 shard_map.116
  58.5 0.1 collective-permute-start.10
  58.6 4.5 %collective-permute-done.10.recv = bf16[224,128]{1,0:T(8,128)(2,1)S(1)} collective-permute-done((bf16[224,128]{1,0:T(8,128)(2,1)S(1)}, bf16[224,128]{1,0:T(8,128)(2,1)S(1)}, u32[]{:S(2)}, u32[]{:S(2)}) %collective-permute-start.10) | collective-permute-done | bytes 57376 | tf_op jit(solution)/shard_map/ppermute | solution.py:225
  63.0 0.1 collective-permute-start.11
  63.1 2.3 %shard_map.118.later = bf16[512,128]{1,0:T(8,128)(2,1)} custom-call(s32[27]{0:T(128)S(1)} %bitcast.19, s32[1]{0:T(128)} %bitcast.2.parity, bf16[512,128]{1,0:T(8,128)(2,1)S(1)} %get-tuple-element.61.grad_one, bf16[64,128]{1,0:T(8,128)(2,1)S(1)} %collective-permute-done.8.later_a.recv_a, bf16[64,128]{1,0:T(8,128)(2,1)S(1)} %collective-permute-done.9.later_b.recv_b, ...), custom_call_target="tpu_custom_call" | custom-call | flops 452984832 | bytes 4000000 | tf_op jit(solution)/shard_map/pallas_call | solution.py:303
  65.5 1.6 %collective-permute-done.11.other = bf16[216,128]{1,0:T(8,128)(2,1)S(1)} collective-permute-done((bf16[216,128]{1,0:T(8,128)(2,1)S(1)}, bf16[216,128]{1,0:T(8,128)(2,1)S(1)}, u32[]{:S(2)}, u32[]{:S(2)}) %collective-permute-start.11) | collective-permute-done | bytes 55328 | tf_op jit(solution)/shard_map/ppermute | solution.py:225
  67.0 0.9 copy-done.1
  67.9 0.1 shard_map.119
  68.0 14.5 %all_to_all.10 = bf16[8,432,128]{2,1,0:T(8,128)(2,1)S(1)} all-to-all(bf16[8,432,128]{2,1,0:T(8,128)(2,1)S(1)} %shard_map.119), channel_id=1, replica_groups=mesh['far'=2,'near'=4,'x'=2,'core'=2] {'near','x'}, dimensions={0} | all-to-all | bytes 1769472 | tf_op jit(solution)/shard_map/all_to_all | solution.py:331
  82.5 3.8 %collective-permute-start.12 = (bf16[27,128,128]{2,1,0:T(8,128)(2,1)S(1)}, bf16[27,128,128]{2,1,0:T(8,128)(2,1)S(1)}, u32[]{:S(2)}, u32[]{:S(2)}) collective-permute-start(bf16[27,128,128]{2,1,0:T(8,128)(2,1)S(1)} %bitcast.20), channel_id=1, source_target_pairs={{0,1},{1,0},{2,3},{3,2},{4,5},{5,4},{6,7},{7,6},{8,9},{9,8},{10,11... | collective-permute-start | bytes 2654216 | tf_op jit(solution)/shard_map/ppermute | solution.py:229
  86.2 0.6 slice.31
  86.8 0.6 slice_reduce_fusion
  88.8 0.6 multiply_bitcast_fusion
  89.4 2.3 %convert_multiply_fusion = (f32[27,128,128]{2,1,0:T(8,128)}, f32[27,128,128]{2,1,0:T(8,128)}) fusion(bf16[27,128,128]{2,1,0:T(8,128)(2,1)S(1)} %collective-permute-done.12, bf16[27,128,128]{2,1,0:T(8,128)(2,1)S(1)} %bitcast.21, pred[]{:T(512)S(6)} %eq.4), kind=kLoop, calls=%fused_computation | loop fusion | flops 2654208 | bytes 5308417 | tf_op jit(solution)/shard_map/mul | solution.py:336
  (23 shorter events, 0.1 us)
Async XLA Ops:
  0.6 20.2 %copy-start.8 = (s32[1,1,27]{2,1,0:T(1,128)S(1)}, s32[1,1,27]{2,1,0:T(1,128)}, u32[]{:S(2)}) copy-start(s32[1,1,27]{2,1,0:T(1,128)} %param.12) | copy-start | bytes 328
  0.6 18.1 %copy-start.11 = (bf16[128,3]{0,1:T(4,128)(2,1)S(1)}, bf16[128,3]{0,1:T(4,128)(2,1)}, u32[]{:S(2)}) copy-start(bf16[128,3]{0,1:T(4,128)(2,1)} %param.15) | copy-start | bytes 2308
  0.7 0.9 copy-start
  1.6 0.7 copy-start.2
  2.3 0.7 copy-start.3
  2.9 17.9 %copy-start.4 = (bf16[27,128,128]{2,1,0:T(8,128)(2,1)S(1)}, bf16[27,128,128]{2,1,0:T(8,128)(2,1)}, u32[]{:S(2)}) copy-start(bf16[27,128,128]{2,1,0:T(8,128)(2,1)} %filt.6) | copy-start | bytes 2654212
  3.3 5.4 %collective-permute-start = (bf16[64,128]{1,0:T(8,128)(2,1)S(1)}, bf16[64,128]{1,0:T(8,128)(2,1)S(1)}, u32[]{:S(2)}, u32[]{:S(2)}) collective-permute-start(bf16[64,128]{1,0:T(8,128)(2,1)S(1)} %get-tuple-element.41), channel_id=1, source_target_pairs={{0,4},{4,0},{8,12},{12,8},{16,20},{20,16},{24,28},{28,24},{1,5},{5... | collective-permute-start | bytes 49160 | tf_op jit(solution)/shard_map/ppermute | solution.py:221
  5.4 5.3 %collective-permute-start.1 = (bf16[64,128]{1,0:T(8,128)(2,1)S(1)}, bf16[64,128]{1,0:T(8,128)(2,1)S(1)}, u32[]{:S(2)}, u32[]{:S(2)}) collective-permute-start(bf16[64,128]{1,0:T(8,128)(2,1)S(1)} %get-tuple-element.42), channel_id=1, source_target_pairs={{0,28},{4,8},{8,4},{12,16},{16,12},{20,24},{24,20},{28,0},{1,29},{... | collective-permute-start | bytes 49160 | tf_op jit(solution)/shard_map/ppermute | solution.py:221
  10.7 1.2 %copy-start.5 = (bf16[27,128,128]{2,1,0:T(8,128)(2,1)S(1)}, bf16[27,128,128]{2,1,0:T(8,128)(2,1)}, u32[]{:S(2)}) copy-start(bf16[27,128,128]{2,1,0:T(8,128)(2,1)} %filt.7) | copy-start | bytes 2654212
  11.8 0.7 copy-start.7
  14.4 1.1 %copy-start.9 = (bf16[640,1152]{1,0:T(8,128)(2,1)}, bf16[640,1152]{1,0:T(8,128)(2,1)S(1)}, u32[]{:S(2)}) copy-start(bf16[640,1152]{1,0:T(8,128)(2,1)S(1)} %get-tuple-element.52.win_one) | copy-start | bytes 4423684
  15.5 3.3 %collective-permute-start.2 = (bf16[64,128]{1,0:T(8,128)(2,1)S(1)}, bf16[64,128]{1,0:T(8,128)(2,1)S(1)}, u32[]{:S(2)}, u32[]{:S(2)}) collective-permute-start(bf16[64,128]{1,0:T(8,128)(2,1)S(1)} %get-tuple-element.45), channel_id=1, source_target_pairs={{0,4},{4,0},{8,12},{12,8},{16,20},{20,16},{24,28},{28,24},{1,5},{5... | collective-permute-start | bytes 49160 | tf_op jit(solution)/shard_map/ppermute | solution.py:221
  15.5 5.3 %collective-permute-start.3 = (bf16[64,128]{1,0:T(8,128)(2,1)S(1)}, bf16[64,128]{1,0:T(8,128)(2,1)S(1)}, u32[]{:S(2)}, u32[]{:S(2)}) collective-permute-start(bf16[64,128]{1,0:T(8,128)(2,1)S(1)} %get-tuple-element.46), channel_id=1, source_target_pairs={{0,28},{4,8},{8,4},{12,16},{16,12},{20,24},{24,20},{28,0},{1,29},{... | collective-permute-start | bytes 49160 | tf_op jit(solution)/shard_map/ppermute | solution.py:221
  20.8 8.0 %copy-start.10 = (bf16[640,1152]{1,0:T(8,128)(2,1)S(1)}, bf16[640,1152]{1,0:T(8,128)(2,1)}, u32[]{:S(2)}) copy-start(bf16[640,1152]{1,0:T(8,128)(2,1)} %copy-done.9) | copy-start | bytes 4423684
  23.4 4.6 %collective-permute-start.4 = (bf16[64,128]{1,0:T(8,128)(2,1)S(1)}, bf16[64,128]{1,0:T(8,128)(2,1)S(1)}, u32[]{:S(2)}, u32[]{:S(2)}) collective-permute-start(bf16[64,128]{1,0:T(8,128)(2,1)S(1)} %get-tuple-element.49), channel_id=1, source_target_pairs={{0,4},{4,0},{8,12},{12,8},{16,20},{20,16},{24,28},{28,24},{1,5},{5... | collective-permute-start | bytes 49160 | tf_op jit(solution)/shard_map/ppermute | solution.py:221
  23.5 5.4 %collective-permute-start.5 = (bf16[64,128]{1,0:T(8,128)(2,1)S(1)}, bf16[64,128]{1,0:T(8,128)(2,1)S(1)}, u32[]{:S(2)}, u32[]{:S(2)}) collective-permute-start(bf16[64,128]{1,0:T(8,128)(2,1)S(1)} %get-tuple-element.50), channel_id=1, source_target_pairs={{0,28},{4,8},{8,4},{12,16},{16,12},{20,24},{24,20},{28,0},{1,29},{... | collective-permute-start | bytes 49160 | tf_op jit(solution)/shard_map/ppermute | solution.py:221
  32.3 6.6 %collective-permute-start.6 = (bf16[27,128,128]{2,1,0:T(8,128)(2,1)S(1)}, bf16[27,128,128]{2,1,0:T(8,128)(2,1)S(1)}, u32[]{:S(2)}, u32[]{:S(2)}) collective-permute-start(bf16[27,128,128]{2,1,0:T(8,128)(2,1)S(1)} %get-tuple-element.67), channel_id=1, source_target_pairs={{0,1},{1,0},{2,3},{3,2},{4,5},{5,4},{6,7},{7,6},{8,9},{9,8},{10,11... | collective-permute-start | bytes 2654216 | tf_op jit(solution)/shard_map/ppermute | solution.py:229
  36.9 2.0 %collective-permute-start.7 = (bf16[8,128]{1,0:T(8,128)(2,1)S(1)}, bf16[8,128]{1,0:T(8,128)(2,1)S(1)}, u32[]{:S(2)}, u32[]{:S(2)}) collective-permute-start(bf16[8,128]{1,0:T(8,128)(2,1)S(1)} %pad_maximum_fusion.small_mine), channel_id=1, source_target_pairs={{0,1},{1,0},{2,3},{3,2},{4,5},{5,4},{6,7},{7,6},{8,9},{9,8},{10,11... | collective-permute-start | bytes 6152 | tf_op jit(solution)/shard_map/ppermute | solution.py:229
  40.1 23.0 %copy-start.6 = (bf16[27,128,128]{2,1,0:T(8,128)(2,1)S(1)}, bf16[27,128,128]{2,1,0:T(8,128)(2,1)}, u32[]{:S(2)}) copy-start(bf16[27,128,128]{2,1,0:T(8,128)(2,1)} %filt.7) | copy-start | bytes 2654212
  40.1 18.3 %all-to-all-start = ((bf16[8,448,128]{2,1,0:T(8,128)(2,1)}), bf16[8,448,128]{2,1,0:T(8,128)(2,1)S(1)}, u32[]{:S(2)}, u32[]{:S(2)}) async-start(bf16[8,448,128]{2,1,0:T(8,128)(2,1)} %shard_map.115), calls=%async_computation | async-start | bytes 1835008 | tf_op jit(solution)/shard_map/all_to_all | solution.py:319
  43.8 4.8 %collective-permute-start.8 = (bf16[64,128]{1,0:T(8,128)(2,1)S(1)}, bf16[64,128]{1,0:T(8,128)(2,1)S(1)}, u32[]{:S(2)}, u32[]{:S(2)}) collective-permute-start(bf16[64,128]{1,0:T(8,128)(2,1)S(1)} %get-tuple-element.56), channel_id=1, source_target_pairs={{0,4},{4,0},{8,12},{12,8},{16,20},{20,16},{24,28},{28,24},{1,5},{5... | collective-permute-start | bytes 49160 | tf_op jit(solution)/shard_map/ppermute | solution.py:221
  45.1 13.2 %collective-permute-start.9 = (bf16[64,128]{1,0:T(8,128)(2,1)S(1)}, bf16[64,128]{1,0:T(8,128)(2,1)S(1)}, u32[]{:S(2)}, u32[]{:S(2)}) collective-permute-start(bf16[64,128]{1,0:T(8,128)(2,1)S(1)} %get-tuple-element.57), channel_id=1, source_target_pairs={{0,28},{4,8},{8,4},{12,16},{16,12},{20,24},{24,20},{28,0},{1,29},{... | collective-permute-start | bytes 49160 | tf_op jit(solution)/shard_map/ppermute | solution.py:221
  58.5 4.5 %collective-permute-start.10 = (bf16[224,128]{1,0:T(8,128)(2,1)S(1)}, bf16[224,128]{1,0:T(8,128)(2,1)S(1)}, u32[]{:S(2)}, u32[]{:S(2)}) collective-permute-start(bf16[224,128]{1,0:T(8,128)(2,1)S(1)} %get-tuple-element.59), channel_id=1, source_target_pairs={{0,16},{16,0},{1,17},{17,1},{2,18},{18,2},{3,19},{19,3},{4,20},{20... | collective-permute-start | bytes 172040 | tf_op jit(solution)/shard_map/ppermute | solution.py:225
  63.0 4.0 %collective-permute-start.11 = (bf16[216,128]{1,0:T(8,128)(2,1)S(1)}, bf16[216,128]{1,0:T(8,128)(2,1)S(1)}, u32[]{:S(2)}, u32[]{:S(2)}) collective-permute-start(bf16[216,128]{1,0:T(8,128)(2,1)S(1)} %get-tuple-element.60.mine), channel_id=1, source_target_pairs={{0,16},{16,0},{1,17},{17,1},{2,18},{18,2},{3,19},{19,3},{4,20},{20... | collective-permute-start | bytes 165896 | tf_op jit(solution)/shard_map/ppermute | solution.py:225
  67.0 0.9 copy-start.1
  82.5 6.9 %collective-permute-start.12 = (bf16[27,128,128]{2,1,0:T(8,128)(2,1)S(1)}, bf16[27,128,128]{2,1,0:T(8,128)(2,1)S(1)}, u32[]{:S(2)}, u32[]{:S(2)}) collective-permute-start(bf16[27,128,128]{2,1,0:T(8,128)(2,1)S(1)} %bitcast.20), channel_id=1, source_target_pairs={{0,1},{1,0},{2,3},{3,2},{4,5},{5,4},{6,7},{7,6},{8,9},{9,8},{10,11... | collective-permute-start | bytes 2654216 | tf_op jit(solution)/shard_map/ppermute | solution.py:229

commit v3 on v2

v3 whole, which is shorter than its diff:
```python
import functools

import jax
import jax.numpy as jnp
from jax import lax
from jax.experimental import pallas as pl
from jax.experimental.pallas import tpu as pltpu
from jax.sharding import Mesh, PartitionSpec as P

EDGE = 8
VOX = 512
LANES = 128
TAPS = 9
SMALL = 8
SPACE = ("far", "near")
F32 = jnp.float32
BF16 = jnp.bfloat16
PARAMS = pltpu.CompilerParams(vmem_limit_bytes=16 * 1024 * 1024)
VMEM = pl.BlockSpec(memory_space=pltpu.VMEM)
ANY = pl.BlockSpec(memory_space=pl.ANY)
SMEM = pl.BlockSpec(memory_space=pltpu.SMEM)


def sds(shape, dtype):
    return jax.ShapeDtypeStruct(shape, dtype)


def contract(a, b, dim_a, dim_b):
    return lax.dot_general(a, b, (((dim_a,), (dim_b,)), ((), ())), preferred_element_type=F32)


def spread_layer(layer):
    return jnp.broadcast_to(layer.astype(F32).reshape(64, 1, LANES), (64, EDGE, LANES))


def from_sides(parity_ref, recv_a, recv_b):
    even = parity_ref[0] == 0
    got_a, got_b = recv_a.astype(F32), recv_b.astype(F32)
    return jnp.where(even, got_b, got_a), jnp.where(even, got_a, got_b)


def build_windows(block, below, above, rule_ref, out_ref):
    cells = block.reshape(64, EDGE, LANES)
    depth = lax.broadcasted_iota(jnp.int32, (1, EDGE, LANES), 1)

    def flag(i, j, k, wanted):
        offset = 9 * i + 3 * j + k
        return jnp.where(rule_ref[offset : offset + 1, :] == wanted, 1.0, 0.0).reshape(1, 1, LANES)

    for k in range(3):
        if k == 1:
            own, other = cells, None
        elif k == 0:
            own, other = pltpu.roll(cells, 1, 1), spread_layer(below)
        else:
            own, other = pltpu.roll(cells, EDGE - 1, 1), spread_layer(above)
        own = own.reshape(EDGE, EDGE, EDGE, LANES)
        if other is not None:
            other = other.reshape(EDGE, EDGE, EDGE, LANES)

        def region(i, j):
            xs = {0: slice(7, 8), 1: slice(0, 8), 2: slice(0, 1)}[i]
            ys = {0: slice(7, 8), 1: slice(0, 8), 2: slice(0, 1)}[j]
            inner = flag(i, j, 1, 0)
            if k == 1:
                return own[xs, ys] * inner[None]
            edge = depth == (0 if k == 0 else EDGE - 1)
            keep = jnp.where(edge, flag(i, j, k, 0), inner)
            take = jnp.where(edge, flag(i, j, k, 1 if k == 0 else 2), 0.0)
            return own[xs, ys] * keep[None] + other[xs, ys] * take[None]

        columns = [jnp.concatenate([region(i, j) for i in range(3)], axis=0).astype(F32) for j in range(3)]
        for j in range(3):
            if j == 0:
                padded = jnp.concatenate([columns[0], columns[1][:, :7]], axis=1)
            elif j == 1:
                padded = columns[1]
            else:
                padded = jnp.concatenate([columns[1][:, 1:], columns[2]], axis=1)
            lane = (3 * j + k) * LANES
            out_ref[:, lane : lane + LANES] = padded.reshape(640, LANES).astype(BF16)


def put_sides(parity_ref, upward, downward, send_a_ref, send_b_ref):
    even = parity_ref[0] == 0
    send_a_ref[...] = jnp.where(even, upward, downward).astype(BF16)
    send_b_ref[...] = jnp.where(even, downward, upward).astype(BF16)


def layers_of(block):
    cells = block.reshape(64, EDGE, LANES)
    return lambda z: cells[:, z, :]


def put_layers(block, parity_ref, send_a_ref, send_b_ref):
    layer = layers_of(block)
    put_sides(parity_ref, layer(EDGE - 1), layer(0), send_a_ref, send_b_ref)


def layer_windows(side, mine, touching, rule, out_ref, row):
    near, behind, wrap = (part.reshape(EDGE, EDGE, LANES) for part in side)
    mine = mine.reshape(EDGE, EDGE, LANES)
    across = 2 if touching == EDGE - 1 else 0
    width = lax.broadcasted_iota(jnp.int32, (1, EDGE, LANES), 1)

    def flag(i, j, k, wanted):
        offset = 9 * i + 3 * j + k
        return jnp.where(rule[offset : offset + 1, :] == wanted, 1.0, 0.0).reshape(1, 1, LANES)

    for k in range(3):
        sources = [(near if k == 1 else behind, 1, 0)]
        if k == across:
            sources = [(wrap, k, 0), (mine, k, 2 if across == 2 else 1)]
        for j in range(3):
            base = first = last = None
            for layer, region, wanted in sources:
                turned = layer if j == 1 else pltpu.roll(layer, 1 if j == 0 else EDGE - 1, 1)

                def gate(i):
                    inner = flag(i, 1, region, wanted)
                    if j == 1:
                        return inner
                    return jnp.where(width == (0 if j == 0 else EDGE - 1), flag(i, j, region, wanted), inner)

                parts = turned * gate(1), turned[7:8] * gate(0), turned[0:1] * gate(2)
                if base is None:
                    base, first, last = parts
                else:
                    base, first, last = base + parts[0], first + parts[1], last + parts[2]
            for i in range(3):
                cells = base
                if i == 0:
                    cells = jnp.concatenate([first, base[:7]], axis=0)
                elif i == 2:
                    cells = jnp.concatenate([base[1:], last], axis=0)
                lane = (9 * i + 3 * j + k) * LANES
                out_ref[row : row + 64, lane : lane + LANES] = cells.reshape(64, LANES).astype(BF16)


def forward_sum(win_ref, filt_ref):
    total = None
    for i in range(3):
        filt = filt_ref[TAPS * i : TAPS * (i + 1)].reshape(TAPS * LANES, LANES)
        term = jnp.dot(win_ref[64 * i : 64 * i + VOX, :], filt, preferred_element_type=F32)
        total = term if total is None else total + term
    return total


def backward_sum(win_ref, filt_ref):
    total = None
    for i in range(3):
        filt = jnp.concatenate([filt_ref[26 - TAPS * i - t] for t in range(TAPS)], axis=1)
        term = contract(win_ref[64 * i : 64 * i + VOX, :], filt, 1, 1)
        total = term if total is None else total + term
    return total


def filter_terms(win_ref, grad, small_ref, wide_ref, out_ref):
    pair = split_pair(small_ref[: SMALL // 2])
    out_ref[27] = jnp.concatenate([pair, jnp.zeros((LANES - SMALL, LANES), F32)], axis=0).astype(BF16)
    wide_ref[...] = jnp.zeros_like(wide_ref)
    for i in range(3):
        wide_ref[64 * i : 64 * i + VOX, LANES * i : LANES * (i + 1)] = grad
    for t in range(TAPS):
        term = contract(win_ref[:, LANES * t : LANES * (t + 1)], wide_ref[...], 0, 0)
        for i in range(3):
            out_ref[TAPS * i + t] = term[:, LANES * i : LANES * (i + 1)].astype(BF16)


def silu_parts(pre):
    sigmoid = 1.0 / (1.0 + jnp.exp(-pre))
    return pre * sigmoid, sigmoid * (1.0 + pre * (1.0 - sigmoid))


def first_kernel(parity, feat_hbm, occ_hbm, rule_hbm, masked, mask, rule_rows, send_a, send_b, feat, occ, rule, sems):
    copies = [
        pltpu.make_async_copy(feat_hbm, feat, sems.at[0]),
        pltpu.make_async_copy(occ_hbm, occ, sems.at[1]),
        pltpu.make_async_copy(rule_hbm, rule, sems.at[2]),
    ]
    for copy in copies:
        copy.start()
    for copy in copies:
        copy.wait()
    rows = lax.broadcasted_iota(jnp.int32, (SMALL, VOX), 0)
    occ_rows = jnp.where(rows == 0, jnp.broadcast_to(occ[...], (SMALL, VOX)), 0).astype(F32).astype(BF16)
    row = lax.broadcasted_iota(jnp.int32, (SMALL, LANES), 0)
    first = jnp.where(row == 0, 1.0, 0.0).astype(BF16)
    filled = contract(occ_rows, first, 0, 0)
    mask[...] = filled
    block = feat[...].astype(F32) * filled
    masked[...] = block.astype(BF16)
    offsets = lax.broadcasted_iota(jnp.int32, (32, LANES), 0)
    found = jnp.zeros((32, LANES), jnp.int32)
    for o in range(27):
        found = jnp.where(offsets == o, rule[0, o], found)
    found = found.astype(F32)
    rule_rows[...] = found
    layer, held = layers_of(block), layers_of(filled)
    top = EDGE - 1
    upward = jnp.concatenate([layer(top), layer(top - 1), layer(0), held(top), found], axis=0)
    downward = jnp.concatenate([layer(0), layer(1), layer(top), held(0), found], axis=0)
    put_sides(parity, upward, downward, send_a, send_b)


def labels_kernel(labels, filt_in, onehot, filt):
    filt[...] = filt_in[...]
    rows = lax.broadcasted_iota(jnp.int32, (SMALL, VOX), 0)
    hot_rows = jnp.where(rows == jnp.broadcast_to(labels[...], (SMALL, VOX)), 1.0, 0.0).astype(BF16)
    row = lax.broadcasted_iota(jnp.int32, (SMALL, LANES), 0)
    lane = lax.broadcasted_iota(jnp.int32, (SMALL, LANES), 1)
    unit = jnp.where(row == lane, 1.0, 0.0).astype(BF16)
    onehot[...] = contract(hot_rows, unit, 0, 0)


def one_kernel(rule, parity, masked, recv_a, recv_b, filt, mask, act, act_below, act_above, pre, win, rim):
    below, above = from_sides(parity, recv_a[...], recv_b[...])
    block = masked[...].astype(F32)
    build_windows(block, below[:64], above[:64], rule, win)
    total = forward_sum(win, filt) * mask[...]
    pre[...] = total
    acted, _ = silu_parts(total)
    act[...] = acted.astype(BF16)
    layer = layers_of(block)
    for side, mine, touching, row in ((below, layer(0), EDGE - 1, 0), (above, layer(EDGE - 1), 0, 64)):
        parts = [side[at : at + 64] for at in (0, 64, 128)]
        layer_windows(parts, mine, touching, side[256:288], rim, row)
    total = None
    wide = TAPS * LANES
    for i in range(3):
        weights = filt[TAPS * i : TAPS * (i + 1)].reshape(wide, LANES)
        term = jnp.dot(rim[:, wide * i : wide * (i + 1)], weights, preferred_element_type=F32)
        total = term if total is None else total + term
    for side, row, out in ((below, 0, act_below), (above, 64, act_above)):
        acted, _ = silu_parts(total[row : row + 64] * side[192:256])
        out[...] = acted.astype(BF16)


def two_kernel(
    classes, rule, parity, act_one, act_below, act_above, filt, mask, onehot, head,
    win, grad, small, send_a, send_b,
):
    build_windows(act_one[...].astype(F32), act_below[...].astype(F32), act_above[...].astype(F32), rule, win)
    filled = mask[...]
    pre = forward_sum(win, filt) * filled
    acted, slope = silu_parts(pre)
    acted = acted.astype(BF16)
    lane = lax.broadcasted_iota(jnp.int32, (VOX, LANES), 1)
    logits = contract(acted, head[...], 1, 1)
    known = lane < classes
    top = jnp.max(jnp.where(known, logits, -jnp.inf), axis=1, keepdims=True)
    powers = jnp.where(known, jnp.exp(jnp.where(known, logits - top, 0.0)), 0.0)
    total_log = top + jnp.log(jnp.sum(powers, axis=1, keepdims=True))
    hot = onehot[...]
    chances = jnp.where(known, jnp.exp(jnp.where(known, logits - total_log, 0.0)), 0.0)
    dlogits = (chances - hot) * filled
    high = dlogits.astype(BF16)
    low = (dlogits - high.astype(F32)).astype(BF16)
    back = jnp.dot(high, head[...], preferred_element_type=F32) + jnp.dot(low, head[...], preferred_element_type=F32)
    out = (back * slope * filled).astype(BF16)
    grad[...] = out
    put_layers(out.astype(F32), parity, send_a, send_b)
    head_rows = (contract(high, acted, 0, 0) + contract(low, acted, 0, 0))[:SMALL]
    losses = jnp.sum((total_log - logits) * hot * filled, axis=0, keepdims=True)
    counted = jnp.sum(filled, axis=0, keepdims=True)
    tail = jnp.where(lane[:1] < classes, losses, jnp.where(lane[:1] == classes, counted, 0.0))
    row = lax.broadcasted_iota(jnp.int32, (SMALL, LANES), 0)
    values = jnp.where(row < classes, head_rows, jnp.where(row == classes, tail, 0.0))
    small[...] = values


def terms_kernel(rule, parity, masked, recv_a, recv_b, win_two, grad, small, out, win_one, wide):
    filter_terms(win_two, grad[...], small, wide, out)
    below, above = from_sides(parity, recv_a[...], recv_b[...])
    build_windows(masked[...].astype(F32), below[:64], above[:64], rule, win_one)


def three_kernel(
    rule, parity, grad_two, recv_a, recv_b, filt, mask, pre, win_one, small,
    grad_one, terms, send_a, send_b, win, wide,
):
    below, above = from_sides(parity, recv_a[...], recv_b[...])
    build_windows(grad_two[...].astype(F32), below, above, rule, win)
    _, slope = silu_parts(pre[...])
    out = (backward_sum(win, filt) * slope * mask[...]).astype(BF16)
    grad_one[...] = out
    put_layers(out.astype(F32), parity, send_a, send_b)
    filter_terms(win_one, out, small, wide, terms)


def four_kernel(rule, parity, grad_one, recv_a, recv_b, filt, mask, out, token, win):
    below, above = from_sides(parity, recv_a[...], recv_b[...])
    build_windows(grad_one[...].astype(F32), below, above, rule, win)
    total = backward_sum(win, filt) * mask[...]
    out[...] = total.astype(BF16)
    token[...] = total[:SMALL]


def call(kernel, outs, specs, scratch=(), flops=0, params=PARAMS):
    return pl.pallas_call(
        kernel,
        out_shape=outs,
        in_specs=specs,
        out_specs=jax.tree.map(lambda _: VMEM, outs),
        scratch_shapes=list(scratch),
        compiler_params=params,
        cost_estimate=pl.CostEstimate(flops=flops, bytes_accessed=4_000_000, transcendentals=0),
    )


BLOCK = sds((VOX, LANES), BF16)
WIDE_BLOCK = sds((VOX, LANES), F32)
LAYER = sds((64, LANES), BF16)
FILTER = sds((27, LANES, LANES), BF16)
SIDE = sds((288, LANES), BF16)
WINDOWS = sds((640, TAPS * LANES), BF16)
TERMS = sds((28, LANES, LANES), BF16)
WIN_SCRATCH = pltpu.VMEM((640, TAPS * LANES), BF16)
SEM = pltpu.SemaphoreType.DMA
WIDE_SCRATCH = pltpu.VMEM((640, 3 * LANES), BF16)
CONV = 2 * 27 * VOX * LANES * LANES


def swap_a(value):
    length = lax.axis_size(SPACE)
    return lax.ppermute(value, SPACE, [(i, i ^ 1) for i in range(length)])


def swap_b(value):
    length = lax.axis_size(SPACE)
    return lax.ppermute(value, SPACE, [(i, (i + 1) % length if i % 2 else (i - 1) % length) for i in range(length)])


def far_swap(value):
    return lax.ppermute(value, "far", [(0, 1), (1, 0)])


def core_swap(value):
    return lax.ppermute(value, "core", [(0, 1), (1, 0)])


def split_pair(value):
    high = value.astype(BF16).astype(F32)
    return jnp.concatenate([high, value - high], axis=0)


def join_pair(pair):
    return pair[: SMALL // 2] + pair[SMALL // 2 : SMALL]


def pair_kernel(rows, peers, core, one, two, other, out):
    small = join_pair(one[27].astype(F32)) + join_pair(other[27].astype(F32))
    tail = jnp.concatenate([split_pair(small), jnp.zeros((SMALL, LANES), F32)], axis=0)
    mine = jnp.where(core[0] == 0, one[:27], two[:27])
    total = mine.reshape(27 * LANES, LANES).astype(F32) + other[:27].reshape(27 * LANES, LANES).astype(F32)
    spare = rows * peers - 27 * LANES
    if spare:
        total = jnp.concatenate([total, jnp.zeros((spare, LANES), F32)], axis=0)
    for p in range(peers):
        out[p] = jnp.concatenate([total[p * rows : (p + 1) * rows], tail], axis=0).astype(BF16)


def half_kernel(rows, peers, parts, later_a, later_b, out):
    total = parts[0].astype(F32)
    for p in range(1, peers):
        total = total + parts[p].astype(F32)
    tail = split_pair(join_pair(total[rows : rows + SMALL]))
    out[...] = jnp.concatenate([total[:rows], tail, jnp.zeros((SMALL, LANES), F32)], axis=0).astype(BF16)


def copies_kernel(rows, peers, classes, mine, other, later, out, head, loss):
    a, b = mine[...].astype(F32), other[...].astype(F32)
    both = (a[:rows] + b[:rows]).astype(BF16)
    for p in range(peers):
        out[p] = both
    tail = join_pair(a[rows:]) + join_pair(b[rows:])
    head[...] = tail[:classes] * (1.0 / VOX)
    last = tail[classes : classes + 1]
    lane = lax.broadcasted_iota(jnp.int32, (1, LANES), 1)
    losses = jnp.sum(jnp.where(lane < classes, last, 0.0), axis=1, keepdims=True)
    counted = jnp.sum(jnp.where(lane == classes, last, 0.0), axis=1, keepdims=True)
    loss[...] = jnp.broadcast_to(losses / counted, (1, LANES))


def local(classes, features, occupancy, labels, rulebook, filter_one, filter_two, head_weight):
    parity = (lax.axis_index(SPACE) % 2).reshape(1).astype(jnp.int32)
    core = lax.axis_index("core").reshape(1).astype(jnp.int32)
    head = jnp.zeros((LANES, LANES), BF16).at[:classes].set(head_weight.T)
    masked, mask, rule, a, b = call(
        first_kernel,
        (BLOCK, WIDE_BLOCK, sds((32, LANES), F32), SIDE, SIDE),
        [SMEM, ANY, ANY, ANY],
        [pltpu.VMEM((VOX, LANES), BF16), pltpu.VMEM((1, VOX), jnp.int32), pltpu.SMEM((1, 27), jnp.int32), SEM((3,))],
    )(parity, features.reshape(VOX, LANES), occupancy.reshape(1, VOX), rulebook.reshape(1, 27))
    a, b = swap_a(a), swap_b(b)
    onehot, filter_here = call(labels_kernel, (WIDE_BLOCK, FILTER), [VMEM] * 2)(labels.reshape(1, VOX), filter_one)
    act_one, act_below, act_above, pre_one = call(
        one_kernel,
        (BLOCK, LAYER, LAYER, WIDE_BLOCK),
        [VMEM, SMEM] + [VMEM] * 5,
        [WIN_SCRATCH, pltpu.VMEM((128, 27 * LANES), BF16)],
        CONV,
    )(rule, parity, masked, a, b, filter_here, mask)
    win_two, grad_two, small, e, f = call(
        functools.partial(two_kernel, classes),
        (WINDOWS, BLOCK, sds((SMALL, LANES), F32), LAYER, LAYER),
        [VMEM, SMEM] + [VMEM] * 7,
        flops=CONV,
    )(rule, parity, act_one, act_below, act_above, filter_two, mask, onehot, head)
    e, f = swap_a(e), swap_b(f)
    terms_two, win_one = call(terms_kernel, (TERMS, WINDOWS), [VMEM, SMEM] + [VMEM] * 6, [WIDE_SCRATCH], CONV)(
        rule, parity, masked, a, b, win_two, grad_two, small
    )
    grad_one, terms_one, g, h = call(
        three_kernel,
        (BLOCK, TERMS, LAYER, LAYER),
        [VMEM, SMEM] + [VMEM] * 8,
        [WIN_SCRATCH, WIDE_SCRATCH],
        2 * CONV,
    )(rule, parity, grad_two, e, f, filter_two, mask, pre_one, win_one, small)
    g, h = swap_a(g), swap_b(h)
    grad_in, token = call(
        four_kernel, (BLOCK, sds((SMALL, LANES), F32)), [VMEM, SMEM] + [VMEM] * 5, [WIN_SCRATCH], CONV
    )(rule, parity, grad_one, g, h, filter_one, mask)
    peers = lax.axis_size("near") * lax.axis_size("x")
    rows = -(-27 * LANES // (peers * 16)) * 16
    away = jnp.where(core[0] == 0, terms_two, terms_one)
    chunks = call(
        functools.partial(pair_kernel, rows, peers),
        sds((peers, rows + 2 * SMALL, LANES), BF16),
        [SMEM] + [VMEM] * 3,
    )(core, terms_one, terms_two, core_swap(away))
    parts = lax.all_to_all(chunks, ("near", "x"), 0, 0, tiled=True)
    part = call(
        functools.partial(half_kernel, rows, peers), sds((rows + 2 * SMALL, LANES), BF16), [VMEM, ANY, ANY]
    )(parts, g, h)
    copies, head_sum, loss = call(
        functools.partial(copies_kernel, rows, peers, classes),
        (sds((peers, rows, LANES), BF16), sds((classes, LANES), F32), sds((1, LANES), F32)),
        [VMEM, VMEM, ANY],
    )(part, far_swap(part), token)
    whole = lax.all_to_all(copies, ("near", "x"), 0, 0, tiled=True)
    whole = whole.reshape(peers * rows, LANES)[: 27 * LANES].reshape(27, LANES, LANES)
    whole_other = core_swap(whole)
    scale = 1.0 / VOX
    return (
        jnp.where(core[0] == 0, whole, whole_other).astype(F32) * scale,
        jnp.where(core[0] == 0, whole_other, whole).astype(F32) * scale,
        head_sum.T,
        loss[0, 0],
        grad_in.reshape(features.shape),
    )


def solution(mesh):
    shape = mesh.devices.shape
    inner = Mesh(mesh.devices.reshape(2, shape[0] // 2, shape[1] // 2, 2), ("far", "near", "x", "core"))
    parts = ("x", "core")
    placed = (
        P(parts, SPACE, None, None),
        P(parts, SPACE, None),
        P(parts, SPACE, None),
        P(parts, SPACE, None),
        P(),
        P(),
        P(),
    )

    def whole(features, occupancy, labels, rulebook, filter_one, filter_two, head_weight):
        step = jax.shard_map(
            functools.partial(local, head_weight.shape[1]),
            mesh=inner,
            in_specs=placed,
            out_specs=(P(), P(), P(), P(), P(parts, SPACE, None, None)),
            check_vma=False,
        )
        return step(features, occupancy, labels, rulebook, filter_one, filter_two, head_weight)

    return whole
```

time: 93.1 us -> 79.8 us (0.86)
  starting transfers between devices: 28.9 us -> 21.6 us
  between operations: 3.29 us -> 0.78 us
  local copies, waits for them, and re-layouts: 6.7 us -> 4.77 us
  waiting for transfers between devices: 22.9 us -> 21.3 us
  other arithmetic: 3.59 us -> 2.37 us
    ppermute x8 -> x6, waiting for transfers between devices: 15 us -> 10.7 us  [the longest x3 10.4 us: swap_b(): lax.ppermute(value, SPACE, [(i, (i + 1) % length if i % 2 else (i - 1) %...]
    ppermute x3 -> x2, starting transfers between devices: 8.43 us -> 4.64 us  [core_swap(): return lax.ppermute(value, 'core', [(0, 1), (1, 0)])]
    ppermute x8 -> x6, starting transfers between devices: 16.6 us -> 13.2 us  [the longest x3 9.62 us: swap_b(): lax.ppermute(value, SPACE, [(i, (i + 1) % length if i % 2 else (i - 1) %...]
    ppermute x3 -> x2, waiting for transfers between devices: 1.95 us -> 4.15 us  [core_swap(): return lax.ppermute(value, 'core', [(0, 1), (1, 0)])]
    unnamed x24 -> x14, local copies, waits for them, and re-layouts: 6.11 us -> 4.09 us
    mul x2 -> x1, other arithmetic: 2.85 us -> 2.27 us  [local(): jnp.where(core[0] == 0, whole_other, whole).astype(F32) * scale]
    ppermute x2 -> x1, waiting for transfers between devices: 6.02 us -> 6.51 us  [far_swap(): return lax.ppermute(value, 'far', [(0, 1), (1, 0)])]
  transfers between devices with their start and end apart: 14 -> 10, of which waited for: 8 -> 6; matrix products, arithmetic and copies ran while one was open for 2% -> 1% of each run, Pallas kernels for 4% -> 4%
where the time goes in v3:
time: 79.8 us; the launch traced here: 79.1 us
  starting transfers between devices  21.6 us (27%)
  waiting for transfers between devices  21.3 us (27%)
  blocking collectives  15.4 us (19%)
  Pallas kernels  12.9 us (16%)
  local copies, waits for them, and re-layouts  4.77 us (6%)
  other arithmetic  2.37 us (3%)
    all_to_all x1, blocking collectives, local(): whole = lax.all_to_all(copies, ('near', 'x'), 0, 0, tiled=True)  15.4 us
    ppermute x3, waiting for transfers between devices, swap_b(): lax.ppermute(value, SPACE, [(i, (i + 1) % length if i % 2 else (i - 1) %...  10.4 us
    ppermute x3, starting transfers between devices, swap_b(): lax.ppermute(value, SPACE, [(i, (i + 1) % length if i % 2 else (i - 1) %...  9.62 us
    ppermute x1, waiting for transfers between devices, far_swap(): return lax.ppermute(value, 'far', [(0, 1), (1, 0)])  6.51 us
    ppermute x2, starting transfers between devices, core_swap(): return lax.ppermute(value, 'core', [(0, 1), (1, 0)])  4.64 us
    ppermute x2, waiting for transfers between devices, core_swap(): return lax.ppermute(value, 'core', [(0, 1), (1, 0)])  4.15 us
    unnamed x14, local copies, waits for them, and re-layouts  4.09 us
    all_to_all x1, starting transfers between devices, local(): parts = lax.all_to_all(chunks, ('near', 'x'), 0, 0, tiled=True)  3.68 us
  transfers between devices with their start and end apart: 10, of which 6 were waited for; matrix products, arithmetic and copies ran while one was open for 1% of the time, Pallas kernels for 4%

profile of v3, /device:TPU:1, one launch (start us, length us, event | category | flops | bytes accessed | tf_op | source)
XLA Modules:
  0.0 79.1 jit_solution(503251977591752413)
XLA Ops:
  0.6 0.0 copy-start.2
  0.7 0.9 %copy-done.2 = bf16[1,1,512,128]{3,2,1,0:T(8,128)(2,1)S(1)} copy-done((bf16[1,1,512,128]{3,2,1,0:T(8,128)(2,1)S(1)}, bf16[1,1,512,128]{3,2,1,0:T(8,128)(2,1)}, u32[]{:S(2)}) %copy-start.2) | copy-done | bytes 131096
  1.6 0.0 copy-start.3
  1.6 0.7 copy-done.3
  2.2 0.0 copy-start.5
  2.2 0.7 copy-done.5
  2.9 1.0 %shard_map.110 = (bf16[512,128]{1,0:T(8,128)(2,1)S(1)}, f32[512,128]{1,0:T(8,128)S(1)}, f32[32,128]{1,0:T(8,128)S(1)}, bf16[288,128]{1,0:T(8,128)(2,1)S(1)}, bf16[288,128]{1,0:T(8,128)(2,1)S(1)}) custom-call(s32[1]{0:T(128)} %bitcast.1.parity, bf16[512,128]{1,0:T(8,128)(2,1)S(1)} %bitcast.12, s32[1,512]{1,0:T(1,128)S(1)} %bitcast.13, s32[1,27]{1,0:T(1,128)S(1)} %bitcast.15), custom_call_target="tpu_custom_call" | custom-call | bytes 4000000 | tf_op jit(solution)/shard_map/pallas_call | solution.py:389
  3.9 2.1 %collective-permute-start = (bf16[288,128]{1,0:T(8,128)(2,1)S(1)}, bf16[288,128]{1,0:T(8,128)(2,1)S(1)}, u32[]{:S(2)}, u32[]{:S(2)}) collective-permute-start(bf16[288,128]{1,0:T(8,128)(2,1)S(1)} %get-tuple-element.46), channel_id=1, source_target_pairs={{0,4},{4,0},{8,12},{12,8},{16,20},{20,16},{24,28},{28,24},{1,5},{5... | collective-permute-start | bytes 221192 | tf_op jit(solution)/shard_map/ppermute | solution.py:326
  6.0 3.3 %collective-permute-start.1 = (bf16[288,128]{1,0:T(8,128)(2,1)S(1)}, bf16[288,128]{1,0:T(8,128)(2,1)S(1)}, u32[]{:S(2)}, u32[]{:S(2)}) collective-permute-start(bf16[288,128]{1,0:T(8,128)(2,1)S(1)} %get-tuple-element.47), channel_id=1, source_target_pairs={{0,28},{4,8},{8,4},{12,16},{16,12},{20,24},{24,20},{28,0},{1,29},{... | collective-permute-start | bytes 221192 | tf_op jit(solution)/shard_map/ppermute | solution.py:331
  9.3 0.7 scatter.4.head
  10.0 0.0 copy-start
  10.0 1.2 %copy-done = bf16[27,128,128]{2,1,0:T(8,128)(2,1)S(1)} copy-done((bf16[27,128,128]{2,1,0:T(8,128)(2,1)S(1)}, bf16[27,128,128]{2,1,0:T(8,128)(2,1)}, u32[]{:S(2)}) %copy-start) | copy-done | bytes 884760
  11.1 0.0 copy-start.4
  11.1 0.7 copy-done.4
  11.8 0.0 copy-start.6
  11.8 0.2 shard_map.111
  12.1 0.0 collective-permute-done.recv_a
  12.1 0.0 collective-permute-done.1.recv_b
  12.1 1.6 %shard_map.112 = (bf16[512,128]{1,0:T(8,128)(2,1)S(1)}, bf16[64,128]{1,0:T(8,128)(2,1)S(1)}, bf16[64,128]{1,0:T(8,128)(2,1)S(1)}, f32[512,128]{1,0:T(8,128)S(1)}) custom-call(f32[32,128]{1,0:T(8,128)S(1)} %get-tuple-element.44.rule, s32[1]{0:T(128)} %bitcast.1.parity, bf16[512,128]{1,0:T(8,128)(2,1)S(1)} %get-tuple-element.45.masked, ...), custom_call_target="tpu_custom_call" | custom-call | flops 452984832 | bytes 4000000 | tf_op jit(solution)/shard_map/pallas_call | solution.py:397
  13.7 0.0 copy-done.6
  13.7 2.0 %shard_map.113 = (bf16[640,1152]{1,0:T(8,128)(2,1)S(1)}, bf16[512,128]{1,0:T(8,128)(2,1)S(1)}, f32[8,128]{1,0:T(8,128)S(1)}, bf16[64,128]{1,0:T(8,128)(2,1)S(1)}, bf16[64,128]{1,0:T(8,128)(2,1)S(1)}) custom-call(f32[32,128]{1,0:T(8,128)S(1)} %get-tuple-element.44.rule, s32[1]{0:T(128)} %bitcast.1.parity, bf16[512,128]{1,0:T(8,128)(2,1)S(1)} %get-tuple-element.50.act_one, ...), custom_call_target="tpu_custom_call" | custom-call | flops 452984832 | bytes 4000000 | tf_op jit(solution)/shard_map/pallas_call | solution.py:404
  15.7 0.1 collective-permute-start.2
  15.8 3.2 %collective-permute-start.3 = (bf16[64,128]{1,0:T(8,128)(2,1)S(1)}, bf16[64,128]{1,0:T(8,128)(2,1)S(1)}, u32[]{:S(2)}, u32[]{:S(2)}) collective-permute-start(bf16[64,128]{1,0:T(8,128)(2,1)S(1)} %get-tuple-element.56), channel_id=1, source_target_pairs={{0,28},{4,8},{8,4},{12,16},{16,12},{20,24},{24,20},{28,0},{1,29},{... | collective-permute-start | bytes 49160 | tf_op jit(solution)/shard_map/ppermute | solution.py:331
  18.9 1.5 %shard_map.114 = (bf16[28,128,128]{2,1,0:T(8,128)(2,1)S(1)}, bf16[640,1152]{1,0:T(8,128)(2,1)S(1)}) custom-call(f32[32,128]{1,0:T(8,128)S(1)} %get-tuple-element.44.rule, s32[1]{0:T(128)} %bitcast.1.parity, bf16[512,128]{1,0:T(8,128)(2,1)S(1)} %get-tuple-element.45.masked, bf16[288,128]{1,0:T(8,128)(2,1)S(1)} %collective-permute-done.recv_a, ...), custom_call_target="tpu_custom_call" | custom-call | flops 452984832 | bytes 4000000 | tf_op jit(solution)/shard_map/pallas_call | solution.py:411
  20.5 0.0 collective-permute-done.2.recv_a
  20.5 0.6 collective-permute-done.3.recv_b
  21.1 2.8 %shard_map.115 = (bf16[512,128]{1,0:T(8,128)(2,1)S(1)}, bf16[28,128,128]{2,1,0:T(8,128)(2,1)S(1)}, bf16[64,128]{1,0:T(8,128)(2,1)S(1)}, bf16[64,128]{1,0:T(8,128)(2,1)S(1)}) custom-call(f32[32,128]{1,0:T(8,128)S(1)} %get-tuple-element.44.rule, s32[1]{0:T(128)} %bitcast.1.parity, bf16[512,128]{1,0:T(8,128)(2,1)S(1)} %get-tuple-element.54.grad.grad_two, ...), custom_call_target="tpu_custom_call" | custom-call | flops 905969664 | bytes 4000000 | tf_op jit(solution)/shard_map/pallas_call | solution.py:414
  23.9 0.1 broadcast_select_fusion
  24.1 3.2 %collective-permute-start.4 = (bf16[28,128,128]{2,1,0:T(8,128)(2,1)S(1)}, bf16[28,128,128]{2,1,0:T(8,128)(2,1)S(1)}, u32[]{:S(2)}, u32[]{:S(2)}) collective-permute-start(bf16[28,128,128]{2,1,0:T(8,128)(2,1)S(1)} %broadcast_select_fusion), channel_id=1, source_target_pairs={{0,1},{1,0},{2,3},{3,2},{4,5},{5,4},{6,7},{7,6},{8,9},{9,8},{10,11... | collective-permute-start | bytes 2752520 | tf_op jit(solution)/shard_map/ppermute | solution.py:339
  27.2 2.1 %collective-permute-done.4.other = bf16[28,128,128]{2,1,0:T(8,128)(2,1)S(1)} collective-permute-done((bf16[28,128,128]{2,1,0:T(8,128)(2,1)S(1)}, bf16[28,128,128]{2,1,0:T(8,128)(2,1)S(1)}, u32[]{:S(2)}, u32[]{:S(2)}) %collective-permute-start.4) | collective-permute-done | bytes 917536 | tf_op jit(solution)/shard_map/ppermute | solution.py:339
  29.3 1.2 %shard_map.116 = bf16[8,448,128]{2,1,0:T(8,128)(2,1)} custom-call(s32[1]{0:T(128)} %bitcast.core, bf16[28,128,128]{2,1,0:T(8,128)(2,1)S(1)} %get-tuple-element.61.one, bf16[28,128,128]{2,1,0:T(8,128)(2,1)S(1)} %get-tuple-element.62.two, bf16[28,128,128]{2,1,0:T(8,128)(2,1)S(1)} %collective-permute-done.4.other), custom_call_target="tpu_custom_call" | custom-call | bytes 4000000 | tf_op jit(solution)/shard_map/pallas_call | solution.py:428
  30.5 0.0 copy-start.1
  30.5 3.7 %all-to-all-start = ((bf16[8,448,128]{2,1,0:T(8,128)(2,1)}), bf16[8,448,128]{2,1,0:T(8,128)(2,1)S(1)}, u32[]{:S(2)}, u32[]{:S(2)}) async-start(bf16[8,448,128]{2,1,0:T(8,128)(2,1)} %shard_map.116), calls=%async_computation | async-start | bytes 1835008 | tf_op jit(solution)/shard_map/all_to_all | solution.py:433
  34.2 1.4 %collective-permute-start.5 = (bf16[64,128]{1,0:T(8,128)(2,1)S(1)}, bf16[64,128]{1,0:T(8,128)(2,1)S(1)}, u32[]{:S(2)}, u32[]{:S(2)}) collective-permute-start(bf16[64,128]{1,0:T(8,128)(2,1)S(1)} %get-tuple-element.63), channel_id=1, source_target_pairs={{0,4},{4,0},{8,12},{12,8},{16,20},{20,16},{24,28},{28,24},{1,5},{5... | collective-permute-start | bytes 49160 | tf_op jit(solution)/shard_map/ppermute | solution.py:326
  35.6 3.2 %collective-permute-start.6 = (bf16[64,128]{1,0:T(8,128)(2,1)S(1)}, bf16[64,128]{1,0:T(8,128)(2,1)S(1)}, u32[]{:S(2)}, u32[]{:S(2)}) collective-permute-start(bf16[64,128]{1,0:T(8,128)(2,1)S(1)} %get-tuple-element.64), channel_id=1, source_target_pairs={{0,28},{4,8},{8,4},{12,16},{16,12},{20,24},{24,20},{28,0},{1,29},{... | collective-permute-start | bytes 49160 | tf_op jit(solution)/shard_map/ppermute | solution.py:331
  38.8 0.3 collective-permute-done.5.later_a.recv_a
  39.0 9.8 %collective-permute-done.6.later_b.recv_b = bf16[64,128]{1,0:T(8,128)(2,1)S(1)} collective-permute-done((bf16[64,128]{1,0:T(8,128)(2,1)S(1)}, bf16[64,128]{1,0:T(8,128)(2,1)S(1)}, u32[]{:S(2)}, u32[]{:S(2)}) %collective-permute-start.6) | collective-permute-done | bytes 16416 | tf_op jit(solution)/shard_map/ppermute | solution.py:331
  48.8 0.0 all-to-all-done.parts
  48.8 0.1 shard_map.117.mine
  48.9 0.1 collective-permute-start.7
  49.0 0.0 copy-done.1
  49.0 1.8 %shard_map.118 = (bf16[512,128]{1,0:T(8,128)(2,1)}, f32[8,128]{1,0:T(8,128)S(1)}) custom-call(f32[32,128]{1,0:T(8,128)S(1)} %get-tuple-element.44.rule, s32[1]{0:T(128)} %bitcast.1.parity, bf16[512,128]{1,0:T(8,128)(2,1)S(1)} %get-tuple-element.65.grad_one, bf16[64,128]{1,0:T(8,128)(2,1)S(1)} %collective-permute-done.5.later_a.recv_a, ...), custom_call_target="tpu_custom_call" | custom-call | flops 452984832 | bytes 4000000 | tf_op jit(solution)/shard_map/pallas_call | solution.py:422
  50.8 6.5 %collective-permute-done.7.other = bf16[448,128]{1,0:T(8,128)(2,1)S(1)} collective-permute-done((bf16[448,128]{1,0:T(8,128)(2,1)S(1)}, bf16[448,128]{1,0:T(8,128)(2,1)S(1)}, u32[]{:S(2)}, u32[]{:S(2)}) %collective-permute-start.7) | collective-permute-done | bytes 114720 | tf_op jit(solution)/shard_map/ppermute | solution.py:335
  57.3 0.6 shard_map.119
  57.9 15.4 %all_to_all.10 = bf16[8,432,128]{2,1,0:T(8,128)(2,1)S(1)} all-to-all(bf16[8,432,128]{2,1,0:T(8,128)(2,1)S(1)} %get-tuple-element.67), channel_id=1, replica_groups=mesh['far'=2,'near'=4,'x'=2,'core'=2] {'near','x'}, dimensions={0} | all-to-all | bytes 1769472 | tf_op jit(solution)/shard_map/all_to_all | solution.py:442
  73.3 1.5 %collective-permute-start.8 = (bf16[27,128,128]{2,1,0:T(8,128)(2,1)S(1)}, bf16[27,128,128]{2,1,0:T(8,128)(2,1)S(1)}, u32[]{:S(2)}, u32[]{:S(2)}) collective-permute-start(bf16[27,128,128]{2,1,0:T(8,128)(2,1)S(1)} %bitcast.16), channel_id=1, source_target_pairs={{0,1},{1,0},{2,3},{3,2},{4,5},{5,4},{6,7},{7,6},{8,9},{9,8},{10,11... | collective-permute-start | bytes 2654216 | tf_op jit(solution)/shard_map/ppermute | solution.py:339
  74.8 2.1 %collective-permute-done.8 = bf16[27,128,128]{2,1,0:T(8,128)(2,1)S(1)} collective-permute-done((bf16[27,128,128]{2,1,0:T(8,128)(2,1)S(1)}, bf16[27,128,128]{2,1,0:T(8,128)(2,1)S(1)}, u32[]{:S(2)}, u32[]{:S(2)}) %collective-permute-start.8) | collective-permute-done | bytes 884768 | tf_op jit(solution)/shard_map/ppermute | solution.py:339
  76.8 2.3 %convert_multiply_fusion = (f32[27,128,128]{2,1,0:T(8,128)}, f32[27,128,128]{2,1,0:T(8,128)}) fusion(bf16[27,128,128]{2,1,0:T(8,128)(2,1)S(1)} %collective-permute-done.8, bf16[27,128,128]{2,1,0:T(8,128)(2,1)S(1)} %bitcast.17, pred[]{:T(512)S(6)} %eq.4), kind=kLoop, calls=%fused_computation | loop fusion | flops 2654208 | bytes 5308417 | tf_op jit(solution)/shard_map/mul | solution.py:448
Async XLA Ops:
  0.6 0.9 %copy-start.2 = (bf16[1,1,512,128]{3,2,1,0:T(8,128)(2,1)S(1)}, bf16[1,1,512,128]{3,2,1,0:T(8,128)(2,1)}, u32[]{:S(2)}) copy-start(bf16[1,1,512,128]{3,2,1,0:T(8,128)(2,1)} %param.9) | copy-start | bytes 393220
  1.6 0.7 copy-start.3
  2.2 0.7 copy-start.5
  3.9 8.2 %collective-permute-start = (bf16[288,128]{1,0:T(8,128)(2,1)S(1)}, bf16[288,128]{1,0:T(8,128)(2,1)S(1)}, u32[]{:S(2)}, u32[]{:S(2)}) collective-permute-start(bf16[288,128]{1,0:T(8,128)(2,1)S(1)} %get-tuple-element.46), channel_id=1, source_target_pairs={{0,4},{4,0},{8,12},{12,8},{16,20},{20,16},{24,28},{28,24},{1,5},{5... | collective-permute-start | bytes 221192 | tf_op jit(solution)/shard_map/ppermute | solution.py:326
  6.0 6.0 %collective-permute-start.1 = (bf16[288,128]{1,0:T(8,128)(2,1)S(1)}, bf16[288,128]{1,0:T(8,128)(2,1)S(1)}, u32[]{:S(2)}, u32[]{:S(2)}) collective-permute-start(bf16[288,128]{1,0:T(8,128)(2,1)S(1)} %get-tuple-element.47), channel_id=1, source_target_pairs={{0,28},{4,8},{8,4},{12,16},{16,12},{20,24},{24,20},{28,0},{1,29},{... | collective-permute-start | bytes 221192 | tf_op jit(solution)/shard_map/ppermute | solution.py:331
  10.0 1.2 %copy-start = (bf16[27,128,128]{2,1,0:T(8,128)(2,1)S(1)}, bf16[27,128,128]{2,1,0:T(8,128)(2,1)}, u32[]{:S(2)}) copy-start(bf16[27,128,128]{2,1,0:T(8,128)(2,1)} %filt.5) | copy-start | bytes 2654212
  11.1 0.7 copy-start.4
  11.8 1.8 %copy-start.6 = (bf16[27,128,128]{2,1,0:T(8,128)(2,1)S(1)}, bf16[27,128,128]{2,1,0:T(8,128)(2,1)}, u32[]{:S(2)}) copy-start(bf16[27,128,128]{2,1,0:T(8,128)(2,1)} %filt.4) | copy-start | bytes 2654212
  15.7 4.8 %collective-permute-start.2 = (bf16[64,128]{1,0:T(8,128)(2,1)S(1)}, bf16[64,128]{1,0:T(8,128)(2,1)S(1)}, u32[]{:S(2)}, u32[]{:S(2)}) collective-permute-start(bf16[64,128]{1,0:T(8,128)(2,1)S(1)} %get-tuple-element.55), channel_id=1, source_target_pairs={{0,4},{4,0},{8,12},{12,8},{16,20},{20,16},{24,28},{28,24},{1,5},{5... | collective-permute-start | bytes 49160 | tf_op jit(solution)/shard_map/ppermute | solution.py:326
  15.8 5.4 %collective-permute-start.3 = (bf16[64,128]{1,0:T(8,128)(2,1)S(1)}, bf16[64,128]{1,0:T(8,128)(2,1)S(1)}, u32[]{:S(2)}, u32[]{:S(2)}) collective-permute-start(bf16[64,128]{1,0:T(8,128)(2,1)S(1)} %get-tuple-element.56), channel_id=1, source_target_pairs={{0,28},{4,8},{8,4},{12,16},{16,12},{20,24},{24,20},{28,0},{1,29},{... | collective-permute-start | bytes 49160 | tf_op jit(solution)/shard_map/ppermute | solution.py:331
  24.1 5.3 %collective-permute-start.4 = (bf16[28,128,128]{2,1,0:T(8,128)(2,1)S(1)}, bf16[28,128,128]{2,1,0:T(8,128)(2,1)S(1)}, u32[]{:S(2)}, u32[]{:S(2)}) collective-permute-start(bf16[28,128,128]{2,1,0:T(8,128)(2,1)S(1)} %broadcast_select_fusion), channel_id=1, source_target_pairs={{0,1},{1,0},{2,3},{3,2},{4,5},{5,4},{6,7},{7,6},{8,9},{9,8},{10,11... | collective-permute-start | bytes 2752520 | tf_op jit(solution)/shard_map/ppermute | solution.py:339
  30.5 18.5 %copy-start.1 = (bf16[27,128,128]{2,1,0:T(8,128)(2,1)S(1)}, bf16[27,128,128]{2,1,0:T(8,128)(2,1)}, u32[]{:S(2)}) copy-start(bf16[27,128,128]{2,1,0:T(8,128)(2,1)} %filt.5) | copy-start | bytes 2654212
  30.5 18.3 %all-to-all-start = ((bf16[8,448,128]{2,1,0:T(8,128)(2,1)}), bf16[8,448,128]{2,1,0:T(8,128)(2,1)S(1)}, u32[]{:S(2)}, u32[]{:S(2)}) async-start(bf16[8,448,128]{2,1,0:T(8,128)(2,1)} %shard_map.116), calls=%async_computation | async-start | bytes 1835008 | tf_op jit(solution)/shard_map/all_to_all | solution.py:433
  34.2 4.8 %collective-permute-start.5 = (bf16[64,128]{1,0:T(8,128)(2,1)S(1)}, bf16[64,128]{1,0:T(8,128)(2,1)S(1)}, u32[]{:S(2)}, u32[]{:S(2)}) collective-permute-start(bf16[64,128]{1,0:T(8,128)(2,1)S(1)} %get-tuple-element.63), channel_id=1, source_target_pairs={{0,4},{4,0},{8,12},{12,8},{16,20},{20,16},{24,28},{28,24},{1,5},{5... | collective-permute-start | bytes 49160 | tf_op jit(solution)/shard_map/ppermute | solution.py:326
  35.6 13.2 %collective-permute-start.6 = (bf16[64,128]{1,0:T(8,128)(2,1)S(1)}, bf16[64,128]{1,0:T(8,128)(2,1)S(1)}, u32[]{:S(2)}, u32[]{:S(2)}) collective-permute-start(bf16[64,128]{1,0:T(8,128)(2,1)S(1)} %get-tuple-element.64), channel_id=1, source_target_pairs={{0,28},{4,8},{8,4},{12,16},{16,12},{20,24},{24,20},{28,0},{1,29},{... | collective-permute-start | bytes 49160 | tf_op jit(solution)/shard_map/ppermute | solution.py:331
  48.9 8.4 %collective-permute-start.7 = (bf16[448,128]{1,0:T(8,128)(2,1)S(1)}, bf16[448,128]{1,0:T(8,128)(2,1)S(1)}, u32[]{:S(2)}, u32[]{:S(2)}) collective-permute-start(bf16[448,128]{1,0:T(8,128)(2,1)S(1)} %shard_map.117.mine), channel_id=1, source_target_pairs={{0,16},{16,0},{1,17},{17,1},{2,18},{18,2},{3,19},{19,3},{4,20},{20... | collective-permute-start | bytes 344072 | tf_op jit(solution)/shard_map/ppermute | solution.py:335
  73.3 3.5 %collective-permute-start.8 = (bf16[27,128,128]{2,1,0:T(8,128)(2,1)S(1)}, bf16[27,128,128]{2,1,0:T(8,128)(2,1)S(1)}, u32[]{:S(2)}, u32[]{:S(2)}) collective-permute-start(bf16[27,128,128]{2,1,0:T(8,128)(2,1)S(1)} %bitcast.16), channel_id=1, source_target_pairs={{0,1},{1,0},{2,3},{3,2},{4,5},{5,4},{6,7},{7,6},{8,9},{9,8},{10,11... | collective-permute-start | bytes 2654216 | tf_op jit(solution)/shard_map/ppermute | solution.py:339

commit v4 on v3

--- a/solution.py
+++ b/solution.py
@@ -16,6 +16,7 @@
 F32 = jnp.float32
 BF16 = jnp.bfloat16
 PARAMS = pltpu.CompilerParams(vmem_limit_bytes=16 * 1024 * 1024)
+ROOMY = pltpu.CompilerParams(vmem_limit_bytes=62 * 1024 * 1024)
 VMEM = pl.BlockSpec(memory_space=pltpu.VMEM)
 ANY = pl.BlockSpec(memory_space=pl.ANY)
 SMEM = pl.BlockSpec(memory_space=pltpu.SMEM)
@@ -33,10 +34,8 @@
     return jnp.broadcast_to(layer.astype(F32).reshape(64, 1, LANES), (64, EDGE, LANES))
 
 
-def from_sides(parity_ref, recv_a, recv_b):
-    even = parity_ref[0] == 0
-    got_a, got_b = recv_a.astype(F32), recv_b.astype(F32)
-    return jnp.where(even, got_b, got_a), jnp.where(even, got_a, got_b)
+def from_sides(recv_a, recv_b):
+    return recv_a.astype(F32), recv_b.astype(F32)
 
 
 def build_windows(block, below, above, rule_ref, out_ref):
@@ -81,10 +80,9 @@
             out_ref[:, lane : lane + LANES] = padded.reshape(640, LANES).astype(BF16)
 
 
-def put_sides(parity_ref, upward, downward, send_a_ref, send_b_ref):
-    even = parity_ref[0] == 0
-    send_a_ref[...] = jnp.where(even, upward, downward).astype(BF16)
-    send_b_ref[...] = jnp.where(even, downward, upward).astype(BF16)
+def put_sides(upward, downward, send_a_ref, send_b_ref):
+    send_a_ref[...] = upward.astype(BF16)
+    send_b_ref[...] = downward.astype(BF16)
 
 
 def layers_of(block):
@@ -92,9 +90,9 @@
     return lambda z: cells[:, z, :]
 
 
-def put_layers(block, parity_ref, send_a_ref, send_b_ref):
+def put_layers(block, send_a_ref, send_b_ref):
     layer = layers_of(block)
-    put_sides(parity_ref, layer(EDGE - 1), layer(0), send_a_ref, send_b_ref)
+    put_sides(layer(EDGE - 1), layer(0), send_a_ref, send_b_ref)
 
 
 def layer_windows(side, mine, touching, rule, out_ref, row):
@@ -172,7 +170,14 @@
     return pre * sigmoid, sigmoid * (1.0 + pre * (1.0 - sigmoid))
 
 
-def first_kernel(parity, feat_hbm, occ_hbm, rule_hbm, masked, mask, rule_rows, send_a, send_b, feat, occ, rule, sems):
+def filled_rows(occ):
+    rows = lax.broadcasted_iota(jnp.int32, (SMALL, VOX), 0)
+    occ_rows = jnp.where(rows == 0, jnp.broadcast_to(occ, (SMALL, VOX)), 0).astype(F32).astype(BF16)
+    row = lax.broadcasted_iota(jnp.int32, (SMALL, LANES), 0)
+    return contract(occ_rows, jnp.where(row == 0, 1.0, 0.0).astype(BF16), 0, 0)
+
+
+def first_kernel(feat_hbm, occ_hbm, rule_hbm, send_a, send_b, feat, occ, rule, sems):
     copies = [
         pltpu.make_async_copy(feat_hbm, feat, sems.at[0]),
         pltpu.make_async_copy(occ_hbm, occ, sems.at[1]),
@@ -182,39 +187,33 @@
         copy.start()
     for copy in copies:
         copy.wait()
-    rows = lax.broadcasted_iota(jnp.int32, (SMALL, VOX), 0)
-    occ_rows = jnp.where(rows == 0, jnp.broadcast_to(occ[...], (SMALL, VOX)), 0).astype(F32).astype(BF16)
-    row = lax.broadcasted_iota(jnp.int32, (SMALL, LANES), 0)
-    first = jnp.where(row == 0, 1.0, 0.0).astype(BF16)
-    filled = contract(occ_rows, first, 0, 0)
-    mask[...] = filled
+    filled = filled_rows(occ[...])
     block = feat[...].astype(F32) * filled
-    masked[...] = block.astype(BF16)
     offsets = lax.broadcasted_iota(jnp.int32, (32, LANES), 0)
     found = jnp.zeros((32, LANES), jnp.int32)
     for o in range(27):
         found = jnp.where(offsets == o, rule[0, o], found)
     found = found.astype(F32)
-    rule_rows[...] = found
     layer, held = layers_of(block), layers_of(filled)
     top = EDGE - 1
     upward = jnp.concatenate([layer(top), layer(top - 1), layer(0), held(top), found], axis=0)
     downward = jnp.concatenate([layer(0), layer(1), layer(top), held(0), found], axis=0)
-    put_sides(parity, upward, downward, send_a, send_b)
-
-
-def labels_kernel(labels, filt_in, onehot, filt):
+    put_sides(upward, downward, send_a, send_b)
+
+
+def prep_kernel(feat, occ, found, filt_in, masked, mask, rule, filt):
     filt[...] = filt_in[...]
-    rows = lax.broadcasted_iota(jnp.int32, (SMALL, VOX), 0)
-    hot_rows = jnp.where(rows == jnp.broadcast_to(labels[...], (SMALL, VOX)), 1.0, 0.0).astype(BF16)
-    row = lax.broadcasted_iota(jnp.int32, (SMALL, LANES), 0)
-    lane = lax.broadcasted_iota(jnp.int32, (SMALL, LANES), 1)
-    unit = jnp.where(row == lane, 1.0, 0.0).astype(BF16)
-    onehot[...] = contract(hot_rows, unit, 0, 0)
-
-
-def one_kernel(rule, parity, masked, recv_a, recv_b, filt, mask, act, act_below, act_above, pre, win, rim):
-    below, above = from_sides(parity, recv_a[...], recv_b[...])
+    row = lax.broadcasted_iota(jnp.int32, (SMALL, 27), 0)
+    rule_rows = jnp.where(row == 0, jnp.broadcast_to(found[...], (SMALL, 27)), 0).astype(F32).astype(BF16)
+    one_row = lax.broadcasted_iota(jnp.int32, (SMALL, LANES), 0)
+    rule[...] = contract(rule_rows, jnp.where(one_row == 0, 1.0, 0.0).astype(BF16), 0, 0)
+    filled = filled_rows(occ[...])
+    mask[...] = filled
+    masked[...] = (feat[...].astype(F32) * filled).astype(BF16)
+
+
+def one_kernel(rule, masked, mask, recv_a, recv_b, filt, act, act_below, act_above, pre, win, rim):
+    below, above = from_sides(recv_a[...], recv_b[...])
     block = masked[...].astype(F32)
     build_windows(block, below[:64], above[:64], rule, win)
     total = forward_sum(win, filt) * mask[...]
@@ -237,63 +236,67 @@
 
 
 def two_kernel(
-    classes, rule, parity, act_one, act_below, act_above, filt, mask, onehot, head,
+    classes, rule, act_one, act_below, act_above, filt, mask, labels, head_rows,
     win, grad, small, send_a, send_b,
 ):
     build_windows(act_one[...].astype(F32), act_below[...].astype(F32), act_above[...].astype(F32), rule, win)
+    head = jnp.concatenate([head_rows[...].astype(F32), jnp.zeros((LANES - classes, LANES), F32)], axis=0).astype(BF16)
+    rows = lax.broadcasted_iota(jnp.int32, (SMALL, VOX), 0)
+    hot_rows = jnp.where(rows == jnp.broadcast_to(labels[...], (SMALL, VOX)), 1.0, 0.0).astype(BF16)
+    unit_row = lax.broadcasted_iota(jnp.int32, (SMALL, LANES), 0)
+    unit_lane = lax.broadcasted_iota(jnp.int32, (SMALL, LANES), 1)
+    hot = contract(hot_rows, jnp.where(unit_row == unit_lane, 1.0, 0.0).astype(BF16), 0, 0)
     filled = mask[...]
     pre = forward_sum(win, filt) * filled
     acted, slope = silu_parts(pre)
     acted = acted.astype(BF16)
     lane = lax.broadcasted_iota(jnp.int32, (VOX, LANES), 1)
-    logits = contract(acted, head[...], 1, 1)
+    logits = contract(acted, head, 1, 1)
     known = lane < classes
     top = jnp.max(jnp.where(known, logits, -jnp.inf), axis=1, keepdims=True)
     powers = jnp.where(known, jnp.exp(jnp.where(known, logits - top, 0.0)), 0.0)
     total_log = top + jnp.log(jnp.sum(powers, axis=1, keepdims=True))
-    hot = onehot[...]
     chances = jnp.where(known, jnp.exp(jnp.where(known, logits - total_log, 0.0)), 0.0)
     dlogits = (chances - hot) * filled
     high = dlogits.astype(BF16)
     low = (dlogits - high.astype(F32)).astype(BF16)
-    back = jnp.dot(high, head[...], preferred_element_type=F32) + jnp.dot(low, head[...], preferred_element_type=F32)
+    back = jnp.dot(high, head, preferred_element_type=F32) + jnp.dot(low, head, preferred_element_type=F32)
     out = (back * slope * filled).astype(BF16)
     grad[...] = out
-    put_layers(out.astype(F32), parity, send_a, send_b)
-    head_rows = (contract(high, acted, 0, 0) + contract(low, acted, 0, 0))[:SMALL]
+    put_layers(out.astype(F32), send_a, send_b)
+    head_terms = (contract(high, acted, 0, 0) + contract(low, acted, 0, 0))[:SMALL]
     losses = jnp.sum((total_log - logits) * hot * filled, axis=0, keepdims=True)
     counted = jnp.sum(filled, axis=0, keepdims=True)
     tail = jnp.where(lane[:1] < classes, losses, jnp.where(lane[:1] == classes, counted, 0.0))
     row = lax.broadcasted_iota(jnp.int32, (SMALL, LANES), 0)
-    values = jnp.where(row < classes, head_rows, jnp.where(row == classes, tail, 0.0))
+    values = jnp.where(row < classes, head_terms, jnp.where(row == classes, tail, 0.0))
     small[...] = values
 
 
-def terms_kernel(rule, parity, masked, recv_a, recv_b, win_two, grad, small, out, win_one, wide):
+def terms_kernel(rule, masked, recv_a, recv_b, win_two, grad, small, out, win_one, wide):
     filter_terms(win_two, grad[...], small, wide, out)
-    below, above = from_sides(parity, recv_a[...], recv_b[...])
+    below, above = from_sides(recv_a[...], recv_b[...])
     build_windows(masked[...].astype(F32), below[:64], above[:64], rule, win_one)
 
 
 def three_kernel(
-    rule, parity, grad_two, recv_a, recv_b, filt, mask, pre, win_one, small,
+    rule, grad_two, recv_a, recv_b, filt, mask, pre, win_one, small,
     grad_one, terms, send_a, send_b, win, wide,
 ):
-    below, above = from_sides(parity, recv_a[...], recv_b[...])
+    below, above = from_sides(recv_a[...], recv_b[...])
     build_windows(grad_two[...].astype(F32), below, above, rule, win)
     _, slope = silu_parts(pre[...])
     out = (backward_sum(win, filt) * slope * mask[...]).astype(BF16)
     grad_one[...] = out
-    put_layers(out.astype(F32), parity, send_a, send_b)
+    put_layers(out.astype(F32), send_a, send_b)
     filter_terms(win_one, out, small, wide, terms)
 
 
-def four_kernel(rule, parity, grad_one, recv_a, recv_b, filt, mask, out, token, win):
-    below, above = from_sides(parity, recv_a[...], recv_b[...])
+def four_kernel(rule, grad_one, recv_a, recv_b, filt, mask, later, out, win):
+    below, above = from_sides(recv_a[...], recv_b[...])
     build_windows(grad_one[...].astype(F32), below, above, rule, win)
     total = backward_sum(win, filt) * mask[...]
     out[...] = total.astype(BF16)
-    token[...] = total[:SMALL]
 
 
 def call(kernel, outs, specs, scratch=(), flops=0, params=PARAMS):
@@ -321,14 +324,14 @@
 CONV = 2 * 27 * VOX * LANES * LANES
 
 
-def swap_a(value):
+def send_up(value):
     length = lax.axis_size(SPACE)
-    return lax.ppermute(value, SPACE, [(i, i ^ 1) for i in range(length)])
-
-
-def swap_b(value):
+    return lax.ppermute(value, SPACE, [(i, (i + 1) % length) for i in range(length)])
+
+
+def send_down(value):
     length = lax.axis_size(SPACE)
-    return lax.ppermute(value, SPACE, [(i, (i + 1) % length if i % 2 else (i - 1) % length) for i in range(length)])
+    return lax.ppermute(value, SPACE, [(i, (i - 1) % length) for i in range(length)])
 
 
 def far_swap(value):
@@ -360,7 +363,7 @@
         out[p] = jnp.concatenate([total[p * rows : (p + 1) * rows], tail], axis=0).astype(BF16)
 
 
-def half_kernel(rows, peers, parts, later_a, later_b, out):
+def half_kernel(rows, peers, parts, out):
     total = parts[0].astype(F32)
     for p in range(1, peers):
         total = total + parts[p].astype(F32)
@@ -368,7 +371,7 @@
     out[...] = jnp.concatenate([total[:rows], tail, jnp.zeros((SMALL, LANES), F32)], axis=0).astype(BF16)
 
 
-def copies_kernel(rows, peers, classes, mine, other, later, out, head, loss):
+def copies_kernel(rows, peers, classes, mine, other, later_a, later_b, out, head, loss):
     a, b = mine[...].astype(F32), other[...].astype(F32)
     both = (a[:rows] + b[:rows]).astype(BF16)
     for p in range(peers):
@@ -383,45 +386,44 @@
 
 
 def local(classes, features, occupancy, labels, rulebook, filter_one, filter_two, head_weight):
-    parity = (lax.axis_index(SPACE) % 2).reshape(1).astype(jnp.int32)
     core = lax.axis_index("core").reshape(1).astype(jnp.int32)
-    head = jnp.zeros((LANES, LANES), BF16).at[:classes].set(head_weight.T)
-    masked, mask, rule, a, b = call(
+    inputs = features.reshape(VOX, LANES), occupancy.reshape(1, VOX), rulebook.reshape(1, 27)
+    a, b = call(
         first_kernel,
-        (BLOCK, WIDE_BLOCK, sds((32, LANES), F32), SIDE, SIDE),
-        [SMEM, ANY, ANY, ANY],
+        (SIDE, SIDE),
+        [ANY] * 3,
         [pltpu.VMEM((VOX, LANES), BF16), pltpu.VMEM((1, VOX), jnp.int32), pltpu.SMEM((1, 27), jnp.int32), SEM((3,))],
-    )(parity, features.reshape(VOX, LANES), occupancy.reshape(1, VOX), rulebook.reshape(1, 27))
-    a, b = swap_a(a), swap_b(b)
-    onehot, filter_here = call(labels_kernel, (WIDE_BLOCK, FILTER), [VMEM] * 2)(labels.reshape(1, VOX), filter_one)
+        params=ROOMY,
+    )(*inputs)
+    a, b = send_up(a), send_down(b)
+    masked, mask, rule, filter_here = call(
+        prep_kernel, (BLOCK, WIDE_BLOCK, sds((27, LANES), F32), FILTER), [VMEM] * 4
+    )(*inputs, filter_one)
     act_one, act_below, act_above, pre_one = call(
         one_kernel,
         (BLOCK, LAYER, LAYER, WIDE_BLOCK),
-        [VMEM, SMEM] + [VMEM] * 5,
+        [VMEM] * 6,
         [WIN_SCRATCH, pltpu.VMEM((128, 27 * LANES), BF16)],
         CONV,
-    )(rule, parity, masked, a, b, filter_here, mask)
+    )(rule, masked, mask, a, b, filter_here)
     win_two, grad_two, small, e, f = call(
         functools.partial(two_kernel, classes),
         (WINDOWS, BLOCK, sds((SMALL, LANES), F32), LAYER, LAYER),
-        [VMEM, SMEM] + [VMEM] * 7,
+        [VMEM] + [VMEM] * 7,
         flops=CONV,
-    )(rule, parity, act_one, act_below, act_above, filter_two, mask, onehot, head)
-    e, f = swap_a(e), swap_b(f)
-    terms_two, win_one = call(terms_kernel, (TERMS, WINDOWS), [VMEM, SMEM] + [VMEM] * 6, [WIDE_SCRATCH], CONV)(
-        rule, parity, masked, a, b, win_two, grad_two, small
+    )(rule, act_one, act_below, act_above, filter_two, mask, labels.reshape(1, VOX), head_weight.T)
+    e, f = send_up(e), send_down(f)
+    terms_two, win_one = call(terms_kernel, (TERMS, WINDOWS), [VMEM] + [VMEM] * 6, [WIDE_SCRATCH], CONV)(
+        rule, masked, a, b, win_two, grad_two, small
     )
     grad_one, terms_one, g, h = call(
         three_kernel,
         (BLOCK, TERMS, LAYER, LAYER),
-        [VMEM, SMEM] + [VMEM] * 8,
+        [VMEM] + [VMEM] * 8,
         [WIN_SCRATCH, WIDE_SCRATCH],
         2 * CONV,
-    )(rule, parity, grad_two, e, f, filter_two, mask, pre_one, win_one, small)
-    g, h = swap_a(g), swap_b(h)
-    grad_in, token = call(
-        four_kernel, (BLOCK, sds((SMALL, LANES), F32)), [VMEM, SMEM] + [VMEM] * 5, [WIN_SCRATCH], CONV
-    )(rule, parity, grad_one, g, h, filter_one, mask)
+    )(rule, grad_two, e, f, filter_two, mask, pre_one, win_one, small)
+    g, h = send_up(g), send_down(h)
     peers = lax.axis_size("near") * lax.axis_size("x")
     rows = -(-27 * LANES // (peers * 16)) * 16
     away = jnp.where(core[0] == 0, terms_two, terms_one)
@@ -432,16 +434,19 @@
     )(core, terms_one, terms_two, core_swap(away))
     parts = lax.all_to_all(chunks, ("near", "x"), 0, 0, tiled=True)
     part = call(
-        functools.partial(half_kernel, rows, peers), sds((rows + 2 * SMALL, LANES), BF16), [VMEM, ANY, ANY]
-    )(parts, g, h)
+        functools.partial(half_kernel, rows, peers), sds((rows + 2 * SMALL, LANES), BF16), [VMEM]
+    )(parts)
     copies, head_sum, loss = call(
         functools.partial(copies_kernel, rows, peers, classes),
         (sds((peers, rows, LANES), BF16), sds((classes, LANES), F32), sds((1, LANES), F32)),
-        [VMEM, VMEM, ANY],
-    )(part, far_swap(part), token)
+        [VMEM, VMEM, ANY, ANY],
+    )(part, far_swap(part), g, h)
     whole = lax.all_to_all(copies, ("near", "x"), 0, 0, tiled=True)
     whole = whole.reshape(peers * rows, LANES)[: 27 * LANES].reshape(27, LANES, LANES)
     whole_other = core_swap(whole)
+    grad_in = call(four_kernel, BLOCK, [VMEM] + [VMEM] * 5 + [ANY], [WIN_SCRATCH], CONV)(
+        rule, grad_one, g, h, filter_one, mask, whole
+    )
     scale = 1.0 / VOX
     return (
         jnp.where(core[0] == 0, whole, whole_other).astype(F32) * scale,

time: 79.8 us -> 75.6 us (0.947)
  waiting for transfers between devices: 21.3 us -> 3.6 us
  blocking collectives: 15.4 us -> 28.2 us
  starting transfers between devices: 21.6 us -> 23.9 us
  local copies, waits for them, and re-layouts: 4.77 us -> 3.42 us
    all_to_all x0 -> x1, blocking collectives: none -> 15.5 us  [local(): parts = lax.all_to_all(chunks, ('near', 'x'), 0, 0, tiled=True)]
    ppermute x6, waiting for transfers between devices: 10.7 us -> 1.24 us  [the longest x3 1.23 us: send_up(): lax.ppermute(value, SPACE, [(i, (i + 1) % length) for i in range(length)])]
    ppermute x1, waiting for transfers between devices: 6.51 us -> 0.01 us  [far_swap(): return lax.ppermute(value, 'far', [(0, 1), (1, 0)])]
    ppermute x1, starting transfers between devices: 0.07 us -> 4.47 us  [far_swap(): return lax.ppermute(value, 'far', [(0, 1), (1, 0)])]
    all_to_all x1 -> x0, starting transfers between devices: 3.68 us -> none  [local(): parts = lax.all_to_all(chunks, ('near', 'x'), 0, 0, tiled=True)]
    all_to_all x1, blocking collectives: 15.4 us -> 12.8 us  [local(): whole = lax.all_to_all(copies, ('near', 'x'), 0, 0, tiled=True)]
    ppermute x2, waiting for transfers between devices: 4.15 us -> 2.36 us  [core_swap(): return lax.ppermute(value, 'core', [(0, 1), (1, 0)])]
    ppermute x2, starting transfers between devices: 4.64 us -> 5.81 us  [core_swap(): return lax.ppermute(value, 'core', [(0, 1), (1, 0)])]
  transfers between devices with their start and end apart: 10 -> 9, of which waited for: 6 -> 3; matrix products, arithmetic and copies ran while one was open for 1% -> 0% of each run, Pallas kernels for 4% -> 5%
where the time goes in v4:
time: 75.6 us; the launch traced here: 75 us
  blocking collectives  28.2 us (37%)
  starting transfers between devices  23.9 us (32%)
  Pallas kernels  12.7 us (17%)
  waiting for transfers between devices  3.6 us (5%)
  local copies, waits for them, and re-layouts  3.42 us (5%)
  other arithmetic  2.37 us (3%)
  between operations  0.79 us (1%)
    all_to_all x1, blocking collectives, local(): parts = lax.all_to_all(chunks, ('near', 'x'), 0, 0, tiled=True)  15.5 us
    all_to_all x1, blocking collectives, local(): whole = lax.all_to_all(copies, ('near', 'x'), 0, 0, tiled=True)  12.8 us
    ppermute x3, starting transfers between devices, send_down(): lax.ppermute(value, SPACE, [(i, (i - 1) % length) for i in range(length)])  11.1 us
    ppermute x2, starting transfers between devices, core_swap(): return lax.ppermute(value, 'core', [(0, 1), (1, 0)])  5.81 us
    ppermute x1, starting transfers between devices, far_swap(): return lax.ppermute(value, 'far', [(0, 1), (1, 0)])  4.47 us
    unnamed x16, local copies, waits for them, and re-layouts  3.42 us
    pallas_call x1, Pallas kernels, local(): call(three_kernel, (BLOCK, TERMS, LAYER, LAYER), [VMEM] + [VMEM] * 8, [WI...  2.75 us
    ppermute x3, starting transfers between devices, send_up(): lax.ppermute(value, SPACE, [(i, (i + 1) % length) for i in range(length)])  2.46 us
  transfers between devices with their start and end apart: 9, of which 3 were waited for; matrix products, arithmetic and copies ran while one was open for 0% of the time, Pallas kernels for 5%

profile of v4, /device:TPU:1, one launch (start us, length us, event | category | flops | bytes accessed | tf_op | source)
XLA Modules:
  0.0 75.0 jit_solution(2808283872555505795)
XLA Ops:
  0.6 0.0 copy-start.7
  0.6 0.0 copy-start.6
  0.7 1.9 %shard_map.111 = (bf16[288,128]{1,0:T(8,128)(2,1)}, bf16[288,128]{1,0:T(8,128)(2,1)}) custom-call(bf16[512,128]{1,0:T(8,128)(2,1)} %bitcast.14, s32[1,512]{1,0:T(1,128)} %bitcast.16, s32[1,27]{1,0:T(1,128)} %bitcast.18), custom_call_target="tpu_custom_call" | custom-call | bytes 4000000 | tf_op jit(solution)/shard_map/pallas_call | solution.py:391
  2.6 2.1 %collective-permute-start = (bf16[288,128]{1,0:T(8,128)(2,1)}, bf16[288,128]{1,0:T(8,128)(2,1)S(1)}, u32[]{:S(2)}, u32[]{:S(2)}) collective-permute-start(bf16[288,128]{1,0:T(8,128)(2,1)} %get-tuple-element.32), channel_id=1, source_target_pairs={{0,4},{4,8},{8,12},{12,16},{16,20},{20,24},{24,28},{28,0},{1,5},{5... | collective-permute-start | bytes 221192 | tf_op jit(solution)/shard_map/ppermute | solution.py:329
  4.7 3.1 %collective-permute-start.1 = (bf16[288,128]{1,0:T(8,128)(2,1)}, bf16[288,128]{1,0:T(8,128)(2,1)S(1)}, u32[]{:S(2)}, u32[]{:S(2)}) collective-permute-start(bf16[288,128]{1,0:T(8,128)(2,1)} %get-tuple-element.33), channel_id=1, source_target_pairs={{0,28},{4,0},{8,4},{12,8},{16,12},{20,16},{24,20},{28,24},{1,29},{... | collective-permute-start | bytes 221192 | tf_op jit(solution)/shard_map/ppermute | solution.py:334
  7.8 0.0 copy-start
  7.8 1.2 %copy-done = bf16[27,128,128]{2,1,0:T(8,128)(2,1)S(1)} copy-done((bf16[27,128,128]{2,1,0:T(8,128)(2,1)S(1)}, bf16[27,128,128]{2,1,0:T(8,128)(2,1)}, u32[]{:S(2)}) %copy-start) | copy-done | bytes 884760
  9.0 0.0 copy-start.2
  9.0 0.9 %copy-done.2 = bf16[1,1,512,128]{3,2,1,0:T(8,128)(2,1)S(1)} copy-done((bf16[1,1,512,128]{3,2,1,0:T(8,128)(2,1)S(1)}, bf16[1,1,512,128]{3,2,1,0:T(8,128)(2,1)}, u32[]{:S(2)}) %copy-start.2) | copy-done | bytes 131096
  9.9 0.0 copy-start.3
  9.9 0.7 copy-done.3
  10.5 0.0 copy-start.4
  10.5 0.7 copy-done.4
  11.2 0.0 copy-start.5
  11.2 0.2 shard_map.110
  11.4 0.0 collective-permute-done.recv_a
  11.5 0.0 collective-permute-done.1.recv_b
  11.5 1.5 %shard_map.112 = (bf16[512,128]{1,0:T(8,128)(2,1)S(1)}, bf16[64,128]{1,0:T(8,128)(2,1)S(1)}, bf16[64,128]{1,0:T(8,128)(2,1)S(1)}, f32[512,128]{1,0:T(8,128)S(1)}) custom-call(f32[27,128]{1,0:T(8,128)S(1)} %get-tuple-element.29.rule, bf16[512,128]{1,0:T(8,128)(2,1)S(1)} %get-tuple-element.30.masked, f32[512,128]{1,0:T(8,128)S(1)} %get-tuple-element.31.mask, ...), custom_call_target="tpu_custom_call" | custom-call | flops 452984832 | bytes 4000000 | tf_op jit(solution)/shard_map/pallas_call | solution.py:402
  13.0 0.0 copy-done.7
  13.0 0.0 copy-done.6
  13.0 0.0 copy-done.5
  13.0 2.0 %shard_map.113 = (bf16[640,1152]{1,0:T(8,128)(2,1)S(1)}, bf16[512,128]{1,0:T(8,128)(2,1)S(1)}, f32[8,128]{1,0:T(8,128)S(1)}, bf16[64,128]{1,0:T(8,128)(2,1)S(1)}, bf16[64,128]{1,0:T(8,128)(2,1)S(1)}) custom-call(f32[27,128]{1,0:T(8,128)S(1)} %get-tuple-element.29.rule, bf16[512,128]{1,0:T(8,128)(2,1)S(1)} %get-tuple-element.35.act_one, ...), custom_call_target="tpu_custom_call" | custom-call | flops 452984832 | bytes 4000000 | tf_op jit(solution)/shard_map/pallas_call | solution.py:409
  15.0 0.1 collective-permute-start.2
  15.1 4.1 %collective-permute-start.3 = (bf16[64,128]{1,0:T(8,128)(2,1)S(1)}, bf16[64,128]{1,0:T(8,128)(2,1)S(1)}, u32[]{:S(2)}, u32[]{:S(2)}) collective-permute-start(bf16[64,128]{1,0:T(8,128)(2,1)S(1)} %get-tuple-element.40), channel_id=1, source_target_pairs={{0,28},{4,0},{8,4},{12,8},{16,12},{20,16},{24,20},{28,24},{1,29},{... | collective-permute-start | bytes 49160 | tf_op jit(solution)/shard_map/ppermute | solution.py:334
  19.2 1.5 %shard_map.114 = (bf16[28,128,128]{2,1,0:T(8,128)(2,1)S(1)}, bf16[640,1152]{1,0:T(8,128)(2,1)S(1)}) custom-call(f32[27,128]{1,0:T(8,128)S(1)} %get-tuple-element.29.rule, bf16[512,128]{1,0:T(8,128)(2,1)S(1)} %get-tuple-element.30.masked, bf16[288,128]{1,0:T(8,128)(2,1)S(1)} %collective-permute-done.recv_a, ...), custom_call_target="tpu_custom_call" | custom-call | flops 452984832 | bytes 4000000 | tf_op jit(solution)/shard_map/pallas_call | solution.py:416
  20.8 0.0 collective-permute-done.2.recv_a
  20.8 0.0 collective-permute-done.3.recv_b
  20.8 2.8 %shard_map.115 = (bf16[512,128]{1,0:T(8,128)(2,1)S(1)}, bf16[28,128,128]{2,1,0:T(8,128)(2,1)S(1)}, bf16[64,128]{1,0:T(8,128)(2,1)S(1)}, bf16[64,128]{1,0:T(8,128)(2,1)S(1)}) custom-call(f32[27,128]{1,0:T(8,128)S(1)} %get-tuple-element.29.rule, bf16[512,128]{1,0:T(8,128)(2,1)S(1)} %get-tuple-element.38.grad.grad_two, ...), custom_call_target="tpu_custom_call" | custom-call | flops 905969664 | bytes 4000000 | tf_op jit(solution)/shard_map/pallas_call | solution.py:419
  23.6 0.1 broadcast_select_fusion
  23.7 1.7 %collective-permute-start.4 = (bf16[28,128,128]{2,1,0:T(8,128)(2,1)S(1)}, bf16[28,128,128]{2,1,0:T(8,128)(2,1)S(1)}, u32[]{:S(2)}, u32[]{:S(2)}) collective-permute-start(bf16[28,128,128]{2,1,0:T(8,128)(2,1)S(1)} %broadcast_select_fusion), channel_id=1, source_target_pairs={{0,1},{1,0},{2,3},{3,2},{4,5},{5,4},{6,7},{7,6},{8,9},{9,8},{10,11... | collective-permute-start | bytes 2752520 | tf_op jit(solution)/shard_map/ppermute | solution.py:342
  25.4 2.1 %collective-permute-done.4.other = bf16[28,128,128]{2,1,0:T(8,128)(2,1)S(1)} collective-permute-done((bf16[28,128,128]{2,1,0:T(8,128)(2,1)S(1)}, bf16[28,128,128]{2,1,0:T(8,128)(2,1)S(1)}, u32[]{:S(2)}, u32[]{:S(2)}) %collective-permute-start.4) | collective-permute-done | bytes 917536 | tf_op jit(solution)/shard_map/ppermute | solution.py:342
  27.5 0.3 shard_map.116
  27.8 15.5 %all_to_all.10.parts = bf16[8,448,128]{2,1,0:T(8,128)(2,1)S(1)} all-to-all(bf16[8,448,128]{2,1,0:T(8,128)(2,1)S(1)} %shard_map.116), channel_id=1, replica_groups=mesh['far'=2,'near'=4,'x'=2,'core'=2] {'near','x'}, dimensions={0} | all-to-all | bytes 1835008 | tf_op jit(solution)/shard_map/all_to_all | solution.py:435
  43.2 0.0 copy-start.1
  43.3 0.1 shard_map.117.mine
  43.4 4.5 %collective-permute-start.5 = (bf16[448,128]{1,0:T(8,128)(2,1)S(1)}, bf16[448,128]{1,0:T(8,128)(2,1)S(1)}, u32[]{:S(2)}, u32[]{:S(2)}) collective-permute-start(bf16[448,128]{1,0:T(8,128)(2,1)S(1)} %shard_map.117.mine), channel_id=1, source_target_pairs={{0,16},{16,0},{1,17},{17,1},{2,18},{18,2},{3,19},{19,3},{4,20},{20... | collective-permute-start | bytes 344072 | tf_op jit(solution)/shard_map/ppermute | solution.py:338
  47.9 0.3 collective-permute-start.6
  48.1 3.9 %collective-permute-start.7 = (bf16[64,128]{1,0:T(8,128)(2,1)S(1)}, bf16[64,128]{1,0:T(8,128)(2,1)S(1)}, u32[]{:S(2)}, u32[]{:S(2)}) collective-permute-start(bf16[64,128]{1,0:T(8,128)(2,1)S(1)} %get-tuple-element.48), channel_id=1, source_target_pairs={{0,28},{4,0},{8,4},{12,8},{16,12},{20,16},{24,20},{28,24},{1,29},{... | collective-permute-start | bytes 49160 | tf_op jit(solution)/shard_map/ppermute | solution.py:334
  52.0 1.2 %collective-permute-done.6.later_a.recv_a = bf16[64,128]{1,0:T(8,128)(2,1)S(1)} collective-permute-done((bf16[64,128]{1,0:T(8,128)(2,1)S(1)}, bf16[64,128]{1,0:T(8,128)(2,1)S(1)}, u32[]{:S(2)}, u32[]{:S(2)}) %collective-permute-start.6) | collective-permute-done | bytes 16416 | tf_op jit(solution)/shard_map/ppermute | solution.py:329
  53.2 0.0 collective-permute-done.7.later_b.recv_b
  53.2 0.0 collective-permute-done.5.other
  53.2 0.6 shard_map.118
  53.9 12.8 %all_to_all.11 = bf16[8,432,128]{2,1,0:T(8,128)(2,1)S(1)} all-to-all(bf16[8,432,128]{2,1,0:T(8,128)(2,1)S(1)} %get-tuple-element.49), channel_id=1, replica_groups=mesh['far'=2,'near'=4,'x'=2,'core'=2] {'near','x'}, dimensions={0} | all-to-all | bytes 1769472 | tf_op jit(solution)/shard_map/all_to_all | solution.py:444
  66.6 4.1 %collective-permute-start.8 = (bf16[27,128,128]{2,1,0:T(8,128)(2,1)S(1)}, bf16[27,128,128]{2,1,0:T(8,128)(2,1)S(1)}, u32[]{:S(2)}, u32[]{:S(2)}) collective-permute-start(bf16[27,128,128]{2,1,0:T(8,128)(2,1)S(1)} %bitcast.11), channel_id=1, source_target_pairs={{0,1},{1,0},{2,3},{3,2},{4,5},{5,4},{6,7},{7,6},{8,9},{9,8},{10,11... | collective-permute-start | bytes 2654216 | tf_op jit(solution)/shard_map/ppermute | solution.py:342
  70.7 0.0 copy-done.1
  70.7 1.8 %shard_map.119 = bf16[512,128]{1,0:T(8,128)(2,1)} custom-call(f32[27,128]{1,0:T(8,128)S(1)} %get-tuple-element.29.rule, bf16[512,128]{1,0:T(8,128)(2,1)S(1)} %get-tuple-element.52.grad_one, bf16[64,128]{1,0:T(8,128)(2,1)S(1)} %collective-permute-done.6.later_a.recv_a, bf16[64,128]{1,0:T(8,128)(2,1)S(1)} %collective-permute-done.7.later_b.recv_b, ...), custom_call_target="tpu_custom_call" | custom-call | flops 452984832 | bytes 4000000 | tf_op jit(solution)/shard_map/pallas_call | solution.py:447
  72.5 0.3 collective-permute-done.8
  72.8 2.3 %convert_multiply_fusion = (f32[27,128,128]{2,1,0:T(8,128)}, f32[27,128,128]{2,1,0:T(8,128)}) fusion(bf16[27,128,128]{2,1,0:T(8,128)(2,1)S(1)} %collective-permute-done.8, bf16[27,128,128]{2,1,0:T(8,128)(2,1)S(1)} %bitcast.13, pred[]{:T(512)S(6)} %eq.2), kind=kLoop, calls=%fused_computation | loop fusion | flops 2654208 | bytes 5308417 | tf_op jit(solution)/shard_map/mul | solution.py:453
Async XLA Ops:
  0.6 12.4 %copy-start.7 = (bf16[128,3]{0,1:T(4,128)(2,1)S(1)}, bf16[128,3]{0,1:T(4,128)(2,1)}, u32[]{:S(2)}) copy-start(bf16[128,3]{0,1:T(4,128)(2,1)} %param.13) | copy-start | bytes 2308
  0.6 12.4 %copy-start.6 = (s32[1,1,512]{2,1,0:T(1,128)S(1)}, s32[1,1,512]{2,1,0:T(1,128)}, u32[]{:S(2)}) copy-start(s32[1,1,512]{2,1,0:T(1,128)} %param.9) | copy-start | bytes 6148
  2.6 8.9 %collective-permute-start = (bf16[288,128]{1,0:T(8,128)(2,1)}, bf16[288,128]{1,0:T(8,128)(2,1)S(1)}, u32[]{:S(2)}, u32[]{:S(2)}) collective-permute-start(bf16[288,128]{1,0:T(8,128)(2,1)} %get-tuple-element.32), channel_id=1, source_target_pairs={{0,4},{4,8},{8,12},{12,16},{16,20},{20,24},{24,28},{28,0},{1,5},{5... | collective-permute-start | bytes 221192 | tf_op jit(solution)/shard_map/ppermute | solution.py:329
  4.7 6.8 %collective-permute-start.1 = (bf16[288,128]{1,0:T(8,128)(2,1)}, bf16[288,128]{1,0:T(8,128)(2,1)S(1)}, u32[]{:S(2)}, u32[]{:S(2)}) collective-permute-start(bf16[288,128]{1,0:T(8,128)(2,1)} %get-tuple-element.33), channel_id=1, source_target_pairs={{0,28},{4,0},{8,4},{12,8},{16,12},{20,16},{24,20},{28,24},{1,29},{... | collective-permute-start | bytes 221192 | tf_op jit(solution)/shard_map/ppermute | solution.py:334
  7.8 1.2 %copy-start = (bf16[27,128,128]{2,1,0:T(8,128)(2,1)S(1)}, bf16[27,128,128]{2,1,0:T(8,128)(2,1)}, u32[]{:S(2)}) copy-start(bf16[27,128,128]{2,1,0:T(8,128)(2,1)} %filt.5) | copy-start | bytes 2654212
  9.0 0.9 %copy-start.2 = (bf16[1,1,512,128]{3,2,1,0:T(8,128)(2,1)S(1)}, bf16[1,1,512,128]{3,2,1,0:T(8,128)(2,1)}, u32[]{:S(2)}) copy-start(bf16[1,1,512,128]{3,2,1,0:T(8,128)(2,1)} %param.7) | copy-start | bytes 393220
  9.9 0.7 copy-start.3
  10.5 0.7 copy-start.4
  11.2 1.8 %copy-start.5 = (bf16[27,128,128]{2,1,0:T(8,128)(2,1)S(1)}, bf16[27,128,128]{2,1,0:T(8,128)(2,1)}, u32[]{:S(2)}) copy-start(bf16[27,128,128]{2,1,0:T(8,128)(2,1)} %filt.4) | copy-start | bytes 2654212
  15.0 5.8 %collective-permute-start.2 = (bf16[64,128]{1,0:T(8,128)(2,1)S(1)}, bf16[64,128]{1,0:T(8,128)(2,1)S(1)}, u32[]{:S(2)}, u32[]{:S(2)}) collective-permute-start(bf16[64,128]{1,0:T(8,128)(2,1)S(1)} %get-tuple-element.39), channel_id=1, source_target_pairs={{0,4},{4,8},{8,12},{12,16},{16,20},{20,24},{24,28},{28,0},{1,5},{5... | collective-permute-start | bytes 49160 | tf_op jit(solution)/shard_map/ppermute | solution.py:329
  15.1 5.7 %collective-permute-start.3 = (bf16[64,128]{1,0:T(8,128)(2,1)S(1)}, bf16[64,128]{1,0:T(8,128)(2,1)S(1)}, u32[]{:S(2)}, u32[]{:S(2)}) collective-permute-start(bf16[64,128]{1,0:T(8,128)(2,1)S(1)} %get-tuple-element.40), channel_id=1, source_target_pairs={{0,28},{4,0},{8,4},{12,8},{16,12},{20,16},{24,20},{28,24},{1,29},{... | collective-permute-start | bytes 49160 | tf_op jit(solution)/shard_map/ppermute | solution.py:334
  23.7 3.8 %collective-permute-start.4 = (bf16[28,128,128]{2,1,0:T(8,128)(2,1)S(1)}, bf16[28,128,128]{2,1,0:T(8,128)(2,1)S(1)}, u32[]{:S(2)}, u32[]{:S(2)}) collective-permute-start(bf16[28,128,128]{2,1,0:T(8,128)(2,1)S(1)} %broadcast_select_fusion), channel_id=1, source_target_pairs={{0,1},{1,0},{2,3},{3,2},{4,5},{5,4},{6,7},{7,6},{8,9},{9,8},{10,11... | collective-permute-start | bytes 2752520 | tf_op jit(solution)/shard_map/ppermute | solution.py:342
  43.2 27.5 %copy-start.1 = (bf16[27,128,128]{2,1,0:T(8,128)(2,1)S(1)}, bf16[27,128,128]{2,1,0:T(8,128)(2,1)}, u32[]{:S(2)}) copy-start(bf16[27,128,128]{2,1,0:T(8,128)(2,1)} %filt.5) | copy-start | bytes 2654212
  43.4 9.9 %collective-permute-start.5 = (bf16[448,128]{1,0:T(8,128)(2,1)S(1)}, bf16[448,128]{1,0:T(8,128)(2,1)S(1)}, u32[]{:S(2)}, u32[]{:S(2)}) collective-permute-start(bf16[448,128]{1,0:T(8,128)(2,1)S(1)} %shard_map.117.mine), channel_id=1, source_target_pairs={{0,16},{16,0},{1,17},{17,1},{2,18},{18,2},{3,19},{19,3},{4,20},{20... | collective-permute-start | bytes 344072 | tf_op jit(solution)/shard_map/ppermute | solution.py:338
  47.9 5.4 %collective-permute-start.6 = (bf16[64,128]{1,0:T(8,128)(2,1)S(1)}, bf16[64,128]{1,0:T(8,128)(2,1)S(1)}, u32[]{:S(2)}, u32[]{:S(2)}) collective-permute-start(bf16[64,128]{1,0:T(8,128)(2,1)S(1)} %get-tuple-element.47), channel_id=1, source_target_pairs={{0,4},{4,8},{8,12},{12,16},{16,20},{20,24},{24,28},{28,0},{1,5},{5... | collective-permute-start | bytes 49160 | tf_op jit(solution)/shard_map/ppermute | solution.py:329
  48.1 5.1 %collective-permute-start.7 = (bf16[64,128]{1,0:T(8,128)(2,1)S(1)}, bf16[64,128]{1,0:T(8,128)(2,1)S(1)}, u32[]{:S(2)}, u32[]{:S(2)}) collective-permute-start(bf16[64,128]{1,0:T(8,128)(2,1)S(1)} %get-tuple-element.48), channel_id=1, source_target_pairs={{0,28},{4,0},{8,4},{12,8},{16,12},{20,16},{24,20},{28,24},{1,29},{... | collective-permute-start | bytes 49160 | tf_op jit(solution)/shard_map/ppermute | solution.py:334
  66.6 6.1 %collective-permute-start.8 = (bf16[27,128,128]{2,1,0:T(8,128)(2,1)S(1)}, bf16[27,128,128]{2,1,0:T(8,128)(2,1)S(1)}, u32[]{:S(2)}, u32[]{:S(2)}) collective-permute-start(bf16[27,128,128]{2,1,0:T(8,128)(2,1)S(1)} %bitcast.11), channel_id=1, source_target_pairs={{0,1},{1,0},{2,3},{3,2},{4,5},{5,4},{6,7},{7,6},{8,9},{9,8},{10,11... | collective-permute-start | bytes 2654216 | tf_op jit(solution)/shard_map/ppermute | solution.py:342

commit v5 on v4

--- a/solution.py
+++ b/solution.py
@@ -34,8 +34,10 @@
     return jnp.broadcast_to(layer.astype(F32).reshape(64, 1, LANES), (64, EDGE, LANES))
 
 
-def from_sides(recv_a, recv_b):
-    return recv_a.astype(F32), recv_b.astype(F32)
+def from_sides(parity_ref, recv_a, recv_b):
+    even = parity_ref[0] == 0
+    got_a, got_b = recv_a.astype(F32), recv_b.astype(F32)
+    return jnp.where(even, got_b, got_a), jnp.where(even, got_a, got_b)
 
 
 def build_windows(block, below, above, rule_ref, out_ref):
@@ -80,9 +82,10 @@
             out_ref[:, lane : lane + LANES] = padded.reshape(640, LANES).astype(BF16)
 
 
-def put_sides(upward, downward, send_a_ref, send_b_ref):
-    send_a_ref[...] = upward.astype(BF16)
-    send_b_ref[...] = downward.astype(BF16)
+def put_sides(parity_ref, upward, downward, send_a_ref, send_b_ref):
+    even = parity_ref[0] == 0
+    send_a_ref[...] = jnp.where(even, upward, downward).astype(BF16)
+    send_b_ref[...] = jnp.where(even, downward, upward).astype(BF16)
 
 
 def layers_of(block):
@@ -90,9 +93,9 @@
     return lambda z: cells[:, z, :]
 
 
-def put_layers(block, send_a_ref, send_b_ref):
+def put_layers(block, parity_ref, send_a_ref, send_b_ref):
     layer = layers_of(block)
-    put_sides(layer(EDGE - 1), layer(0), send_a_ref, send_b_ref)
+    put_sides(parity_ref, layer(EDGE - 1), layer(0), send_a_ref, send_b_ref)
 
 
 def layer_windows(side, mine, touching, rule, out_ref, row):
@@ -177,7 +180,7 @@
     return contract(occ_rows, jnp.where(row == 0, 1.0, 0.0).astype(BF16), 0, 0)
 
 
-def first_kernel(feat_hbm, occ_hbm, rule_hbm, send_a, send_b, feat, occ, rule, sems):
+def first_kernel(parity, feat_hbm, occ_hbm, rule_hbm, send_a, send_b, feat, occ, rule, sems):
     copies = [
         pltpu.make_async_copy(feat_hbm, feat, sems.at[0]),
         pltpu.make_async_copy(occ_hbm, occ, sems.at[1]),
@@ -198,7 +201,7 @@
     top = EDGE - 1
     upward = jnp.concatenate([layer(top), layer(top - 1), layer(0), held(top), found], axis=0)
     downward = jnp.concatenate([layer(0), layer(1), layer(top), held(0), found], axis=0)
-    put_sides(upward, downward, send_a, send_b)
+    put_sides(parity, upward, downward, send_a, send_b)
 
 
 def prep_kernel(feat, occ, found, filt_in, masked, mask, rule, filt):
@@ -212,8 +215,8 @@
     masked[...] = (feat[...].astype(F32) * filled).astype(BF16)
 
 
-def one_kernel(rule, masked, mask, recv_a, recv_b, filt, act, act_below, act_above, pre, win, rim):
-    below, above = from_sides(recv_a[...], recv_b[...])
+def one_kernel(parity, rule, masked, mask, recv_a, recv_b, filt, act, act_below, act_above, pre, win, rim):
+    below, above = from_sides(parity, recv_a[...], recv_b[...])
     block = masked[...].astype(F32)
     build_windows(block, below[:64], above[:64], rule, win)
     total = forward_sum(win, filt) * mask[...]
@@ -236,7 +239,7 @@
 
 
 def two_kernel(
-    classes, rule, act_one, act_below, act_above, filt, mask, labels, head_rows,
+    classes, parity, rule, act_one, act_below, act_above, filt, mask, labels, head_rows,
     win, grad, small, send_a, send_b,
 ):
     build_windows(act_one[...].astype(F32), act_below[...].astype(F32), act_above[...].astype(F32), rule, win)
@@ -263,7 +266,7 @@
     back = jnp.dot(high, head, preferred_element_type=F32) + jnp.dot(low, head, preferred_element_type=F32)
     out = (back * slope * filled).astype(BF16)
     grad[...] = out
-    put_layers(out.astype(F32), send_a, send_b)
+    put_layers(out.astype(F32), parity, send_a, send_b)
     head_terms = (contract(high, acted, 0, 0) + contract(low, acted, 0, 0))[:SMALL]
     losses = jnp.sum((total_log - logits) * hot * filled, axis=0, keepdims=True)
     counted = jnp.sum(filled, axis=0, keepdims=True)
@@ -273,38 +276,54 @@
     small[...] = values
 
 
-def terms_kernel(rule, masked, recv_a, recv_b, win_two, grad, small, out, win_one, wide):
+def terms_kernel(parity, rule, masked, recv_a, recv_b, win_two, grad, small, out, win_one, wide):
     filter_terms(win_two, grad[...], small, wide, out)
-    below, above = from_sides(recv_a[...], recv_b[...])
+    below, above = from_sides(parity, recv_a[...], recv_b[...])
     build_windows(masked[...].astype(F32), below[:64], above[:64], rule, win_one)
 
 
 def three_kernel(
-    rule, grad_two, recv_a, recv_b, filt, mask, pre, win_one, small,
+    parity, rule, grad_two, recv_a, recv_b, filt, mask, pre, win_one, small,
     grad_one, terms, send_a, send_b, win, wide,
 ):
-    below, above = from_sides(recv_a[...], recv_b[...])
+    below, above = from_sides(parity, recv_a[...], recv_b[...])
     build_windows(grad_two[...].astype(F32), below, above, rule, win)
     _, slope = silu_parts(pre[...])
     out = (backward_sum(win, filt) * slope * mask[...]).astype(BF16)
     grad_one[...] = out
-    put_layers(out.astype(F32), send_a, send_b)
+    put_layers(out.astype(F32), parity, send_a, send_b)
     filter_terms(win_one, out, small, wide, terms)
 
 
-def four_kernel(rule, grad_one, recv_a, recv_b, filt, mask, later, out, win):
-    below, above = from_sides(recv_a[...], recv_b[...])
+def four_kernel(parity, rule, grad_one, recv_a, recv_b, filt, mask, out, win):
+    below, above = from_sides(parity, recv_a[...], recv_b[...])
     build_windows(grad_one[...].astype(F32), below, above, rule, win)
     total = backward_sum(win, filt) * mask[...]
     out[...] = total.astype(BF16)
 
 
-def call(kernel, outs, specs, scratch=(), flops=0, params=PARAMS):
+def own_kernel(core, whole, one, two, wide, sems):
+    for part in range(3):
+        at = pl.ds(TAPS * part, TAPS)
+        wide[at] = whole[at].astype(F32) * (1.0 / VOX)
+        for wanted, out in ((0, one), (1, two)):
+            pl.when(core[0] == wanted)(pltpu.make_async_copy(wide.at[at], out.at[at], sems.at[part]).start)
+    for part in range(3):
+        at = pl.ds(TAPS * part, TAPS)
+        pltpu.make_async_copy(wide.at[at], one.at[at], sems.at[part]).wait()
+
+
+def other_kernel(core, whole, one_in, two_in, one, two, wide, sems):
+    own_kernel(core, whole, one, two, wide, sems)
+
+
+def call(kernel, outs, specs, scratch=(), flops=0, params=PARAMS, out_specs=None, alias=None):
     return pl.pallas_call(
         kernel,
         out_shape=outs,
         in_specs=specs,
-        out_specs=jax.tree.map(lambda _: VMEM, outs),
+        out_specs=jax.tree.map(lambda _: VMEM, outs) if out_specs is None else out_specs,
+        input_output_aliases=alias or {},
         scratch_shapes=list(scratch),
         compiler_params=params,
         cost_estimate=pl.CostEstimate(flops=flops, bytes_accessed=4_000_000, transcendentals=0),
@@ -324,14 +343,19 @@
 CONV = 2 * 27 * VOX * LANES * LANES
 
 
-def send_up(value):
+def swap_a(value):
     length = lax.axis_size(SPACE)
-    return lax.ppermute(value, SPACE, [(i, (i + 1) % length) for i in range(length)])
-
-
-def send_down(value):
+    return lax.ppermute(value, SPACE, [(i, i ^ 1) for i in range(length)])
+
+
+def swap_b(value):
     length = lax.axis_size(SPACE)
-    return lax.ppermute(value, SPACE, [(i, (i - 1) % length) for i in range(length)])
+    pairs = []
+    for i in range(length):
+        to = i + 1 if i % 2 else i - 1
+        for c in range(2):
+            pairs.append((2 * i + c, 2 * to + c if 0 <= to < length else 2 * i + 1 - c))
+    return lax.ppermute(value, SPACE + ("core",), pairs)
 
 
 def far_swap(value):
@@ -386,44 +410,45 @@
 
 
 def local(classes, features, occupancy, labels, rulebook, filter_one, filter_two, head_weight):
+    parity = (lax.axis_index(SPACE) % 2).reshape(1).astype(jnp.int32)
     core = lax.axis_index("core").reshape(1).astype(jnp.int32)
     inputs = features.reshape(VOX, LANES), occupancy.reshape(1, VOX), rulebook.reshape(1, 27)
     a, b = call(
         first_kernel,
         (SIDE, SIDE),
-        [ANY] * 3,
+        [SMEM] + [ANY] * 3,
         [pltpu.VMEM((VOX, LANES), BF16), pltpu.VMEM((1, VOX), jnp.int32), pltpu.SMEM((1, 27), jnp.int32), SEM((3,))],
         params=ROOMY,
-    )(*inputs)
-    a, b = send_up(a), send_down(b)
+    )(parity, *inputs)
+    a, b = swap_a(a), swap_b(b)
     masked, mask, rule, filter_here = call(
         prep_kernel, (BLOCK, WIDE_BLOCK, sds((27, LANES), F32), FILTER), [VMEM] * 4
     )(*inputs, filter_one)
     act_one, act_below, act_above, pre_one = call(
         one_kernel,
         (BLOCK, LAYER, LAYER, WIDE_BLOCK),
-        [VMEM] * 6,
+        [SMEM] + [VMEM] * 6,
         [WIN_SCRATCH, pltpu.VMEM((128, 27 * LANES), BF16)],
         CONV,
-    )(rule, masked, mask, a, b, filter_here)
+    )(parity, rule, masked, mask, a, b, filter_here)
     win_two, grad_two, small, e, f = call(
         functools.partial(two_kernel, classes),
         (WINDOWS, BLOCK, sds((SMALL, LANES), F32), LAYER, LAYER),
-        [VMEM] + [VMEM] * 7,
+        [SMEM] + [VMEM] * 8,
         flops=CONV,
-    )(rule, act_one, act_below, act_above, filter_two, mask, labels.reshape(1, VOX), head_weight.T)
-    e, f = send_up(e), send_down(f)
-    terms_two, win_one = call(terms_kernel, (TERMS, WINDOWS), [VMEM] + [VMEM] * 6, [WIDE_SCRATCH], CONV)(
-        rule, masked, a, b, win_two, grad_two, small
+    )(parity, rule, act_one, act_below, act_above, filter_two, mask, labels.reshape(1, VOX), head_weight.T)
+    e, f = swap_a(e), swap_b(f)
+    terms_two, win_one = call(terms_kernel, (TERMS, WINDOWS), [SMEM] + [VMEM] * 7, [WIDE_SCRATCH], CONV)(
+        parity, rule, masked, a, b, win_two, grad_two, small
     )
     grad_one, terms_one, g, h = call(
         three_kernel,
         (BLOCK, TERMS, LAYER, LAYER),
-        [VMEM] + [VMEM] * 8,
+        [SMEM] + [VMEM] * 9,
         [WIN_SCRATCH, WIDE_SCRATCH],
         2 * CONV,
-    )(rule, grad_two, e, f, filter_two, mask, pre_one, win_one, small)
-    g, h = send_up(g), send_down(h)
+    )(parity, rule, grad_two, e, f, filter_two, mask, pre_one, win_one, small)
+    g, h = swap_a(g), swap_b(h)
     peers = lax.axis_size("near") * lax.axis_size("x")
     rows = -(-27 * LANES // (peers * 16)) * 16
     away = jnp.where(core[0] == 0, terms_two, terms_one)
@@ -444,13 +469,18 @@
     whole = lax.all_to_all(copies, ("near", "x"), 0, 0, tiled=True)
     whole = whole.reshape(peers * rows, LANES)[: 27 * LANES].reshape(27, LANES, LANES)
     whole_other = core_swap(whole)
-    grad_in = call(four_kernel, BLOCK, [VMEM] + [VMEM] * 5 + [ANY], [WIN_SCRATCH], CONV)(
-        rule, grad_one, g, h, filter_one, mask, whole
+    grad_in = call(four_kernel, BLOCK, [SMEM] + [VMEM] * 6, [WIN_SCRATCH], CONV)(
+        parity, rule, grad_one, g, h, filter_one, mask
     )
-    scale = 1.0 / VOX
+    wide = sds((27, LANES, LANES), F32)
+    room = [pltpu.VMEM((27, LANES, LANES), F32), SEM((3,))]
+    parts = call(own_kernel, (wide, wide), [SMEM, VMEM], room, out_specs=(ANY, ANY))(core, whole)
+    sum_one, sum_two = call(
+        other_kernel, (wide, wide), [SMEM, VMEM, ANY, ANY], room, out_specs=(ANY, ANY), alias={2: 0, 3: 1}
+    )(1 - core, whole_other, *parts)
     return (
-        jnp.where(core[0] == 0, whole, whole_other).astype(F32) * scale,
-        jnp.where(core[0] == 0, whole_other, whole).astype(F32) * scale,
+        sum_one,
+        sum_two,
         head_sum.T,
         loss[0, 0],
         grad_in.reshape(features.shape),

time: 75.6 us -> 72.5 us (0.959)
  starting transfers between devices: 23.9 us -> 13.3 us
  blocking collectives: 28.2 us -> 33.2 us
  Pallas kernels: 12.7 us -> 15.5 us
  waiting for transfers between devices: 3.6 us -> 6 us
  other arithmetic: 2.37 us -> 0.1 us
    ppermute x6, starting transfers between devices: 13.6 us -> 8.73 us  [the longest x3 4.72 us: swap_b(): return lax.ppermute(value, SPACE + ('core',), pairs)]
    all_to_all x1, blocking collectives: 15.5 us -> 19.3 us  [local(): parts = lax.all_to_all(chunks, ('near', 'x'), 0, 0, tiled=True)]
    ppermute x1, starting transfers between devices: 4.47 us -> 1.36 us  [far_swap(): return lax.ppermute(value, 'far', [(0, 1), (1, 0)])]
    ppermute x1, waiting for transfers between devices: 0.01 us -> 2.84 us  [far_swap(): return lax.ppermute(value, 'far', [(0, 1), (1, 0)])]
    pallas_call x5 -> x7, Pallas kernels: 9.52 us -> 12.2 us  [the longest x1 2.84 us: local(): call(three_kernel, (BLOCK, TERMS, LAYER, LAYER), [SMEM] + [VMEM] * 9, [WI...]
    ppermute x2, starting transfers between devices: 5.81 us -> 3.17 us  [core_swap(): return lax.ppermute(value, 'core', [(0, 1), (1, 0)])]
    mul x1 -> x0, other arithmetic: 2.27 us -> none  [local(): jnp.where(core[0] == 0, whole_other, whole).astype(F32) * scale]
    all_to_all x1, blocking collectives: 12.8 us -> 13.9 us  [local(): whole = lax.all_to_all(copies, ('near', 'x'), 0, 0, tiled=True)]
  transfers between devices with their start and end apart: 9 -> 9, of which waited for: 3 -> 3; matrix products, arithmetic and copies ran while one was open for 0% -> 0% of each run, Pallas kernels for 5% -> 7%
where the time goes in v5:
time: 72.5 us; the launch traced here: 72.2 us
  blocking collectives  33.2 us (46%)
  Pallas kernels  15.5 us (21%)
  starting transfers between devices  13.3 us (18%)
  waiting for transfers between devices  6 us (8%)
  local copies, waits for them, and re-layouts  3.42 us (5%)
  between operations  0.81 us (1%)
    all_to_all x1, blocking collectives, local(): parts = lax.all_to_all(chunks, ('near', 'x'), 0, 0, tiled=True)  19.3 us
    all_to_all x1, blocking collectives, local(): whole = lax.all_to_all(copies, ('near', 'x'), 0, 0, tiled=True)  13.9 us
    ppermute x3, starting transfers between devices, swap_b(): return lax.ppermute(value, SPACE + ('core',), pairs)  4.72 us
    ppermute x3, starting transfers between devices, swap_a(): return lax.ppermute(value, SPACE, [(i, i ^ 1) for i in range(length)])  4.01 us
    unnamed x16, local copies, waits for them, and re-layouts  3.42 us
    ppermute x2, starting transfers between devices, core_swap(): return lax.ppermute(value, 'core', [(0, 1), (1, 0)])  3.17 us
    ppermute x1, waiting for transfers between devices, far_swap(): return lax.ppermute(value, 'far', [(0, 1), (1, 0)])  2.84 us
    pallas_call x1, Pallas kernels, local(): call(three_kernel, (BLOCK, TERMS, LAYER, LAYER), [SMEM] + [VMEM] * 9, [WI...  2.84 us
  transfers between devices with their start and end apart: 9, of which 3 were waited for; matrix products, arithmetic and copies ran while one was open for 0% of the time, Pallas kernels for 7%

profile of v5, /device:TPU:1, one launch (start us, length us, event | category | flops | bytes accessed | tf_op | source)
XLA Modules:
  0.0 72.2 jit_solution(10946442692253985693)
XLA Ops:
  0.6 0.0 copy-start.7
  0.6 0.0 copy-start.6
  0.7 1.9 %shard_map.111 = (bf16[288,128]{1,0:T(8,128)(2,1)}, bf16[288,128]{1,0:T(8,128)(2,1)}) custom-call(s32[1]{0:T(128)} %bitcast.1.parity, bf16[512,128]{1,0:T(8,128)(2,1)} %bitcast.14, s32[1,512]{1,0:T(1,128)} %bitcast.16, s32[1,27]{1,0:T(1,128)} %bitcast.18), custom_call_target="tpu_custom_call" | custom-call | bytes 4000000 | tf_op jit(solution)/shard_map/pallas_call | solution.py:416
  2.6 2.1 %collective-permute-start = (bf16[288,128]{1,0:T(8,128)(2,1)}, bf16[288,128]{1,0:T(8,128)(2,1)S(1)}, u32[]{:S(2)}, u32[]{:S(2)}) collective-permute-start(bf16[288,128]{1,0:T(8,128)(2,1)} %get-tuple-element.36), channel_id=1, source_target_pairs={{0,4},{4,0},{8,12},{12,8},{16,20},{20,16},{24,28},{28,24},{1,5},{5... | collective-permute-start | bytes 221192 | tf_op jit(solution)/shard_map/ppermute | solution.py:348
  4.7 1.0 %collective-permute-start.1 = (bf16[288,128]{1,0:T(8,128)(2,1)}, bf16[288,128]{1,0:T(8,128)(2,1)S(1)}, u32[]{:S(2)}, u32[]{:S(2)}) collective-permute-start(bf16[288,128]{1,0:T(8,128)(2,1)} %get-tuple-element.37), channel_id=1, source_target_pairs={{0,1},{1,0},{4,8},{5,9},{8,4},{9,5},{12,16},{13,17},{16,12},{17,13... | collective-permute-start | bytes 221192 | tf_op jit(solution)/shard_map/ppermute | solution.py:358
  5.7 0.0 copy-start
  5.7 1.2 %copy-done = bf16[27,128,128]{2,1,0:T(8,128)(2,1)S(1)} copy-done((bf16[27,128,128]{2,1,0:T(8,128)(2,1)S(1)}, bf16[27,128,128]{2,1,0:T(8,128)(2,1)}, u32[]{:S(2)}) %copy-start) | copy-done | bytes 884760
  6.8 0.0 copy-start.2
  6.8 0.9 %copy-done.2 = bf16[1,1,512,128]{3,2,1,0:T(8,128)(2,1)S(1)} copy-done((bf16[1,1,512,128]{3,2,1,0:T(8,128)(2,1)S(1)}, bf16[1,1,512,128]{3,2,1,0:T(8,128)(2,1)}, u32[]{:S(2)}) %copy-start.2) | copy-done | bytes 131096
  7.7 0.0 copy-start.3
  7.7 0.7 copy-done.3
  8.4 0.0 copy-start.4
  8.4 0.7 copy-done.4
  9.1 0.0 copy-start.5
  9.1 0.2 shard_map.110
  9.3 0.0 collective-permute-done.recv_a
  9.3 0.0 collective-permute-done.1.recv_b
  9.3 1.6 %shard_map.112 = (bf16[512,128]{1,0:T(8,128)(2,1)S(1)}, bf16[64,128]{1,0:T(8,128)(2,1)S(1)}, bf16[64,128]{1,0:T(8,128)(2,1)S(1)}, f32[512,128]{1,0:T(8,128)S(1)}) custom-call(s32[1]{0:T(128)} %bitcast.1.parity, f32[27,128]{1,0:T(8,128)S(1)} %get-tuple-element.33.rule, bf16[512,128]{1,0:T(8,128)(2,1)S(1)} %get-tuple-element.34.masked, ...), custom_call_target="tpu_custom_call" | custom-call | flops 452984832 | bytes 4000000 | tf_op jit(solution)/shard_map/pallas_call | solution.py:427
  11.0 0.0 copy-done.7
  11.0 0.0 copy-done.6
  11.0 0.0 copy-done.5
  11.0 2.0 %shard_map.113 = (bf16[640,1152]{1,0:T(8,128)(2,1)S(1)}, bf16[512,128]{1,0:T(8,128)(2,1)S(1)}, f32[8,128]{1,0:T(8,128)S(1)}, bf16[64,128]{1,0:T(8,128)(2,1)S(1)}, bf16[64,128]{1,0:T(8,128)(2,1)S(1)}) custom-call(s32[1]{0:T(128)} %bitcast.1.parity, f32[27,128]{1,0:T(8,128)S(1)} %get-tuple-element.33.rule, bf16[512,128]{1,0:T(8,128)(2,1)S(1)} %get-tuple-element.39.act_one, ...), custom_call_target="tpu_custom_call" | custom-call | flops 452984832 | bytes 4000000 | tf_op jit(solution)/shard_map/pallas_call | solution.py:434
  13.0 1.6 %collective-permute-start.2 = (bf16[64,128]{1,0:T(8,128)(2,1)S(1)}, bf16[64,128]{1,0:T(8,128)(2,1)S(1)}, u32[]{:S(2)}, u32[]{:S(2)}) collective-permute-start(bf16[64,128]{1,0:T(8,128)(2,1)S(1)} %get-tuple-element.43), channel_id=1, source_target_pairs={{0,4},{4,0},{8,12},{12,8},{16,20},{20,16},{24,28},{28,24},{1,5},{5... | collective-permute-start | bytes 49160 | tf_op jit(solution)/shard_map/ppermute | solution.py:348
  14.6 1.5 %collective-permute-start.3 = (bf16[64,128]{1,0:T(8,128)(2,1)S(1)}, bf16[64,128]{1,0:T(8,128)(2,1)S(1)}, u32[]{:S(2)}, u32[]{:S(2)}) collective-permute-start(bf16[64,128]{1,0:T(8,128)(2,1)S(1)} %get-tuple-element.44), channel_id=1, source_target_pairs={{0,1},{1,0},{4,8},{5,9},{8,4},{9,5},{12,16},{13,17},{16,12},{17,13... | collective-permute-start | bytes 49160 | tf_op jit(solution)/shard_map/ppermute | solution.py:358
  16.1 1.5 %shard_map.114 = (bf16[28,128,128]{2,1,0:T(8,128)(2,1)S(1)}, bf16[640,1152]{1,0:T(8,128)(2,1)S(1)}) custom-call(s32[1]{0:T(128)} %bitcast.1.parity, f32[27,128]{1,0:T(8,128)S(1)} %get-tuple-element.33.rule, bf16[512,128]{1,0:T(8,128)(2,1)S(1)} %get-tuple-element.34.masked, bf16[288,128]{1,0:T(8,128)(2,1)S(1)} %collective-permute-done.recv_a, ...), custom_call_target="tpu_custom_call" | custom-call | flops 452984832 | bytes 4000000 | tf_op jit(solution)/shard_map/pallas_call | solution.py:441
  17.6 0.0 collective-permute-done.2.recv_a
  17.6 0.0 collective-permute-done.3.recv_b
  17.6 2.8 %shard_map.115 = (bf16[512,128]{1,0:T(8,128)(2,1)S(1)}, bf16[28,128,128]{2,1,0:T(8,128)(2,1)S(1)}, bf16[64,128]{1,0:T(8,128)(2,1)S(1)}, bf16[64,128]{1,0:T(8,128)(2,1)S(1)}) custom-call(s32[1]{0:T(128)} %bitcast.1.parity, f32[27,128]{1,0:T(8,128)S(1)} %get-tuple-element.33.rule, bf16[512,128]{1,0:T(8,128)(2,1)S(1)} %get-tuple-element.42.grad.grad_two, ...), custom_call_target="tpu_custom_call" | custom-call | flops 905969664 | bytes 4000000 | tf_op jit(solution)/shard_map/pallas_call | solution.py:444
  20.5 0.1 broadcast_select_fusion
  20.6 0.2 collective-permute-start.4
  20.8 2.3 %collective-permute-done.4.other = bf16[28,128,128]{2,1,0:T(8,128)(2,1)S(1)} collective-permute-done((bf16[28,128,128]{2,1,0:T(8,128)(2,1)S(1)}, bf16[28,128,128]{2,1,0:T(8,128)(2,1)S(1)}, u32[]{:S(2)}, u32[]{:S(2)}) %collective-permute-start.4) | collective-permute-done | bytes 917536 | tf_op jit(solution)/shard_map/ppermute | solution.py:366
  23.1 0.3 shard_map.116
  23.4 19.3 %all_to_all.10.parts = bf16[8,448,128]{2,1,0:T(8,128)(2,1)S(1)} all-to-all(bf16[8,448,128]{2,1,0:T(8,128)(2,1)S(1)} %shard_map.116), channel_id=1, replica_groups=mesh['far'=2,'near'=4,'x'=2,'core'=2] {'near','x'}, dimensions={0} | all-to-all | bytes 1835008 | tf_op jit(solution)/shard_map/all_to_all | solution.py:460
  42.7 0.1 shard_map.117.mine
  42.8 1.4 %collective-permute-start.5 = (bf16[448,128]{1,0:T(8,128)(2,1)S(1)}, bf16[448,128]{1,0:T(8,128)(2,1)S(1)}, u32[]{:S(2)}, u32[]{:S(2)}) collective-permute-start(bf16[448,128]{1,0:T(8,128)(2,1)S(1)} %shard_map.117.mine), channel_id=1, source_target_pairs={{0,16},{16,0},{1,17},{17,1},{2,18},{18,2},{3,19},{19,3},{4,20},{20... | collective-permute-start | bytes 344072 | tf_op jit(solution)/shard_map/ppermute | solution.py:362
  44.2 0.3 collective-permute-start.6
  44.5 2.3 %collective-permute-start.7 = (bf16[64,128]{1,0:T(8,128)(2,1)S(1)}, bf16[64,128]{1,0:T(8,128)(2,1)S(1)}, u32[]{:S(2)}, u32[]{:S(2)}) collective-permute-start(bf16[64,128]{1,0:T(8,128)(2,1)S(1)} %get-tuple-element.52), channel_id=1, source_target_pairs={{0,1},{1,0},{4,8},{5,9},{8,4},{9,5},{12,16},{13,17},{16,12},{17,13... | collective-permute-start | bytes 49160 | tf_op jit(solution)/shard_map/ppermute | solution.py:358
  46.7 0.0 collective-permute-done.6.later_a.recv_a
  46.8 0.8 %collective-permute-done.7.later_b.recv_b = bf16[64,128]{1,0:T(8,128)(2,1)S(1)} collective-permute-done((bf16[64,128]{1,0:T(8,128)(2,1)S(1)}, bf16[64,128]{1,0:T(8,128)(2,1)S(1)}, u32[]{:S(2)}, u32[]{:S(2)}) %collective-permute-start.7) | collective-permute-done | bytes 16416 | tf_op jit(solution)/shard_map/ppermute | solution.py:358
  47.6 2.8 %collective-permute-done.5.other = bf16[448,128]{1,0:T(8,128)(2,1)S(1)} collective-permute-done((bf16[448,128]{1,0:T(8,128)(2,1)S(1)}, bf16[448,128]{1,0:T(8,128)(2,1)S(1)}, u32[]{:S(2)}, u32[]{:S(2)}) %collective-permute-start.5) | collective-permute-done | bytes 114720 | tf_op jit(solution)/shard_map/ppermute | solution.py:362
  50.4 0.6 shard_map.118
  51.0 13.9 %all_to_all.11 = bf16[8,432,128]{2,1,0:T(8,128)(2,1)S(1)} all-to-all(bf16[8,432,128]{2,1,0:T(8,128)(2,1)S(1)} %get-tuple-element.53), channel_id=1, replica_groups=mesh['far'=2,'near'=4,'x'=2,'core'=2] {'near','x'}, dimensions={0} | all-to-all | bytes 1769472 | tf_op jit(solution)/shard_map/all_to_all | solution.py:469
  64.9 2.9 %collective-permute-start.8 = (bf16[27,128,128]{2,1,0:T(8,128)(2,1)S(1)}, bf16[27,128,128]{2,1,0:T(8,128)(2,1)S(1)}, u32[]{:S(2)}, u32[]{:S(2)}) collective-permute-start(bf16[27,128,128]{2,1,0:T(8,128)(2,1)S(1)} %bitcast.12), channel_id=1, source_target_pairs={{0,1},{1,0},{2,3},{3,2},{4,5},{5,4},{6,7},{7,6},{8,9},{9,8},{10,11... | collective-permute-start | bytes 2654216 | tf_op jit(solution)/shard_map/ppermute | solution.py:366
  67.9 0.0 copy-done.1
  67.9 1.8 %shard_map.121 = bf16[512,128]{1,0:T(8,128)(2,1)} custom-call(s32[1]{0:T(128)} %bitcast.1.parity, f32[27,128]{1,0:T(8,128)S(1)} %get-tuple-element.33.rule, bf16[512,128]{1,0:T(8,128)(2,1)S(1)} %get-tuple-element.60.grad_one, bf16[64,128]{1,0:T(8,128)(2,1)S(1)} %collective-permute-done.6.later_a.recv_a, ...), custom_call_target="tpu_custom_call" | custom-call | flops 452984832 | bytes 4000000 | tf_op jit(solution)/shard_map/pallas_call | solution.py:472
  69.7 1.3 %shard_map.119 = (f32[27,128,128]{2,1,0:T(8,128)}, f32[27,128,128]{2,1,0:T(8,128)}) custom-call(s32[1]{0:T(128)} %bitcast.core, bf16[27,128,128]{2,1,0:T(8,128)(2,1)S(1)} %bitcast.13), custom_call_target="tpu_custom_call" | custom-call | bytes 4000000 | tf_op jit(solution)/shard_map/pallas_call | solution.py:477
  71.0 0.0 collective-permute-done.8.whole
  71.0 1.3 %shard_map.120 = (f32[27,128,128]{2,1,0:T(8,128)}, f32[27,128,128]{2,1,0:T(8,128)}) custom-call(s32[1]{0:T(128)S(6)} %sub.3.core, bf16[27,128,128]{2,1,0:T(8,128)(2,1)S(1)} %collective-permute-done.8.whole, f32[27,128,128]{2,1,0:T(8,128)} %get-tuple-element.54.one_in, ...), custom_call_target="tpu_custom_call", output_to_operand_aliasing={{0}: (2, {}), {1}: (3, {})} | custom-call | bytes 4000000 | tf_op jit(solution)/shard_map/pallas_call | solution.py:478
  (1 shorter events, 0.0 us)
Async XLA Ops:
  0.6 10.3 %copy-start.7 = (bf16[128,3]{0,1:T(4,128)(2,1)S(1)}, bf16[128,3]{0,1:T(4,128)(2,1)}, u32[]{:S(2)}) copy-start(bf16[128,3]{0,1:T(4,128)(2,1)} %param.13) | copy-start | bytes 2308
  0.6 10.3 %copy-start.6 = (s32[1,1,512]{2,1,0:T(1,128)S(1)}, s32[1,1,512]{2,1,0:T(1,128)}, u32[]{:S(2)}) copy-start(s32[1,1,512]{2,1,0:T(1,128)} %param.9) | copy-start | bytes 6148
  2.6 6.7 %collective-permute-start = (bf16[288,128]{1,0:T(8,128)(2,1)}, bf16[288,128]{1,0:T(8,128)(2,1)S(1)}, u32[]{:S(2)}, u32[]{:S(2)}) collective-permute-start(bf16[288,128]{1,0:T(8,128)(2,1)} %get-tuple-element.36), channel_id=1, source_target_pairs={{0,4},{4,0},{8,12},{12,8},{16,20},{20,16},{24,28},{28,24},{1,5},{5... | collective-permute-start | bytes 221192 | tf_op jit(solution)/shard_map/ppermute | solution.py:348
  4.7 4.6 %collective-permute-start.1 = (bf16[288,128]{1,0:T(8,128)(2,1)}, bf16[288,128]{1,0:T(8,128)(2,1)S(1)}, u32[]{:S(2)}, u32[]{:S(2)}) collective-permute-start(bf16[288,128]{1,0:T(8,128)(2,1)} %get-tuple-element.37), channel_id=1, source_target_pairs={{0,1},{1,0},{4,8},{5,9},{8,4},{9,5},{12,16},{13,17},{16,12},{17,13... | collective-permute-start | bytes 221192 | tf_op jit(solution)/shard_map/ppermute | solution.py:358
  5.7 1.2 %copy-start = (bf16[27,128,128]{2,1,0:T(8,128)(2,1)S(1)}, bf16[27,128,128]{2,1,0:T(8,128)(2,1)}, u32[]{:S(2)}) copy-start(bf16[27,128,128]{2,1,0:T(8,128)(2,1)} %filt.5) | copy-start | bytes 2654212
  6.8 0.9 %copy-start.2 = (bf16[1,1,512,128]{3,2,1,0:T(8,128)(2,1)S(1)}, bf16[1,1,512,128]{3,2,1,0:T(8,128)(2,1)}, u32[]{:S(2)}) copy-start(bf16[1,1,512,128]{3,2,1,0:T(8,128)(2,1)} %param.7) | copy-start | bytes 393220
  7.7 0.7 copy-start.3
  8.4 0.7 copy-start.4
  9.1 1.9 %copy-start.5 = (bf16[27,128,128]{2,1,0:T(8,128)(2,1)S(1)}, bf16[27,128,128]{2,1,0:T(8,128)(2,1)}, u32[]{:S(2)}) copy-start(bf16[27,128,128]{2,1,0:T(8,128)(2,1)} %filt.4) | copy-start | bytes 2654212
  13.0 4.6 %collective-permute-start.2 = (bf16[64,128]{1,0:T(8,128)(2,1)S(1)}, bf16[64,128]{1,0:T(8,128)(2,1)S(1)}, u32[]{:S(2)}, u32[]{:S(2)}) collective-permute-start(bf16[64,128]{1,0:T(8,128)(2,1)S(1)} %get-tuple-element.43), channel_id=1, source_target_pairs={{0,4},{4,0},{8,12},{12,8},{16,20},{20,16},{24,28},{28,24},{1,5},{5... | collective-permute-start | bytes 49160 | tf_op jit(solution)/shard_map/ppermute | solution.py:348
  14.6 3.0 %collective-permute-start.3 = (bf16[64,128]{1,0:T(8,128)(2,1)S(1)}, bf16[64,128]{1,0:T(8,128)(2,1)S(1)}, u32[]{:S(2)}, u32[]{:S(2)}) collective-permute-start(bf16[64,128]{1,0:T(8,128)(2,1)S(1)} %get-tuple-element.44), channel_id=1, source_target_pairs={{0,1},{1,0},{4,8},{5,9},{8,4},{9,5},{12,16},{13,17},{16,12},{17,13... | collective-permute-start | bytes 49160 | tf_op jit(solution)/shard_map/ppermute | solution.py:358
  20.6 2.5 %collective-permute-start.4 = (bf16[28,128,128]{2,1,0:T(8,128)(2,1)S(1)}, bf16[28,128,128]{2,1,0:T(8,128)(2,1)S(1)}, u32[]{:S(2)}, u32[]{:S(2)}) collective-permute-start(bf16[28,128,128]{2,1,0:T(8,128)(2,1)S(1)} %broadcast_select_fusion), channel_id=1, source_target_pairs={{0,1},{1,0},{2,3},{3,2},{4,5},{5,4},{6,7},{7,6},{8,9},{9,8},{10,11... | collective-permute-start | bytes 2752520 | tf_op jit(solution)/shard_map/ppermute | solution.py:366
  42.7 25.2 %copy-start.1 = (bf16[27,128,128]{2,1,0:T(8,128)(2,1)S(1)}, bf16[27,128,128]{2,1,0:T(8,128)(2,1)}, u32[]{:S(2)}) copy-start(bf16[27,128,128]{2,1,0:T(8,128)(2,1)} %filt.5) | copy-start | bytes 2654212
  42.8 7.6 %collective-permute-start.5 = (bf16[448,128]{1,0:T(8,128)(2,1)S(1)}, bf16[448,128]{1,0:T(8,128)(2,1)S(1)}, u32[]{:S(2)}, u32[]{:S(2)}) collective-permute-start(bf16[448,128]{1,0:T(8,128)(2,1)S(1)} %shard_map.117.mine), channel_id=1, source_target_pairs={{0,16},{16,0},{1,17},{17,1},{2,18},{18,2},{3,19},{19,3},{4,20},{20... | collective-permute-start | bytes 344072 | tf_op jit(solution)/shard_map/ppermute | solution.py:362
  44.2 2.6 %collective-permute-start.6 = (bf16[64,128]{1,0:T(8,128)(2,1)S(1)}, bf16[64,128]{1,0:T(8,128)(2,1)S(1)}, u32[]{:S(2)}, u32[]{:S(2)}) collective-permute-start(bf16[64,128]{1,0:T(8,128)(2,1)S(1)} %get-tuple-element.51), channel_id=1, source_target_pairs={{0,4},{4,0},{8,12},{12,8},{16,20},{20,16},{24,28},{28,24},{1,5},{5... | collective-permute-start | bytes 49160 | tf_op jit(solution)/shard_map/ppermute | solution.py:348
  44.5 3.1 %collective-permute-start.7 = (bf16[64,128]{1,0:T(8,128)(2,1)S(1)}, bf16[64,128]{1,0:T(8,128)(2,1)S(1)}, u32[]{:S(2)}, u32[]{:S(2)}) collective-permute-start(bf16[64,128]{1,0:T(8,128)(2,1)S(1)} %get-tuple-element.52), channel_id=1, source_target_pairs={{0,1},{1,0},{4,8},{5,9},{8,4},{9,5},{12,16},{13,17},{16,12},{17,13... | collective-permute-start | bytes 49160 | tf_op jit(solution)/shard_map/ppermute | solution.py:358
  64.9 6.0 %collective-permute-start.8 = (bf16[27,128,128]{2,1,0:T(8,128)(2,1)S(1)}, bf16[27,128,128]{2,1,0:T(8,128)(2,1)S(1)}, u32[]{:S(2)}, u32[]{:S(2)}) collective-permute-start(bf16[27,128,128]{2,1,0:T(8,128)(2,1)S(1)} %bitcast.12), channel_id=1, source_target_pairs={{0,1},{1,0},{2,3},{3,2},{4,5},{5,4},{6,7},{7,6},{8,9},{9,8},{10,11... | collective-permute-start | bytes 2654216 | tf_op jit(solution)/shard_map/ppermute | solution.py:366

commit v6 on v5

--- a/solution.py
+++ b/solution.py
@@ -156,16 +156,20 @@
     return total
 
 
-def filter_terms(win_ref, grad, small_ref, wide_ref, out_ref):
-    pair = split_pair(small_ref[: SMALL // 2])
-    out_ref[27] = jnp.concatenate([pair, jnp.zeros((LANES - SMALL, LANES), F32)], axis=0).astype(BF16)
+def filter_terms(win_ref, grad, core_ref, wide_ref, tiles_ref, mine_ref, away_ref):
     wide_ref[...] = jnp.zeros_like(wide_ref)
     for i in range(3):
         wide_ref[64 * i : 64 * i + VOX, LANES * i : LANES * (i + 1)] = grad
     for t in range(TAPS):
         term = contract(win_ref[:, LANES * t : LANES * (t + 1)], wide_ref[...], 0, 0)
         for i in range(3):
-            out_ref[TAPS * i + t] = term[:, LANES * i : LANES * (i + 1)].astype(BF16)
+            tile = term[:, LANES * i : LANES * (i + 1)].astype(BF16)
+            at = 2 * (TAPS * i + t)
+            tiles_ref[at // 27, at % 27] = tile[:64]
+            tiles_ref[(at + 1) // 27, (at + 1) % 27] = tile[64:]
+    core = core_ref[0]
+    mine_ref[:27] = tiles_ref[core]
+    away_ref[:27] = tiles_ref[1 - core]
 
 
 def silu_parts(pre):
@@ -276,15 +280,19 @@
     small[...] = values
 
 
-def terms_kernel(parity, rule, masked, recv_a, recv_b, win_two, grad, small, out, win_one, wide):
-    filter_terms(win_two, grad[...], small, wide, out)
+def terms_kernel(
+    core, parity, rule, masked, recv_a, recv_b, win_two, grad, small, mine, away, win_one, wide, tiles
+):
+    filter_terms(win_two, grad[...], core, wide, tiles, mine, away)
+    pair = jnp.concatenate([split_pair(small[: SMALL // 2]), jnp.zeros((64 - SMALL, LANES), F32)], axis=0).astype(BF16)
+    mine[27], away[27] = pair, pair
     below, above = from_sides(parity, recv_a[...], recv_b[...])
     build_windows(masked[...].astype(F32), below[:64], above[:64], rule, win_one)
 
 
 def three_kernel(
-    parity, rule, grad_two, recv_a, recv_b, filt, mask, pre, win_one, small,
-    grad_one, terms, send_a, send_b, win, wide,
+    core, parity, rule, grad_two, recv_a, recv_b, filt, mask, pre, win_one,
+    grad_one, mine, away, send_a, send_b, win, wide, tiles,
 ):
     below, above = from_sides(parity, recv_a[...], recv_b[...])
     build_windows(grad_two[...].astype(F32), below, above, rule, win)
@@ -292,7 +300,7 @@
     out = (backward_sum(win, filt) * slope * mask[...]).astype(BF16)
     grad_one[...] = out
     put_layers(out.astype(F32), parity, send_a, send_b)
-    filter_terms(win_one, out, small, wide, terms)
+    filter_terms(win_one, out, core, wide, tiles, mine, away)
 
 
 def four_kernel(parity, rule, grad_one, recv_a, recv_b, filt, mask, out, win):
@@ -303,14 +311,15 @@
 
 
 def own_kernel(core, whole, one, two, wide, sems):
-    for part in range(3):
-        at = pl.ds(TAPS * part, TAPS)
-        wide[at] = whole[at].astype(F32) * (1.0 / VOX)
-        for wanted, out in ((0, one), (1, two)):
-            pl.when(core[0] == wanted)(pltpu.make_async_copy(wide.at[at], out.at[at], sems.at[part]).start)
-    for part in range(3):
-        at = pl.ds(TAPS * part, TAPS)
-        pltpu.make_async_copy(wide.at[at], one.at[at], sems.at[part]).wait()
+    copies = []
+    for layer, out in enumerate((one, two)):
+        for part in range(3):
+            at = pl.ds(TAPS * part, TAPS)
+            wide[layer, at] = whole[layer, at].astype(F32) * (1.0 / VOX)
+            copies.append(pltpu.make_async_copy(wide.at[layer, at], out.at[core[0], at], sems.at[3 * layer + part]))
+            copies[-1].start()
+    for copy in copies:
+        copy.wait()
 
 
 def other_kernel(core, whole, one_in, two_in, one, two, wide, sems):
@@ -336,7 +345,9 @@
 FILTER = sds((27, LANES, LANES), BF16)
 SIDE = sds((288, LANES), BF16)
 WINDOWS = sds((640, TAPS * LANES), BF16)
-TERMS = sds((28, LANES, LANES), BF16)
+TERMS = sds((27, 64, LANES), BF16)
+GIVEN = sds((28, 64, LANES), BF16)
+TILES_SCRATCH = pltpu.VMEM((2, 27, 64, LANES), BF16)
 WIN_SCRATCH = pltpu.VMEM((640, TAPS * LANES), BF16)
 SEM = pltpu.SemaphoreType.DMA
 WIDE_SCRATCH = pltpu.VMEM((640, 3 * LANES), BF16)
@@ -375,11 +386,14 @@
     return pair[: SMALL // 2] + pair[SMALL // 2 : SMALL]
 
 
-def pair_kernel(rows, peers, core, one, two, other, out):
-    small = join_pair(one[27].astype(F32)) + join_pair(other[27].astype(F32))
+def pair_kernel(rows, peers, one, one_other, two, two_other, out):
+    small = join_pair(two[27].astype(F32)) + join_pair(two_other[27].astype(F32))
     tail = jnp.concatenate([split_pair(small), jnp.zeros((SMALL, LANES), F32)], axis=0)
-    mine = jnp.where(core[0] == 0, one[:27], two[:27])
-    total = mine.reshape(27 * LANES, LANES).astype(F32) + other[:27].reshape(27 * LANES, LANES).astype(F32)
+    halves = [
+        a[:27].reshape(27 * 64, LANES).astype(F32) + b[:27].reshape(27 * 64, LANES).astype(F32)
+        for a, b in ((one, one_other), (two, two_other))
+    ]
+    total = jnp.concatenate(halves, axis=0)
     spare = rows * peers - 27 * LANES
     if spare:
         total = jnp.concatenate([total, jnp.zeros((spare, LANES), F32)], axis=0)
@@ -438,25 +452,23 @@
         flops=CONV,
     )(parity, rule, act_one, act_below, act_above, filter_two, mask, labels.reshape(1, VOX), head_weight.T)
     e, f = swap_a(e), swap_b(f)
-    terms_two, win_one = call(terms_kernel, (TERMS, WINDOWS), [SMEM] + [VMEM] * 7, [WIDE_SCRATCH], CONV)(
-        parity, rule, masked, a, b, win_two, grad_two, small
-    )
-    grad_one, terms_one, g, h = call(
+    mine_two, away_two, win_one = call(
+        terms_kernel, (GIVEN, GIVEN, WINDOWS), [SMEM] * 2 + [VMEM] * 7, [WIDE_SCRATCH, TILES_SCRATCH], CONV
+    )(core, parity, rule, masked, a, b, win_two, grad_two, small)
+    other_two = core_swap(away_two)
+    grad_one, mine_one, away_one, g, h = call(
         three_kernel,
-        (BLOCK, TERMS, LAYER, LAYER),
-        [SMEM] + [VMEM] * 9,
-        [WIN_SCRATCH, WIDE_SCRATCH],
+        (BLOCK, TERMS, TERMS, LAYER, LAYER),
+        [SMEM] * 2 + [VMEM] * 8,
+        [WIN_SCRATCH, WIDE_SCRATCH, TILES_SCRATCH],
         2 * CONV,
-    )(parity, rule, grad_two, e, f, filter_two, mask, pre_one, win_one, small)
+    )(core, parity, rule, grad_two, e, f, filter_two, mask, pre_one, win_one)
     g, h = swap_a(g), swap_b(h)
     peers = lax.axis_size("near") * lax.axis_size("x")
     rows = -(-27 * LANES // (peers * 16)) * 16
-    away = jnp.where(core[0] == 0, terms_two, terms_one)
     chunks = call(
-        functools.partial(pair_kernel, rows, peers),
-        sds((peers, rows + 2 * SMALL, LANES), BF16),
-        [SMEM] + [VMEM] * 3,
-    )(core, terms_one, terms_two, core_swap(away))
+        functools.partial(pair_kernel, rows, peers), sds((peers, rows + 2 * SMALL, LANES), BF16), [VMEM] * 4
+    )(mine_one, core_swap(away_one), mine_two, other_two)
     parts = lax.all_to_all(chunks, ("near", "x"), 0, 0, tiled=True)
     part = call(
         functools.partial(half_kernel, rows, peers), sds((rows + 2 * SMALL, LANES), BF16), [VMEM]
@@ -467,20 +479,20 @@
         [VMEM, VMEM, ANY, ANY],
     )(part, far_swap(part), g, h)
     whole = lax.all_to_all(copies, ("near", "x"), 0, 0, tiled=True)
-    whole = whole.reshape(peers * rows, LANES)[: 27 * LANES].reshape(27, LANES, LANES)
+    whole = whole.reshape(peers * rows, LANES)[: 27 * LANES].reshape(2, 27, 64, LANES)
     whole_other = core_swap(whole)
     grad_in = call(four_kernel, BLOCK, [SMEM] + [VMEM] * 6, [WIN_SCRATCH], CONV)(
         parity, rule, grad_one, g, h, filter_one, mask
     )
-    wide = sds((27, LANES, LANES), F32)
-    room = [pltpu.VMEM((27, LANES, LANES), F32), SEM((3,))]
+    wide = sds((2, 27, 64, LANES), F32)
+    room = [pltpu.VMEM((2, 27, 64, LANES), F32), SEM((6,))]
     parts = call(own_kernel, (wide, wide), [SMEM, VMEM], room, out_specs=(ANY, ANY))(core, whole)
     sum_one, sum_two = call(
         other_kernel, (wide, wide), [SMEM, VMEM, ANY, ANY], room, out_specs=(ANY, ANY), alias={2: 0, 3: 1}
     )(1 - core, whole_other, *parts)
     return (
-        sum_one,
-        sum_two,
+        sum_one.reshape(27, LANES, LANES),
+        sum_two.reshape(27, LANES, LANES),
         head_sum.T,
         loss[0, 0],
         grad_in.reshape(features.shape),

time: 72.5 us -> 71.7 us (0.989)
  waiting for transfers between devices: 6 us -> 5.12 us
    ppermute x2 -> x3, waiting for transfers between devices: 2.31 us -> 1.43 us  [core_swap(): return lax.ppermute(value, 'core', [(0, 1), (1, 0)])]
    ppermute x2 -> x3, starting transfers between devices: 3.17 us -> 3.56 us  [core_swap(): return lax.ppermute(value, 'core', [(0, 1), (1, 0)])]
  transfers between devices with their start and end apart: 9 -> 10, of which waited for: 3 -> 3; matrix products, arithmetic and copies ran while one was open for 0% -> 0% of each run, Pallas kernels for 7% -> 11%
where the time goes in v6:
time: 71.7 us; the launch traced here: 71.4 us
  blocking collectives  32.9 us (46%)
  Pallas kernels  15.5 us (22%)
  starting transfers between devices  13.7 us (19%)
  waiting for transfers between devices  5.12 us (7%)
  local copies, waits for them, and re-layouts  3.42 us (5%)
  between operations  0.81 us (1%)
    all_to_all x1, blocking collectives, local(): parts = lax.all_to_all(chunks, ('near', 'x'), 0, 0, tiled=True)  19 us
    all_to_all x1, blocking collectives, local(): whole = lax.all_to_all(copies, ('near', 'x'), 0, 0, tiled=True)  13.9 us
    ppermute x3, starting transfers between devices, swap_b(): return lax.ppermute(value, SPACE + ('core',), pairs)  4.73 us
    ppermute x3, starting transfers between devices, swap_a(): return lax.ppermute(value, SPACE, [(i, i ^ 1) for i in range(length)])  4.01 us
    ppermute x3, starting transfers between devices, core_swap(): return lax.ppermute(value, 'core', [(0, 1), (1, 0)])  3.56 us
    unnamed x16, local copies, waits for them, and re-layouts  3.42 us
    pallas_call x1, Pallas kernels, local(): call(three_kernel, (BLOCK, TERMS, TERMS, LAYER, LAYER), [SMEM] * 2 + [VME...  2.88 us
    ppermute x1, waiting for transfers between devices, far_swap(): return lax.ppermute(value, 'far', [(0, 1), (1, 0)])  2.84 us
  transfers between devices with their start and end apart: 10, of which 3 were waited for; matrix products, arithmetic and copies ran while one was open for 0% of the time, Pallas kernels for 11%

profile of v6, /device:TPU:1, one launch (start us, length us, event | category | flops | bytes accessed | tf_op | source)
XLA Modules:
  0.0 71.4 jit_solution(8323250988050030404)
XLA Ops:
  0.6 0.0 copy-start.7
  0.6 0.0 copy-start.6
  0.7 1.9 %shard_map.111 = (bf16[288,128]{1,0:T(8,128)(2,1)}, bf16[288,128]{1,0:T(8,128)(2,1)}) custom-call(s32[1]{0:T(128)} %bitcast.1.parity, bf16[512,128]{1,0:T(8,128)(2,1)} %bitcast.16, s32[1,512]{1,0:T(1,128)} %bitcast.18, s32[1,27]{1,0:T(1,128)} %bitcast.20), custom_call_target="tpu_custom_call" | custom-call | bytes 4000000 | tf_op jit(solution)/shard_map/pallas_call | solution.py:430
  2.6 2.1 %collective-permute-start = (bf16[288,128]{1,0:T(8,128)(2,1)}, bf16[288,128]{1,0:T(8,128)(2,1)S(1)}, u32[]{:S(2)}, u32[]{:S(2)}) collective-permute-start(bf16[288,128]{1,0:T(8,128)(2,1)} %get-tuple-element.38), channel_id=1, source_target_pairs={{0,4},{4,0},{8,12},{12,8},{16,20},{20,16},{24,28},{28,24},{1,5},{5... | collective-permute-start | bytes 221192 | tf_op jit(solution)/shard_map/ppermute | solution.py:359
  4.7 1.0 %collective-permute-start.1 = (bf16[288,128]{1,0:T(8,128)(2,1)}, bf16[288,128]{1,0:T(8,128)(2,1)S(1)}, u32[]{:S(2)}, u32[]{:S(2)}) collective-permute-start(bf16[288,128]{1,0:T(8,128)(2,1)} %get-tuple-element.39), channel_id=1, source_target_pairs={{0,1},{1,0},{4,8},{5,9},{8,4},{9,5},{12,16},{13,17},{16,12},{17,13... | collective-permute-start | bytes 221192 | tf_op jit(solution)/shard_map/ppermute | solution.py:369
  5.7 0.0 copy-start
  5.7 1.2 %copy-done = bf16[27,128,128]{2,1,0:T(8,128)(2,1)S(1)} copy-done((bf16[27,128,128]{2,1,0:T(8,128)(2,1)S(1)}, bf16[27,128,128]{2,1,0:T(8,128)(2,1)}, u32[]{:S(2)}) %copy-start) | copy-done | bytes 884760
  6.8 0.0 copy-start.2
  6.8 0.9 %copy-done.2 = bf16[1,1,512,128]{3,2,1,0:T(8,128)(2,1)S(1)} copy-done((bf16[1,1,512,128]{3,2,1,0:T(8,128)(2,1)S(1)}, bf16[1,1,512,128]{3,2,1,0:T(8,128)(2,1)}, u32[]{:S(2)}) %copy-start.2) | copy-done | bytes 131096
  7.7 0.0 copy-start.3
  7.7 0.7 copy-done.3
  8.4 0.7 copy-done.4
  9.1 0.0 copy-start.5
  9.1 0.2 shard_map.110
  9.3 0.0 collective-permute-done.recv_a
  9.3 0.0 collective-permute-done.1.recv_b
  9.3 1.6 %shard_map.112 = (bf16[512,128]{1,0:T(8,128)(2,1)S(1)}, bf16[64,128]{1,0:T(8,128)(2,1)S(1)}, bf16[64,128]{1,0:T(8,128)(2,1)S(1)}, f32[512,128]{1,0:T(8,128)S(1)}) custom-call(s32[1]{0:T(128)} %bitcast.1.parity, f32[27,128]{1,0:T(8,128)S(1)} %get-tuple-element.35.rule, bf16[512,128]{1,0:T(8,128)(2,1)S(1)} %get-tuple-element.36.masked, ...), custom_call_target="tpu_custom_call" | custom-call | flops 452984832 | bytes 4000000 | tf_op jit(solution)/shard_map/pallas_call | solution.py:441
  10.9 0.0 copy-done.7
  11.0 0.0 copy-done.6
  11.0 0.0 copy-done.5
  11.0 2.0 %shard_map.113 = (bf16[640,1152]{1,0:T(8,128)(2,1)S(1)}, bf16[512,128]{1,0:T(8,128)(2,1)S(1)}, f32[8,128]{1,0:T(8,128)S(1)}, bf16[64,128]{1,0:T(8,128)(2,1)S(1)}, bf16[64,128]{1,0:T(8,128)(2,1)S(1)}) custom-call(s32[1]{0:T(128)} %bitcast.1.parity, f32[27,128]{1,0:T(8,128)S(1)} %get-tuple-element.35.rule, bf16[512,128]{1,0:T(8,128)(2,1)S(1)} %get-tuple-element.41.act_one, ...), custom_call_target="tpu_custom_call" | custom-call | flops 452984832 | bytes 4000000 | tf_op jit(solution)/shard_map/pallas_call | solution.py:448
  13.0 1.6 %collective-permute-start.2 = (bf16[64,128]{1,0:T(8,128)(2,1)S(1)}, bf16[64,128]{1,0:T(8,128)(2,1)S(1)}, u32[]{:S(2)}, u32[]{:S(2)}) collective-permute-start(bf16[64,128]{1,0:T(8,128)(2,1)S(1)} %get-tuple-element.45), channel_id=1, source_target_pairs={{0,4},{4,0},{8,12},{12,8},{16,20},{20,16},{24,28},{28,24},{1,5},{5... | collective-permute-start | bytes 49160 | tf_op jit(solution)/shard_map/ppermute | solution.py:359
  14.5 1.5 %collective-permute-start.3 = (bf16[64,128]{1,0:T(8,128)(2,1)S(1)}, bf16[64,128]{1,0:T(8,128)(2,1)S(1)}, u32[]{:S(2)}, u32[]{:S(2)}) collective-permute-start(bf16[64,128]{1,0:T(8,128)(2,1)S(1)} %get-tuple-element.46), channel_id=1, source_target_pairs={{0,1},{1,0},{4,8},{5,9},{8,4},{9,5},{12,16},{13,17},{16,12},{17,13... | collective-permute-start | bytes 49160 | tf_op jit(solution)/shard_map/ppermute | solution.py:369
  16.1 1.6 %shard_map.114 = (bf16[28,64,128]{2,1,0:T(8,128)(2,1)S(1)}, bf16[28,64,128]{2,1,0:T(8,128)(2,1)S(1)}, bf16[640,1152]{1,0:T(8,128)(2,1)S(1)}) custom-call(s32[1]{0:T(128)} %bitcast.core, s32[1]{0:T(128)} %bitcast.1.parity, f32[27,128]{1,0:T(8,128)S(1)} %get-tuple-element.35.rule, bf16[512,128]{1,0:T(8,128)(2,1)S(1)} %get-tuple-element.36.masked, ...), custom_call_target="tpu_custom_call" | custom-call | flops 452984832 | bytes 4000000 | tf_op jit(solution)/shard_map/pallas_call | solution.py:455
  17.7 0.1 collective-permute-start.5
  17.8 0.0 collective-permute-done.2.recv_a
  17.8 0.0 collective-permute-done.3.recv_b
  17.8 2.9 %shard_map.115 = (bf16[512,128]{1,0:T(8,128)(2,1)S(1)}, bf16[27,64,128]{2,1,0:T(8,128)(2,1)S(1)}, bf16[27,64,128]{2,1,0:T(8,128)(2,1)S(1)}, bf16[64,128]{1,0:T(8,128)(2,1)S(1)}, bf16[64,128]{1,0:T(8,128)(2,1)S(1)}) custom-call(s32[1]{0:T(128)} %bitcast.core, s32[1]{0:T(128)} %bitcast.1.parity, f32[27,128]{1,0:T(8,128)S(1)} %get-tuple-element.35.rule, ...), custom_call_target="tpu_custom_call" | custom-call | flops 905969664 | bytes 4000000 | tf_op jit(solution)/shard_map/pallas_call | solution.py:459
  20.7 0.5 collective-permute-start.4
  21.2 1.4 %collective-permute-done.4.one_other = bf16[27,64,128]{2,1,0:T(8,128)(2,1)S(1)} collective-permute-done((bf16[27,64,128]{2,1,0:T(8,128)(2,1)S(1)}, bf16[27,64,128]{2,1,0:T(8,128)(2,1)S(1)}, u32[]{:S(2)}, u32[]{:S(2)}) %collective-permute-start.4) | collective-permute-done | bytes 442400 | tf_op jit(solution)/shard_map/ppermute | solution.py:377
  22.7 0.0 collective-permute-done.5.two_other
  22.7 0.2 shard_map.116
  22.9 19.0 %all_to_all.10.parts = bf16[8,448,128]{2,1,0:T(8,128)(2,1)S(1)} all-to-all(bf16[8,448,128]{2,1,0:T(8,128)(2,1)S(1)} %shard_map.116), channel_id=1, replica_groups=mesh['far'=2,'near'=4,'x'=2,'core'=2] {'near','x'}, dimensions={0} | all-to-all | bytes 1835008 | tf_op jit(solution)/shard_map/all_to_all | solution.py:472
  41.9 0.1 shard_map.117.mine
  42.0 1.4 %collective-permute-start.6 = (bf16[448,128]{1,0:T(8,128)(2,1)S(1)}, bf16[448,128]{1,0:T(8,128)(2,1)S(1)}, u32[]{:S(2)}, u32[]{:S(2)}) collective-permute-start(bf16[448,128]{1,0:T(8,128)(2,1)S(1)} %shard_map.117.mine), channel_id=1, source_target_pairs={{0,16},{16,0},{1,17},{17,1},{2,18},{18,2},{3,19},{19,3},{4,20},{20... | collective-permute-start | bytes 344072 | tf_op jit(solution)/shard_map/ppermute | solution.py:373
  43.3 0.3 collective-permute-start.7
  43.6 2.3 %collective-permute-start.8 = (bf16[64,128]{1,0:T(8,128)(2,1)S(1)}, bf16[64,128]{1,0:T(8,128)(2,1)S(1)}, u32[]{:S(2)}, u32[]{:S(2)}) collective-permute-start(bf16[64,128]{1,0:T(8,128)(2,1)S(1)} %get-tuple-element.56), channel_id=1, source_target_pairs={{0,1},{1,0},{4,8},{5,9},{8,4},{9,5},{12,16},{13,17},{16,12},{17,13... | collective-permute-start | bytes 49160 | tf_op jit(solution)/shard_map/ppermute | solution.py:369
  45.9 0.0 collective-permute-done.7.later_a.recv_a
  45.9 0.8 %collective-permute-done.8.later_b.recv_b = bf16[64,128]{1,0:T(8,128)(2,1)S(1)} collective-permute-done((bf16[64,128]{1,0:T(8,128)(2,1)S(1)}, bf16[64,128]{1,0:T(8,128)(2,1)S(1)}, u32[]{:S(2)}, u32[]{:S(2)}) %collective-permute-start.8) | collective-permute-done | bytes 16416 | tf_op jit(solution)/shard_map/ppermute | solution.py:369
  46.7 2.8 %collective-permute-done.6.other = bf16[448,128]{1,0:T(8,128)(2,1)S(1)} collective-permute-done((bf16[448,128]{1,0:T(8,128)(2,1)S(1)}, bf16[448,128]{1,0:T(8,128)(2,1)S(1)}, u32[]{:S(2)}, u32[]{:S(2)}) %collective-permute-start.6) | collective-permute-done | bytes 114720 | tf_op jit(solution)/shard_map/ppermute | solution.py:373
  49.6 0.6 shard_map.118
  50.2 13.9 %all_to_all.11 = bf16[8,432,128]{2,1,0:T(8,128)(2,1)S(1)} all-to-all(bf16[8,432,128]{2,1,0:T(8,128)(2,1)S(1)} %get-tuple-element.57), channel_id=1, replica_groups=mesh['far'=2,'near'=4,'x'=2,'core'=2] {'near','x'}, dimensions={0} | all-to-all | bytes 1769472 | tf_op jit(solution)/shard_map/all_to_all | solution.py:481
  64.1 2.9 %collective-permute-start.9 = (bf16[2,27,64,128]{3,2,1,0:T(8,128)(2,1)S(1)}, bf16[2,27,64,128]{3,2,1,0:T(8,128)(2,1)S(1)}, u32[]{:S(2)}, u32[]{:S(2)}) collective-permute-start(bf16[2,27,64,128]{3,2,1,0:T(8,128)(2,1)S(1)} %bitcast.14), channel_id=1, source_target_pairs={{0,1},{1,0},{2,3},{3,2},{4,5},{5,4},{6,7},{7,6},{8,9},{9,8},{10,11... | collective-permute-start | bytes 2654216 | tf_op jit(solution)/shard_map/ppermute | solution.py:377
  67.0 0.0 copy-done.1
  67.0 1.8 %shard_map.121 = bf16[512,128]{1,0:T(8,128)(2,1)} custom-call(s32[1]{0:T(128)} %bitcast.1.parity, f32[27,128]{1,0:T(8,128)S(1)} %get-tuple-element.35.rule, bf16[512,128]{1,0:T(8,128)(2,1)S(1)} %get-tuple-element.64.grad_one, bf16[64,128]{1,0:T(8,128)(2,1)S(1)} %collective-permute-done.7.later_a.recv_a, ...), custom_call_target="tpu_custom_call" | custom-call | flops 452984832 | bytes 4000000 | tf_op jit(solution)/shard_map/pallas_call | solution.py:484
  68.8 1.3 %shard_map.119 = (f32[2,27,64,128]{3,2,1,0:T(8,128)}, f32[2,27,64,128]{3,2,1,0:T(8,128)}) custom-call(s32[1]{0:T(128)} %bitcast.core, bf16[2,27,64,128]{3,2,1,0:T(8,128)(2,1)S(1)} %bitcast.15), custom_call_target="tpu_custom_call" | custom-call | bytes 4000000 | tf_op jit(solution)/shard_map/pallas_call | solution.py:489
  70.1 0.0 collective-permute-done.9.whole
  70.1 1.3 %shard_map.120 = (f32[2,27,64,128]{3,2,1,0:T(8,128)}, f32[2,27,64,128]{3,2,1,0:T(8,128)}) custom-call(s32[1]{0:T(128)S(6)} %sub.3.core, bf16[2,27,64,128]{3,2,1,0:T(8,128)(2,1)S(1)} %collective-permute-done.9.whole, f32[2,27,64,128]{3,2,1,0:T(8,128)} %get-tuple-element.58.one_in, ...), custom_call_target="tpu_custom_call", output_to_operand_aliasing={{0}: (2, {}), {1}: (3, {})} | custom-call | bytes 4000000 | tf_op jit(solution)/shard_map/pallas_call | solution.py:490
  (2 shorter events, 0.0 us)
Async XLA Ops:
  0.6 10.3 %copy-start.7 = (bf16[128,3]{0,1:T(4,128)(2,1)S(1)}, bf16[128,3]{0,1:T(4,128)(2,1)}, u32[]{:S(2)}) copy-start(bf16[128,3]{0,1:T(4,128)(2,1)} %param.13) | copy-start | bytes 2308
  0.6 10.3 %copy-start.6 = (s32[1,1,512]{2,1,0:T(1,128)S(1)}, s32[1,1,512]{2,1,0:T(1,128)}, u32[]{:S(2)}) copy-start(s32[1,1,512]{2,1,0:T(1,128)} %param.9) | copy-start | bytes 6148
  2.6 6.7 %collective-permute-start = (bf16[288,128]{1,0:T(8,128)(2,1)}, bf16[288,128]{1,0:T(8,128)(2,1)S(1)}, u32[]{:S(2)}, u32[]{:S(2)}) collective-permute-start(bf16[288,128]{1,0:T(8,128)(2,1)} %get-tuple-element.38), channel_id=1, source_target_pairs={{0,4},{4,0},{8,12},{12,8},{16,20},{20,16},{24,28},{28,24},{1,5},{5... | collective-permute-start | bytes 221192 | tf_op jit(solution)/shard_map/ppermute | solution.py:359
  4.7 4.6 %collective-permute-start.1 = (bf16[288,128]{1,0:T(8,128)(2,1)}, bf16[288,128]{1,0:T(8,128)(2,1)S(1)}, u32[]{:S(2)}, u32[]{:S(2)}) collective-permute-start(bf16[288,128]{1,0:T(8,128)(2,1)} %get-tuple-element.39), channel_id=1, source_target_pairs={{0,1},{1,0},{4,8},{5,9},{8,4},{9,5},{12,16},{13,17},{16,12},{17,13... | collective-permute-start | bytes 221192 | tf_op jit(solution)/shard_map/ppermute | solution.py:369
  5.7 1.2 %copy-start = (bf16[27,128,128]{2,1,0:T(8,128)(2,1)S(1)}, bf16[27,128,128]{2,1,0:T(8,128)(2,1)}, u32[]{:S(2)}) copy-start(bf16[27,128,128]{2,1,0:T(8,128)(2,1)} %filt.5) | copy-start | bytes 2654212
  6.8 0.9 %copy-start.2 = (bf16[1,1,512,128]{3,2,1,0:T(8,128)(2,1)S(1)}, bf16[1,1,512,128]{3,2,1,0:T(8,128)(2,1)}, u32[]{:S(2)}) copy-start(bf16[1,1,512,128]{3,2,1,0:T(8,128)(2,1)} %param.7) | copy-start | bytes 393220
  7.7 0.7 copy-start.3
  8.4 0.7 copy-start.4
  9.1 1.9 %copy-start.5 = (bf16[27,128,128]{2,1,0:T(8,128)(2,1)S(1)}, bf16[27,128,128]{2,1,0:T(8,128)(2,1)}, u32[]{:S(2)}) copy-start(bf16[27,128,128]{2,1,0:T(8,128)(2,1)} %filt.4) | copy-start | bytes 2654212
  13.0 4.8 %collective-permute-start.2 = (bf16[64,128]{1,0:T(8,128)(2,1)S(1)}, bf16[64,128]{1,0:T(8,128)(2,1)S(1)}, u32[]{:S(2)}, u32[]{:S(2)}) collective-permute-start(bf16[64,128]{1,0:T(8,128)(2,1)S(1)} %get-tuple-element.45), channel_id=1, source_target_pairs={{0,4},{4,0},{8,12},{12,8},{16,20},{20,16},{24,28},{28,24},{1,5},{5... | collective-permute-start | bytes 49160 | tf_op jit(solution)/shard_map/ppermute | solution.py:359
  14.5 3.2 %collective-permute-start.3 = (bf16[64,128]{1,0:T(8,128)(2,1)S(1)}, bf16[64,128]{1,0:T(8,128)(2,1)S(1)}, u32[]{:S(2)}, u32[]{:S(2)}) collective-permute-start(bf16[64,128]{1,0:T(8,128)(2,1)S(1)} %get-tuple-element.46), channel_id=1, source_target_pairs={{0,1},{1,0},{4,8},{5,9},{8,4},{9,5},{12,16},{13,17},{16,12},{17,13... | collective-permute-start | bytes 49160 | tf_op jit(solution)/shard_map/ppermute | solution.py:369
  17.7 5.0 %collective-permute-start.5 = (bf16[28,64,128]{2,1,0:T(8,128)(2,1)S(1)}, bf16[28,64,128]{2,1,0:T(8,128)(2,1)S(1)}, u32[]{:S(2)}, u32[]{:S(2)}) collective-permute-start(bf16[28,64,128]{2,1,0:T(8,128)(2,1)S(1)} %get-tuple-element.54), channel_id=1, source_target_pairs={{0,1},{1,0},{2,3},{3,2},{4,5},{5,4},{6,7},{7,6},{8,9},{9,8},{10,11... | collective-permute-start | bytes 1376264 | tf_op jit(solution)/shard_map/ppermute | solution.py:377
  20.7 2.0 %collective-permute-start.4 = (bf16[27,64,128]{2,1,0:T(8,128)(2,1)S(1)}, bf16[27,64,128]{2,1,0:T(8,128)(2,1)S(1)}, u32[]{:S(2)}, u32[]{:S(2)}) collective-permute-start(bf16[27,64,128]{2,1,0:T(8,128)(2,1)S(1)} %get-tuple-element.52), channel_id=1, source_target_pairs={{0,1},{1,0},{2,3},{3,2},{4,5},{5,4},{6,7},{7,6},{8,9},{9,8},{10,11... | collective-permute-start | bytes 1327112 | tf_op jit(solution)/shard_map/ppermute | solution.py:377
  41.9 25.2 %copy-start.1 = (bf16[27,128,128]{2,1,0:T(8,128)(2,1)S(1)}, bf16[27,128,128]{2,1,0:T(8,128)(2,1)}, u32[]{:S(2)}) copy-start(bf16[27,128,128]{2,1,0:T(8,128)(2,1)} %filt.5) | copy-start | bytes 2654212
  42.0 7.6 %collective-permute-start.6 = (bf16[448,128]{1,0:T(8,128)(2,1)S(1)}, bf16[448,128]{1,0:T(8,128)(2,1)S(1)}, u32[]{:S(2)}, u32[]{:S(2)}) collective-permute-start(bf16[448,128]{1,0:T(8,128)(2,1)S(1)} %shard_map.117.mine), channel_id=1, source_target_pairs={{0,16},{16,0},{1,17},{17,1},{2,18},{18,2},{3,19},{19,3},{4,20},{20... | collective-permute-start | bytes 344072 | tf_op jit(solution)/shard_map/ppermute | solution.py:373
  43.3 2.6 %collective-permute-start.7 = (bf16[64,128]{1,0:T(8,128)(2,1)S(1)}, bf16[64,128]{1,0:T(8,128)(2,1)S(1)}, u32[]{:S(2)}, u32[]{:S(2)}) collective-permute-start(bf16[64,128]{1,0:T(8,128)(2,1)S(1)} %get-tuple-element.55), channel_id=1, source_target_pairs={{0,4},{4,0},{8,12},{12,8},{16,20},{20,16},{24,28},{28,24},{1,5},{5... | collective-permute-start | bytes 49160 | tf_op jit(solution)/shard_map/ppermute | solution.py:359
  43.6 3.1 %collective-permute-start.8 = (bf16[64,128]{1,0:T(8,128)(2,1)S(1)}, bf16[64,128]{1,0:T(8,128)(2,1)S(1)}, u32[]{:S(2)}, u32[]{:S(2)}) collective-permute-start(bf16[64,128]{1,0:T(8,128)(2,1)S(1)} %get-tuple-element.56), channel_id=1, source_target_pairs={{0,1},{1,0},{4,8},{5,9},{8,4},{9,5},{12,16},{13,17},{16,12},{17,13... | collective-permute-start | bytes 49160 | tf_op jit(solution)/shard_map/ppermute | solution.py:369
  64.1 6.0 %collective-permute-start.9 = (bf16[2,27,64,128]{3,2,1,0:T(8,128)(2,1)S(1)}, bf16[2,27,64,128]{3,2,1,0:T(8,128)(2,1)S(1)}, u32[]{:S(2)}, u32[]{:S(2)}) collective-permute-start(bf16[2,27,64,128]{3,2,1,0:T(8,128)(2,1)S(1)} %bitcast.14), channel_id=1, source_target_pairs={{0,1},{1,0},{2,3},{3,2},{4,5},{5,4},{6,7},{7,6},{8,9},{9,8},{10,11... | collective-permute-start | bytes 2654216 | tf_op jit(solution)/shard_map/ppermute | solution.py:377

commit v7 on v6

--- a/solution.py
+++ b/solution.py
@@ -138,22 +138,18 @@
                 out_ref[row : row + 64, lane : lane + LANES] = cells.reshape(64, LANES).astype(BF16)
 
 
+def shifted_sum(wide):
+    return sum(wide[64 * i : 64 * i + VOX, LANES * i : LANES * (i + 1)] for i in range(3))
+
+
 def forward_sum(win_ref, filt_ref):
-    total = None
-    for i in range(3):
-        filt = filt_ref[TAPS * i : TAPS * (i + 1)].reshape(TAPS * LANES, LANES)
-        term = jnp.dot(win_ref[64 * i : 64 * i + VOX, :], filt, preferred_element_type=F32)
-        total = term if total is None else total + term
-    return total
+    parts = [filt_ref[TAPS * i : TAPS * (i + 1)].reshape(TAPS * LANES, LANES) for i in range(3)]
+    return shifted_sum(jnp.dot(win_ref[...], jnp.concatenate(parts, axis=1), preferred_element_type=F32))
 
 
 def backward_sum(win_ref, filt_ref):
-    total = None
-    for i in range(3):
-        filt = jnp.concatenate([filt_ref[26 - TAPS * i - t] for t in range(TAPS)], axis=1)
-        term = contract(win_ref[64 * i : 64 * i + VOX, :], filt, 1, 1)
-        total = term if total is None else total + term
-    return total
+    parts = [jnp.concatenate([filt_ref[26 - TAPS * i - t] for t in range(TAPS)], axis=1) for i in range(3)]
+    return shifted_sum(contract(win_ref[...], jnp.concatenate(parts, axis=0), 1, 1))
 
 
 def filter_terms(win_ref, grad, core_ref, wide_ref, tiles_ref, mine_ref, away_ref):

time: 71.7 us -> 70.5 us (0.983)
  Pallas kernels: 15.5 us -> 14.4 us
  transfers between devices with their start and end apart: 10 -> 10, of which waited for: 3 -> 3; matrix products, arithmetic and copies ran while one was open for 0% -> 0% of each run, Pallas kernels for 11% -> 10%
where the time goes in v7:
time: 70.5 us; the launch traced here: 70.2 us
  blocking collectives  32.9 us (47%)
  Pallas kernels  14.4 us (20%)
  starting transfers between devices  13.7 us (19%)
  waiting for transfers between devices  5.12 us (7%)
  local copies, waits for them, and re-layouts  3.42 us (5%)
  between operations  0.81 us (1%)
    all_to_all x1, blocking collectives, local(): parts = lax.all_to_all(chunks, ('near', 'x'), 0, 0, tiled=True)  19 us
    all_to_all x1, blocking collectives, local(): whole = lax.all_to_all(copies, ('near', 'x'), 0, 0, tiled=True)  13.9 us
    ppermute x3, starting transfers between devices, swap_b(): return lax.ppermute(value, SPACE + ('core',), pairs)  4.73 us
    ppermute x3, starting transfers between devices, swap_a(): return lax.ppermute(value, SPACE, [(i, i ^ 1) for i in range(length)])  4.01 us
    ppermute x3, starting transfers between devices, core_swap(): return lax.ppermute(value, 'core', [(0, 1), (1, 0)])  3.56 us
    unnamed x16, local copies, waits for them, and re-layouts  3.42 us
    ppermute x1, waiting for transfers between devices, far_swap(): return lax.ppermute(value, 'far', [(0, 1), (1, 0)])  2.84 us
    pallas_call x1, Pallas kernels, local(): call(three_kernel, (BLOCK, TERMS, TERMS, LAYER, LAYER), [SMEM] * 2 + [VME...  2.36 us
  transfers between devices with their start and end apart: 10, of which 3 were waited for; matrix products, arithmetic and copies ran while one was open for 0% of the time, Pallas kernels for 10%

profile of v7, /device:TPU:1, one launch (start us, length us, event | category | flops | bytes accessed | tf_op | source)
XLA Modules:
  0.0 70.2 jit_solution(11319413825487365678)
XLA Ops:
  0.6 0.0 copy-start.7
  0.6 0.0 copy-start.6
  0.7 1.9 %shard_map.111 = (bf16[288,128]{1,0:T(8,128)(2,1)}, bf16[288,128]{1,0:T(8,128)(2,1)}) custom-call(s32[1]{0:T(128)} %bitcast.1.parity, bf16[512,128]{1,0:T(8,128)(2,1)} %bitcast.16, s32[1,512]{1,0:T(1,128)} %bitcast.18, s32[1,27]{1,0:T(1,128)} %bitcast.20), custom_call_target="tpu_custom_call" | custom-call | bytes 4000000 | tf_op jit(solution)/shard_map/pallas_call | solution.py:426
  2.6 2.1 %collective-permute-start = (bf16[288,128]{1,0:T(8,128)(2,1)}, bf16[288,128]{1,0:T(8,128)(2,1)S(1)}, u32[]{:S(2)}, u32[]{:S(2)}) collective-permute-start(bf16[288,128]{1,0:T(8,128)(2,1)} %get-tuple-element.38), channel_id=1, source_target_pairs={{0,4},{4,0},{8,12},{12,8},{16,20},{20,16},{24,28},{28,24},{1,5},{5... | collective-permute-start | bytes 221192 | tf_op jit(solution)/shard_map/ppermute | solution.py:355
  4.7 1.0 %collective-permute-start.1 = (bf16[288,128]{1,0:T(8,128)(2,1)}, bf16[288,128]{1,0:T(8,128)(2,1)S(1)}, u32[]{:S(2)}, u32[]{:S(2)}) collective-permute-start(bf16[288,128]{1,0:T(8,128)(2,1)} %get-tuple-element.39), channel_id=1, source_target_pairs={{0,1},{1,0},{4,8},{5,9},{8,4},{9,5},{12,16},{13,17},{16,12},{17,13... | collective-permute-start | bytes 221192 | tf_op jit(solution)/shard_map/ppermute | solution.py:365
  5.7 0.0 copy-start
  5.7 1.2 %copy-done = bf16[27,128,128]{2,1,0:T(8,128)(2,1)S(1)} copy-done((bf16[27,128,128]{2,1,0:T(8,128)(2,1)S(1)}, bf16[27,128,128]{2,1,0:T(8,128)(2,1)}, u32[]{:S(2)}) %copy-start) | copy-done | bytes 884760
  6.8 0.0 copy-start.2
  6.8 0.9 %copy-done.2 = bf16[1,1,512,128]{3,2,1,0:T(8,128)(2,1)S(1)} copy-done((bf16[1,1,512,128]{3,2,1,0:T(8,128)(2,1)S(1)}, bf16[1,1,512,128]{3,2,1,0:T(8,128)(2,1)}, u32[]{:S(2)}) %copy-start.2) | copy-done | bytes 131096
  7.7 0.0 copy-start.3
  7.7 0.7 copy-done.3
  8.4 0.7 copy-done.4
  9.1 0.0 copy-start.5
  9.1 0.2 shard_map.110
  9.3 0.0 collective-permute-done.recv_a
  9.3 0.0 collective-permute-done.1.recv_b
  9.3 1.4 %shard_map.112 = (bf16[512,128]{1,0:T(8,128)(2,1)S(1)}, bf16[64,128]{1,0:T(8,128)(2,1)S(1)}, bf16[64,128]{1,0:T(8,128)(2,1)S(1)}, f32[512,128]{1,0:T(8,128)S(1)}) custom-call(s32[1]{0:T(128)} %bitcast.1.parity, f32[27,128]{1,0:T(8,128)S(1)} %get-tuple-element.35.rule, bf16[512,128]{1,0:T(8,128)(2,1)S(1)} %get-tuple-element.36.masked, ...), custom_call_target="tpu_custom_call" | custom-call | flops 452984832 | bytes 4000000 | tf_op jit(solution)/shard_map/pallas_call | solution.py:437
  10.7 0.0 copy-done.7
  10.7 0.0 copy-done.6
  10.7 0.0 copy-done.5
  10.7 1.7 %shard_map.113 = (bf16[640,1152]{1,0:T(8,128)(2,1)S(1)}, bf16[512,128]{1,0:T(8,128)(2,1)S(1)}, f32[8,128]{1,0:T(8,128)S(1)}, bf16[64,128]{1,0:T(8,128)(2,1)S(1)}, bf16[64,128]{1,0:T(8,128)(2,1)S(1)}) custom-call(s32[1]{0:T(128)} %bitcast.1.parity, f32[27,128]{1,0:T(8,128)S(1)} %get-tuple-element.35.rule, bf16[512,128]{1,0:T(8,128)(2,1)S(1)} %get-tuple-element.41.act_one, ...), custom_call_target="tpu_custom_call" | custom-call | flops 452984832 | bytes 4000000 | tf_op jit(solution)/shard_map/pallas_call | solution.py:444
  12.4 1.6 %collective-permute-start.2 = (bf16[64,128]{1,0:T(8,128)(2,1)S(1)}, bf16[64,128]{1,0:T(8,128)(2,1)S(1)}, u32[]{:S(2)}, u32[]{:S(2)}) collective-permute-start(bf16[64,128]{1,0:T(8,128)(2,1)S(1)} %get-tuple-element.45), channel_id=1, source_target_pairs={{0,4},{4,0},{8,12},{12,8},{16,20},{20,16},{24,28},{28,24},{1,5},{5... | collective-permute-start | bytes 49160 | tf_op jit(solution)/shard_map/ppermute | solution.py:355
  14.0 1.5 %collective-permute-start.3 = (bf16[64,128]{1,0:T(8,128)(2,1)S(1)}, bf16[64,128]{1,0:T(8,128)(2,1)S(1)}, u32[]{:S(2)}, u32[]{:S(2)}) collective-permute-start(bf16[64,128]{1,0:T(8,128)(2,1)S(1)} %get-tuple-element.46), channel_id=1, source_target_pairs={{0,1},{1,0},{4,8},{5,9},{8,4},{9,5},{12,16},{13,17},{16,12},{17,13... | collective-permute-start | bytes 49160 | tf_op jit(solution)/shard_map/ppermute | solution.py:365
  15.5 1.6 %shard_map.114 = (bf16[28,64,128]{2,1,0:T(8,128)(2,1)S(1)}, bf16[28,64,128]{2,1,0:T(8,128)(2,1)S(1)}, bf16[640,1152]{1,0:T(8,128)(2,1)S(1)}) custom-call(s32[1]{0:T(128)} %bitcast.core, s32[1]{0:T(128)} %bitcast.1.parity, f32[27,128]{1,0:T(8,128)S(1)} %get-tuple-element.35.rule, bf16[512,128]{1,0:T(8,128)(2,1)S(1)} %get-tuple-element.36.masked, ...), custom_call_target="tpu_custom_call" | custom-call | flops 452984832 | bytes 4000000 | tf_op jit(solution)/shard_map/pallas_call | solution.py:451
  17.2 0.1 collective-permute-start.5
  17.3 0.0 collective-permute-done.2.recv_a
  17.3 0.0 collective-permute-done.3.recv_b
  17.3 2.4 %shard_map.115 = (bf16[512,128]{1,0:T(8,128)(2,1)S(1)}, bf16[27,64,128]{2,1,0:T(8,128)(2,1)S(1)}, bf16[27,64,128]{2,1,0:T(8,128)(2,1)S(1)}, bf16[64,128]{1,0:T(8,128)(2,1)S(1)}, bf16[64,128]{1,0:T(8,128)(2,1)S(1)}) custom-call(s32[1]{0:T(128)} %bitcast.core, s32[1]{0:T(128)} %bitcast.1.parity, f32[27,128]{1,0:T(8,128)S(1)} %get-tuple-element.35.rule, ...), custom_call_target="tpu_custom_call" | custom-call | flops 905969664 | bytes 4000000 | tf_op jit(solution)/shard_map/pallas_call | solution.py:455
  19.6 0.5 collective-permute-start.4
  20.2 1.4 %collective-permute-done.4.one_other = bf16[27,64,128]{2,1,0:T(8,128)(2,1)S(1)} collective-permute-done((bf16[27,64,128]{2,1,0:T(8,128)(2,1)S(1)}, bf16[27,64,128]{2,1,0:T(8,128)(2,1)S(1)}, u32[]{:S(2)}, u32[]{:S(2)}) %collective-permute-start.4) | collective-permute-done | bytes 442400 | tf_op jit(solution)/shard_map/ppermute | solution.py:373
  21.6 0.0 collective-permute-done.5.two_other
  21.6 0.2 shard_map.116
  21.8 19.0 %all_to_all.10.parts = bf16[8,448,128]{2,1,0:T(8,128)(2,1)S(1)} all-to-all(bf16[8,448,128]{2,1,0:T(8,128)(2,1)S(1)} %shard_map.116), channel_id=1, replica_groups=mesh['far'=2,'near'=4,'x'=2,'core'=2] {'near','x'}, dimensions={0} | all-to-all | bytes 1835008 | tf_op jit(solution)/shard_map/all_to_all | solution.py:468
  40.8 0.1 shard_map.117.mine
  40.9 1.4 %collective-permute-start.6 = (bf16[448,128]{1,0:T(8,128)(2,1)S(1)}, bf16[448,128]{1,0:T(8,128)(2,1)S(1)}, u32[]{:S(2)}, u32[]{:S(2)}) collective-permute-start(bf16[448,128]{1,0:T(8,128)(2,1)S(1)} %shard_map.117.mine), channel_id=1, source_target_pairs={{0,16},{16,0},{1,17},{17,1},{2,18},{18,2},{3,19},{19,3},{4,20},{20... | collective-permute-start | bytes 344072 | tf_op jit(solution)/shard_map/ppermute | solution.py:369
  42.3 0.3 collective-permute-start.7
  42.6 2.3 %collective-permute-start.8 = (bf16[64,128]{1,0:T(8,128)(2,1)S(1)}, bf16[64,128]{1,0:T(8,128)(2,1)S(1)}, u32[]{:S(2)}, u32[]{:S(2)}) collective-permute-start(bf16[64,128]{1,0:T(8,128)(2,1)S(1)} %get-tuple-element.56), channel_id=1, source_target_pairs={{0,1},{1,0},{4,8},{5,9},{8,4},{9,5},{12,16},{13,17},{16,12},{17,13... | collective-permute-start | bytes 49160 | tf_op jit(solution)/shard_map/ppermute | solution.py:365
  44.8 0.0 collective-permute-done.7.later_a.recv_a
  44.9 0.8 %collective-permute-done.8.later_b.recv_b = bf16[64,128]{1,0:T(8,128)(2,1)S(1)} collective-permute-done((bf16[64,128]{1,0:T(8,128)(2,1)S(1)}, bf16[64,128]{1,0:T(8,128)(2,1)S(1)}, u32[]{:S(2)}, u32[]{:S(2)}) %collective-permute-start.8) | collective-permute-done | bytes 16416 | tf_op jit(solution)/shard_map/ppermute | solution.py:365
  45.7 2.8 %collective-permute-done.6.other = bf16[448,128]{1,0:T(8,128)(2,1)S(1)} collective-permute-done((bf16[448,128]{1,0:T(8,128)(2,1)S(1)}, bf16[448,128]{1,0:T(8,128)(2,1)S(1)}, u32[]{:S(2)}, u32[]{:S(2)}) %collective-permute-start.6) | collective-permute-done | bytes 114720 | tf_op jit(solution)/shard_map/ppermute | solution.py:369
  48.5 0.6 shard_map.118
  49.1 13.9 %all_to_all.11 = bf16[8,432,128]{2,1,0:T(8,128)(2,1)S(1)} all-to-all(bf16[8,432,128]{2,1,0:T(8,128)(2,1)S(1)} %get-tuple-element.57), channel_id=1, replica_groups=mesh['far'=2,'near'=4,'x'=2,'core'=2] {'near','x'}, dimensions={0} | all-to-all | bytes 1769472 | tf_op jit(solution)/shard_map/all_to_all | solution.py:477
  63.0 2.9 %collective-permute-start.9 = (bf16[2,27,64,128]{3,2,1,0:T(8,128)(2,1)S(1)}, bf16[2,27,64,128]{3,2,1,0:T(8,128)(2,1)S(1)}, u32[]{:S(2)}, u32[]{:S(2)}) collective-permute-start(bf16[2,27,64,128]{3,2,1,0:T(8,128)(2,1)S(1)} %bitcast.14), channel_id=1, source_target_pairs={{0,1},{1,0},{2,3},{3,2},{4,5},{5,4},{6,7},{7,6},{8,9},{9,8},{10,11... | collective-permute-start | bytes 2654216 | tf_op jit(solution)/shard_map/ppermute | solution.py:373
  66.0 0.0 copy-done.1
  66.0 1.7 %shard_map.121 = bf16[512,128]{1,0:T(8,128)(2,1)} custom-call(s32[1]{0:T(128)} %bitcast.1.parity, f32[27,128]{1,0:T(8,128)S(1)} %get-tuple-element.35.rule, bf16[512,128]{1,0:T(8,128)(2,1)S(1)} %get-tuple-element.64.grad_one, bf16[64,128]{1,0:T(8,128)(2,1)S(1)} %collective-permute-done.7.later_a.recv_a, ...), custom_call_target="tpu_custom_call" | custom-call | flops 452984832 | bytes 4000000 | tf_op jit(solution)/shard_map/pallas_call | solution.py:480
  67.7 1.3 %shard_map.119 = (f32[2,27,64,128]{3,2,1,0:T(8,128)}, f32[2,27,64,128]{3,2,1,0:T(8,128)}) custom-call(s32[1]{0:T(128)} %bitcast.core, bf16[2,27,64,128]{3,2,1,0:T(8,128)(2,1)S(1)} %bitcast.15), custom_call_target="tpu_custom_call" | custom-call | bytes 4000000 | tf_op jit(solution)/shard_map/pallas_call | solution.py:485
  69.0 0.0 collective-permute-done.9.whole
  69.0 1.3 %shard_map.120 = (f32[2,27,64,128]{3,2,1,0:T(8,128)}, f32[2,27,64,128]{3,2,1,0:T(8,128)}) custom-call(s32[1]{0:T(128)S(6)} %sub.3.core, bf16[2,27,64,128]{3,2,1,0:T(8,128)(2,1)S(1)} %collective-permute-done.9.whole, f32[2,27,64,128]{3,2,1,0:T(8,128)} %get-tuple-element.58.one_in, ...), custom_call_target="tpu_custom_call", output_to_operand_aliasing={{0}: (2, {}), {1}: (3, {})} | custom-call | bytes 4000000 | tf_op jit(solution)/shard_map/pallas_call | solution.py:486
  (2 shorter events, 0.0 us)
Async XLA Ops:
  0.6 10.1 %copy-start.7 = (bf16[128,3]{0,1:T(4,128)(2,1)S(1)}, bf16[128,3]{0,1:T(4,128)(2,1)}, u32[]{:S(2)}) copy-start(bf16[128,3]{0,1:T(4,128)(2,1)} %param.13) | copy-start | bytes 2308
  0.6 10.1 %copy-start.6 = (s32[1,1,512]{2,1,0:T(1,128)S(1)}, s32[1,1,512]{2,1,0:T(1,128)}, u32[]{:S(2)}) copy-start(s32[1,1,512]{2,1,0:T(1,128)} %param.9) | copy-start | bytes 6148
  2.6 6.7 %collective-permute-start = (bf16[288,128]{1,0:T(8,128)(2,1)}, bf16[288,128]{1,0:T(8,128)(2,1)S(1)}, u32[]{:S(2)}, u32[]{:S(2)}) collective-permute-start(bf16[288,128]{1,0:T(8,128)(2,1)} %get-tuple-element.38), channel_id=1, source_target_pairs={{0,4},{4,0},{8,12},{12,8},{16,20},{20,16},{24,28},{28,24},{1,5},{5... | collective-permute-start | bytes 221192 | tf_op jit(solution)/shard_map/ppermute | solution.py:355
  4.7 4.6 %collective-permute-start.1 = (bf16[288,128]{1,0:T(8,128)(2,1)}, bf16[288,128]{1,0:T(8,128)(2,1)S(1)}, u32[]{:S(2)}, u32[]{:S(2)}) collective-permute-start(bf16[288,128]{1,0:T(8,128)(2,1)} %get-tuple-element.39), channel_id=1, source_target_pairs={{0,1},{1,0},{4,8},{5,9},{8,4},{9,5},{12,16},{13,17},{16,12},{17,13... | collective-permute-start | bytes 221192 | tf_op jit(solution)/shard_map/ppermute | solution.py:365
  5.7 1.2 %copy-start = (bf16[27,128,128]{2,1,0:T(8,128)(2,1)S(1)}, bf16[27,128,128]{2,1,0:T(8,128)(2,1)}, u32[]{:S(2)}) copy-start(bf16[27,128,128]{2,1,0:T(8,128)(2,1)} %filt.5) | copy-start | bytes 2654212
  6.8 0.9 %copy-start.2 = (bf16[1,1,512,128]{3,2,1,0:T(8,128)(2,1)S(1)}, bf16[1,1,512,128]{3,2,1,0:T(8,128)(2,1)}, u32[]{:S(2)}) copy-start(bf16[1,1,512,128]{3,2,1,0:T(8,128)(2,1)} %param.7) | copy-start | bytes 393220
  7.7 0.7 copy-start.3
  8.4 0.7 copy-start.4
  9.1 1.7 %copy-start.5 = (bf16[27,128,128]{2,1,0:T(8,128)(2,1)S(1)}, bf16[27,128,128]{2,1,0:T(8,128)(2,1)}, u32[]{:S(2)}) copy-start(bf16[27,128,128]{2,1,0:T(8,128)(2,1)} %filt.4) | copy-start | bytes 2654212
  12.4 4.8 %collective-permute-start.2 = (bf16[64,128]{1,0:T(8,128)(2,1)S(1)}, bf16[64,128]{1,0:T(8,128)(2,1)S(1)}, u32[]{:S(2)}, u32[]{:S(2)}) collective-permute-start(bf16[64,128]{1,0:T(8,128)(2,1)S(1)} %get-tuple-element.45), channel_id=1, source_target_pairs={{0,4},{4,0},{8,12},{12,8},{16,20},{20,16},{24,28},{28,24},{1,5},{5... | collective-permute-start | bytes 49160 | tf_op jit(solution)/shard_map/ppermute | solution.py:355
  14.0 3.2 %collective-permute-start.3 = (bf16[64,128]{1,0:T(8,128)(2,1)S(1)}, bf16[64,128]{1,0:T(8,128)(2,1)S(1)}, u32[]{:S(2)}, u32[]{:S(2)}) collective-permute-start(bf16[64,128]{1,0:T(8,128)(2,1)S(1)} %get-tuple-element.46), channel_id=1, source_target_pairs={{0,1},{1,0},{4,8},{5,9},{8,4},{9,5},{12,16},{13,17},{16,12},{17,13... | collective-permute-start | bytes 49160 | tf_op jit(solution)/shard_map/ppermute | solution.py:365
  17.2 4.4 %collective-permute-start.5 = (bf16[28,64,128]{2,1,0:T(8,128)(2,1)S(1)}, bf16[28,64,128]{2,1,0:T(8,128)(2,1)S(1)}, u32[]{:S(2)}, u32[]{:S(2)}) collective-permute-start(bf16[28,64,128]{2,1,0:T(8,128)(2,1)S(1)} %get-tuple-element.54), channel_id=1, source_target_pairs={{0,1},{1,0},{2,3},{3,2},{4,5},{5,4},{6,7},{7,6},{8,9},{9,8},{10,11... | collective-permute-start | bytes 1376264 | tf_op jit(solution)/shard_map/ppermute | solution.py:373
  19.6 2.0 %collective-permute-start.4 = (bf16[27,64,128]{2,1,0:T(8,128)(2,1)S(1)}, bf16[27,64,128]{2,1,0:T(8,128)(2,1)S(1)}, u32[]{:S(2)}, u32[]{:S(2)}) collective-permute-start(bf16[27,64,128]{2,1,0:T(8,128)(2,1)S(1)} %get-tuple-element.52), channel_id=1, source_target_pairs={{0,1},{1,0},{2,3},{3,2},{4,5},{5,4},{6,7},{7,6},{8,9},{9,8},{10,11... | collective-permute-start | bytes 1327112 | tf_op jit(solution)/shard_map/ppermute | solution.py:373
  40.8 25.2 %copy-start.1 = (bf16[27,128,128]{2,1,0:T(8,128)(2,1)S(1)}, bf16[27,128,128]{2,1,0:T(8,128)(2,1)}, u32[]{:S(2)}) copy-start(bf16[27,128,128]{2,1,0:T(8,128)(2,1)} %filt.5) | copy-start | bytes 2654212
  40.9 7.6 %collective-permute-start.6 = (bf16[448,128]{1,0:T(8,128)(2,1)S(1)}, bf16[448,128]{1,0:T(8,128)(2,1)S(1)}, u32[]{:S(2)}, u32[]{:S(2)}) collective-permute-start(bf16[448,128]{1,0:T(8,128)(2,1)S(1)} %shard_map.117.mine), channel_id=1, source_target_pairs={{0,16},{16,0},{1,17},{17,1},{2,18},{18,2},{3,19},{19,3},{4,20},{20... | collective-permute-start | bytes 344072 | tf_op jit(solution)/shard_map/ppermute | solution.py:369
  42.3 2.6 %collective-permute-start.7 = (bf16[64,128]{1,0:T(8,128)(2,1)S(1)}, bf16[64,128]{1,0:T(8,128)(2,1)S(1)}, u32[]{:S(2)}, u32[]{:S(2)}) collective-permute-start(bf16[64,128]{1,0:T(8,128)(2,1)S(1)} %get-tuple-element.55), channel_id=1, source_target_pairs={{0,4},{4,0},{8,12},{12,8},{16,20},{20,16},{24,28},{28,24},{1,5},{5... | collective-permute-start | bytes 49160 | tf_op jit(solution)/shard_map/ppermute | solution.py:355
  42.6 3.1 %collective-permute-start.8 = (bf16[64,128]{1,0:T(8,128)(2,1)S(1)}, bf16[64,128]{1,0:T(8,128)(2,1)S(1)}, u32[]{:S(2)}, u32[]{:S(2)}) collective-permute-start(bf16[64,128]{1,0:T(8,128)(2,1)S(1)} %get-tuple-element.56), channel_id=1, source_target_pairs={{0,1},{1,0},{4,8},{5,9},{8,4},{9,5},{12,16},{13,17},{16,12},{17,13... | collective-permute-start | bytes 49160 | tf_op jit(solution)/shard_map/ppermute | solution.py:365
  63.0 5.9 %collective-permute-start.9 = (bf16[2,27,64,128]{3,2,1,0:T(8,128)(2,1)S(1)}, bf16[2,27,64,128]{3,2,1,0:T(8,128)(2,1)S(1)}, u32[]{:S(2)}, u32[]{:S(2)}) collective-permute-start(bf16[2,27,64,128]{3,2,1,0:T(8,128)(2,1)S(1)} %bitcast.14), channel_id=1, source_target_pairs={{0,1},{1,0},{2,3},{3,2},{4,5},{5,4},{6,7},{7,6},{8,9},{9,8},{10,11... | collective-permute-start | bytes 2654216 | tf_op jit(solution)/shard_map/ppermute | solution.py:373

commit v8 on v7

--- a/solution.py
+++ b/solution.py
@@ -157,7 +157,9 @@
     for i in range(3):
         wide_ref[64 * i : 64 * i + VOX, LANES * i : LANES * (i + 1)] = grad
     for t in range(TAPS):
-        term = contract(win_ref[:, LANES * t : LANES * (t + 1)], wide_ref[...], 0, 0)
+        if t % 9 == 0:
+            terms = contract(win_ref[:, LANES * t : LANES * (t + 9)], wide_ref[...], 0, 0)
+        term = terms[LANES * (t % 9) : LANES * (t % 9 + 1)]
         for i in range(3):
             tile = term[:, LANES * i : LANES * (i + 1)].astype(BF16)
             at = 2 * (TAPS * i + t)

time: 70.5 us -> 70.4 us (level)
  no operation moved by 1% of the time
where the time goes in v8:
time: 70.4 us; the launch traced here: 70.1 us
  blocking collectives  32.9 us (47%)
  Pallas kernels  14.1 us (20%)
  starting transfers between devices  13.7 us (19%)
  waiting for transfers between devices  5.12 us (7%)
  local copies, waits for them, and re-layouts  3.42 us (5%)
  between operations  0.81 us (1%)
    all_to_all x1, blocking collectives, local(): parts = lax.all_to_all(chunks, ('near', 'x'), 0, 0, tiled=True)  19 us
    all_to_all x1, blocking collectives, local(): whole = lax.all_to_all(copies, ('near', 'x'), 0, 0, tiled=True)  13.9 us
    ppermute x3, starting transfers between devices, swap_b(): return lax.ppermute(value, SPACE + ('core',), pairs)  4.73 us
    ppermute x3, starting transfers between devices, swap_a(): return lax.ppermute(value, SPACE, [(i, i ^ 1) for i in range(length)])  4.01 us
    ppermute x3, starting transfers between devices, core_swap(): return lax.ppermute(value, 'core', [(0, 1), (1, 0)])  3.55 us
    unnamed x16, local copies, waits for them, and re-layouts  3.42 us
    ppermute x1, waiting for transfers between devices, far_swap(): return lax.ppermute(value, 'far', [(0, 1), (1, 0)])  2.84 us
    pallas_call x1, Pallas kernels, local(): call(three_kernel, (BLOCK, TERMS, TERMS, LAYER, LAYER), [SMEM] * 2 + [VME...  2.21 us
  transfers between devices with their start and end apart: 10, of which 3 were waited for; matrix products, arithmetic and copies ran while one was open for 0% of the time, Pallas kernels for 10%

profile of v8, /device:TPU:1, one launch (start us, length us, event | category | flops | bytes accessed | tf_op | source)
XLA Modules:
  0.0 70.1 jit_solution(17913155804213723960)
XLA Ops:
  0.6 0.0 copy-start.7
  0.6 0.0 copy-start.6
  0.7 1.9 %shard_map.111 = (bf16[288,128]{1,0:T(8,128)(2,1)}, bf16[288,128]{1,0:T(8,128)(2,1)}) custom-call(s32[1]{0:T(128)} %bitcast.1.parity, bf16[512,128]{1,0:T(8,128)(2,1)} %bitcast.16, s32[1,512]{1,0:T(1,128)} %bitcast.18, s32[1,27]{1,0:T(1,128)} %bitcast.20), custom_call_target="tpu_custom_call" | custom-call | bytes 4000000 | tf_op jit(solution)/shard_map/pallas_call | solution.py:428
  2.6 2.1 %collective-permute-start = (bf16[288,128]{1,0:T(8,128)(2,1)}, bf16[288,128]{1,0:T(8,128)(2,1)S(1)}, u32[]{:S(2)}, u32[]{:S(2)}) collective-permute-start(bf16[288,128]{1,0:T(8,128)(2,1)} %get-tuple-element.38), channel_id=1, source_target_pairs={{0,4},{4,0},{8,12},{12,8},{16,20},{20,16},{24,28},{28,24},{1,5},{5... | collective-permute-start | bytes 221192 | tf_op jit(solution)/shard_map/ppermute | solution.py:357
  4.7 1.0 %collective-permute-start.1 = (bf16[288,128]{1,0:T(8,128)(2,1)}, bf16[288,128]{1,0:T(8,128)(2,1)S(1)}, u32[]{:S(2)}, u32[]{:S(2)}) collective-permute-start(bf16[288,128]{1,0:T(8,128)(2,1)} %get-tuple-element.39), channel_id=1, source_target_pairs={{0,1},{1,0},{4,8},{5,9},{8,4},{9,5},{12,16},{13,17},{16,12},{17,13... | collective-permute-start | bytes 221192 | tf_op jit(solution)/shard_map/ppermute | solution.py:367
  5.7 0.0 copy-start
  5.7 1.2 %copy-done = bf16[27,128,128]{2,1,0:T(8,128)(2,1)S(1)} copy-done((bf16[27,128,128]{2,1,0:T(8,128)(2,1)S(1)}, bf16[27,128,128]{2,1,0:T(8,128)(2,1)}, u32[]{:S(2)}) %copy-start) | copy-done | bytes 884760
  6.8 0.0 copy-start.2
  6.8 0.9 %copy-done.2 = bf16[1,1,512,128]{3,2,1,0:T(8,128)(2,1)S(1)} copy-done((bf16[1,1,512,128]{3,2,1,0:T(8,128)(2,1)S(1)}, bf16[1,1,512,128]{3,2,1,0:T(8,128)(2,1)}, u32[]{:S(2)}) %copy-start.2) | copy-done | bytes 131096
  7.7 0.0 copy-start.3
  7.7 0.7 copy-done.3
  8.4 0.7 copy-done.4
  9.1 0.0 copy-start.5
  9.1 0.2 shard_map.110
  9.3 0.0 collective-permute-done.recv_a
  9.3 0.0 collective-permute-done.1.recv_b
  9.3 1.4 %shard_map.112 = (bf16[512,128]{1,0:T(8,128)(2,1)S(1)}, bf16[64,128]{1,0:T(8,128)(2,1)S(1)}, bf16[64,128]{1,0:T(8,128)(2,1)S(1)}, f32[512,128]{1,0:T(8,128)S(1)}) custom-call(s32[1]{0:T(128)} %bitcast.1.parity, f32[27,128]{1,0:T(8,128)S(1)} %get-tuple-element.35.rule, bf16[512,128]{1,0:T(8,128)(2,1)S(1)} %get-tuple-element.36.masked, ...), custom_call_target="tpu_custom_call" | custom-call | flops 452984832 | bytes 4000000 | tf_op jit(solution)/shard_map/pallas_call | solution.py:439
  10.7 0.0 copy-done.7
  10.7 0.0 copy-done.6
  10.7 0.0 copy-done.5
  10.7 1.7 %shard_map.113 = (bf16[640,1152]{1,0:T(8,128)(2,1)S(1)}, bf16[512,128]{1,0:T(8,128)(2,1)S(1)}, f32[8,128]{1,0:T(8,128)S(1)}, bf16[64,128]{1,0:T(8,128)(2,1)S(1)}, bf16[64,128]{1,0:T(8,128)(2,1)S(1)}) custom-call(s32[1]{0:T(128)} %bitcast.1.parity, f32[27,128]{1,0:T(8,128)S(1)} %get-tuple-element.35.rule, bf16[512,128]{1,0:T(8,128)(2,1)S(1)} %get-tuple-element.41.act_one, ...), custom_call_target="tpu_custom_call" | custom-call | flops 452984832 | bytes 4000000 | tf_op jit(solution)/shard_map/pallas_call | solution.py:446
  12.4 1.6 %collective-permute-start.2 = (bf16[64,128]{1,0:T(8,128)(2,1)S(1)}, bf16[64,128]{1,0:T(8,128)(2,1)S(1)}, u32[]{:S(2)}, u32[]{:S(2)}) collective-permute-start(bf16[64,128]{1,0:T(8,128)(2,1)S(1)} %get-tuple-element.45), channel_id=1, source_target_pairs={{0,4},{4,0},{8,12},{12,8},{16,20},{20,16},{24,28},{28,24},{1,5},{5... | collective-permute-start | bytes 49160 | tf_op jit(solution)/shard_map/ppermute | solution.py:357
  14.0 1.5 %collective-permute-start.3 = (bf16[64,128]{1,0:T(8,128)(2,1)S(1)}, bf16[64,128]{1,0:T(8,128)(2,1)S(1)}, u32[]{:S(2)}, u32[]{:S(2)}) collective-permute-start(bf16[64,128]{1,0:T(8,128)(2,1)S(1)} %get-tuple-element.46), channel_id=1, source_target_pairs={{0,1},{1,0},{4,8},{5,9},{8,4},{9,5},{12,16},{13,17},{16,12},{17,13... | collective-permute-start | bytes 49160 | tf_op jit(solution)/shard_map/ppermute | solution.py:367
  15.5 1.6 %shard_map.114 = (bf16[28,64,128]{2,1,0:T(8,128)(2,1)S(1)}, bf16[28,64,128]{2,1,0:T(8,128)(2,1)S(1)}, bf16[640,1152]{1,0:T(8,128)(2,1)S(1)}) custom-call(s32[1]{0:T(128)} %bitcast.core, s32[1]{0:T(128)} %bitcast.1.parity, f32[27,128]{1,0:T(8,128)S(1)} %get-tuple-element.35.rule, bf16[512,128]{1,0:T(8,128)(2,1)S(1)} %get-tuple-element.36.masked, ...), custom_call_target="tpu_custom_call" | custom-call | flops 452984832 | bytes 4000000 | tf_op jit(solution)/shard_map/pallas_call | solution.py:453
  17.1 0.1 collective-permute-start.5
  17.2 0.0 collective-permute-done.2.recv_a
  17.2 0.0 collective-permute-done.3.recv_b
  17.2 2.2 %shard_map.115 = (bf16[512,128]{1,0:T(8,128)(2,1)S(1)}, bf16[27,64,128]{2,1,0:T(8,128)(2,1)S(1)}, bf16[27,64,128]{2,1,0:T(8,128)(2,1)S(1)}, bf16[64,128]{1,0:T(8,128)(2,1)S(1)}, bf16[64,128]{1,0:T(8,128)(2,1)S(1)}) custom-call(s32[1]{0:T(128)} %bitcast.core, s32[1]{0:T(128)} %bitcast.1.parity, f32[27,128]{1,0:T(8,128)S(1)} %get-tuple-element.35.rule, ...), custom_call_target="tpu_custom_call" | custom-call | flops 905969664 | bytes 4000000 | tf_op jit(solution)/shard_map/pallas_call | solution.py:457
  19.4 0.5 collective-permute-start.4
  20.0 1.4 %collective-permute-done.4.one_other = bf16[27,64,128]{2,1,0:T(8,128)(2,1)S(1)} collective-permute-done((bf16[27,64,128]{2,1,0:T(8,128)(2,1)S(1)}, bf16[27,64,128]{2,1,0:T(8,128)(2,1)S(1)}, u32[]{:S(2)}, u32[]{:S(2)}) %collective-permute-start.4) | collective-permute-done | bytes 442400 | tf_op jit(solution)/shard_map/ppermute | solution.py:375
  21.4 0.0 collective-permute-done.5.two_other
  21.4 0.2 shard_map.116
  21.6 19.0 %all_to_all.10.parts = bf16[8,448,128]{2,1,0:T(8,128)(2,1)S(1)} all-to-all(bf16[8,448,128]{2,1,0:T(8,128)(2,1)S(1)} %shard_map.116), channel_id=1, replica_groups=mesh['far'=2,'near'=4,'x'=2,'core'=2] {'near','x'}, dimensions={0} | all-to-all | bytes 1835008 | tf_op jit(solution)/shard_map/all_to_all | solution.py:470
  40.7 0.1 shard_map.117.mine
  40.8 1.4 %collective-permute-start.6 = (bf16[448,128]{1,0:T(8,128)(2,1)S(1)}, bf16[448,128]{1,0:T(8,128)(2,1)S(1)}, u32[]{:S(2)}, u32[]{:S(2)}) collective-permute-start(bf16[448,128]{1,0:T(8,128)(2,1)S(1)} %shard_map.117.mine), channel_id=1, source_target_pairs={{0,16},{16,0},{1,17},{17,1},{2,18},{18,2},{3,19},{19,3},{4,20},{20... | collective-permute-start | bytes 344072 | tf_op jit(solution)/shard_map/ppermute | solution.py:371
  42.1 0.3 collective-permute-start.7
  42.4 2.3 %collective-permute-start.8 = (bf16[64,128]{1,0:T(8,128)(2,1)S(1)}, bf16[64,128]{1,0:T(8,128)(2,1)S(1)}, u32[]{:S(2)}, u32[]{:S(2)}) collective-permute-start(bf16[64,128]{1,0:T(8,128)(2,1)S(1)} %get-tuple-element.56), channel_id=1, source_target_pairs={{0,1},{1,0},{4,8},{5,9},{8,4},{9,5},{12,16},{13,17},{16,12},{17,13... | collective-permute-start | bytes 49160 | tf_op jit(solution)/shard_map/ppermute | solution.py:367
  44.7 0.0 collective-permute-done.7.later_a.recv_a
  44.7 0.8 %collective-permute-done.8.later_b.recv_b = bf16[64,128]{1,0:T(8,128)(2,1)S(1)} collective-permute-done((bf16[64,128]{1,0:T(8,128)(2,1)S(1)}, bf16[64,128]{1,0:T(8,128)(2,1)S(1)}, u32[]{:S(2)}, u32[]{:S(2)}) %collective-permute-start.8) | collective-permute-done | bytes 16416 | tf_op jit(solution)/shard_map/ppermute | solution.py:367
  45.5 2.8 %collective-permute-done.6.other = bf16[448,128]{1,0:T(8,128)(2,1)S(1)} collective-permute-done((bf16[448,128]{1,0:T(8,128)(2,1)S(1)}, bf16[448,128]{1,0:T(8,128)(2,1)S(1)}, u32[]{:S(2)}, u32[]{:S(2)}) %collective-permute-start.6) | collective-permute-done | bytes 114720 | tf_op jit(solution)/shard_map/ppermute | solution.py:371
  48.4 0.6 shard_map.118
  49.0 13.9 %all_to_all.11 = bf16[8,432,128]{2,1,0:T(8,128)(2,1)S(1)} all-to-all(bf16[8,432,128]{2,1,0:T(8,128)(2,1)S(1)} %get-tuple-element.57), channel_id=1, replica_groups=mesh['far'=2,'near'=4,'x'=2,'core'=2] {'near','x'}, dimensions={0} | all-to-all | bytes 1769472 | tf_op jit(solution)/shard_map/all_to_all | solution.py:479
  62.9 2.9 %collective-permute-start.9 = (bf16[2,27,64,128]{3,2,1,0:T(8,128)(2,1)S(1)}, bf16[2,27,64,128]{3,2,1,0:T(8,128)(2,1)S(1)}, u32[]{:S(2)}, u32[]{:S(2)}) collective-permute-start(bf16[2,27,64,128]{3,2,1,0:T(8,128)(2,1)S(1)} %bitcast.14), channel_id=1, source_target_pairs={{0,1},{1,0},{2,3},{3,2},{4,5},{5,4},{6,7},{7,6},{8,9},{9,8},{10,11... | collective-permute-start | bytes 2654216 | tf_op jit(solution)/shard_map/ppermute | solution.py:375
  65.8 0.0 copy-done.1
  65.8 1.7 %shard_map.121 = bf16[512,128]{1,0:T(8,128)(2,1)} custom-call(s32[1]{0:T(128)} %bitcast.1.parity, f32[27,128]{1,0:T(8,128)S(1)} %get-tuple-element.35.rule, bf16[512,128]{1,0:T(8,128)(2,1)S(1)} %get-tuple-element.64.grad_one, bf16[64,128]{1,0:T(8,128)(2,1)S(1)} %collective-permute-done.7.later_a.recv_a, ...), custom_call_target="tpu_custom_call" | custom-call | flops 452984832 | bytes 4000000 | tf_op jit(solution)/shard_map/pallas_call | solution.py:482
  67.5 1.3 %shard_map.119 = (f32[2,27,64,128]{3,2,1,0:T(8,128)}, f32[2,27,64,128]{3,2,1,0:T(8,128)}) custom-call(s32[1]{0:T(128)} %bitcast.core, bf16[2,27,64,128]{3,2,1,0:T(8,128)(2,1)S(1)} %bitcast.15), custom_call_target="tpu_custom_call" | custom-call | bytes 4000000 | tf_op jit(solution)/shard_map/pallas_call | solution.py:487
  68.8 0.0 collective-permute-done.9.whole
  68.8 1.3 %shard_map.120 = (f32[2,27,64,128]{3,2,1,0:T(8,128)}, f32[2,27,64,128]{3,2,1,0:T(8,128)}) custom-call(s32[1]{0:T(128)S(6)} %sub.3.core, bf16[2,27,64,128]{3,2,1,0:T(8,128)(2,1)S(1)} %collective-permute-done.9.whole, f32[2,27,64,128]{3,2,1,0:T(8,128)} %get-tuple-element.58.one_in, ...), custom_call_target="tpu_custom_call", output_to_operand_aliasing={{0}: (2, {}), {1}: (3, {})} | custom-call | bytes 4000000 | tf_op jit(solution)/shard_map/pallas_call | solution.py:488
  (2 shorter events, 0.0 us)
Async XLA Ops:
  0.6 10.1 %copy-start.7 = (bf16[128,3]{0,1:T(4,128)(2,1)S(1)}, bf16[128,3]{0,1:T(4,128)(2,1)}, u32[]{:S(2)}) copy-start(bf16[128,3]{0,1:T(4,128)(2,1)} %param.13) | copy-start | bytes 2308
  0.6 10.1 %copy-start.6 = (s32[1,1,512]{2,1,0:T(1,128)S(1)}, s32[1,1,512]{2,1,0:T(1,128)}, u32[]{:S(2)}) copy-start(s32[1,1,512]{2,1,0:T(1,128)} %param.9) | copy-start | bytes 6148
  2.6 6.7 %collective-permute-start = (bf16[288,128]{1,0:T(8,128)(2,1)}, bf16[288,128]{1,0:T(8,128)(2,1)S(1)}, u32[]{:S(2)}, u32[]{:S(2)}) collective-permute-start(bf16[288,128]{1,0:T(8,128)(2,1)} %get-tuple-element.38), channel_id=1, source_target_pairs={{0,4},{4,0},{8,12},{12,8},{16,20},{20,16},{24,28},{28,24},{1,5},{5... | collective-permute-start | bytes 221192 | tf_op jit(solution)/shard_map/ppermute | solution.py:357
  4.7 4.6 %collective-permute-start.1 = (bf16[288,128]{1,0:T(8,128)(2,1)}, bf16[288,128]{1,0:T(8,128)(2,1)S(1)}, u32[]{:S(2)}, u32[]{:S(2)}) collective-permute-start(bf16[288,128]{1,0:T(8,128)(2,1)} %get-tuple-element.39), channel_id=1, source_target_pairs={{0,1},{1,0},{4,8},{5,9},{8,4},{9,5},{12,16},{13,17},{16,12},{17,13... | collective-permute-start | bytes 221192 | tf_op jit(solution)/shard_map/ppermute | solution.py:367
  5.7 1.2 %copy-start = (bf16[27,128,128]{2,1,0:T(8,128)(2,1)S(1)}, bf16[27,128,128]{2,1,0:T(8,128)(2,1)}, u32[]{:S(2)}) copy-start(bf16[27,128,128]{2,1,0:T(8,128)(2,1)} %filt.5) | copy-start | bytes 2654212
  6.8 0.9 %copy-start.2 = (bf16[1,1,512,128]{3,2,1,0:T(8,128)(2,1)S(1)}, bf16[1,1,512,128]{3,2,1,0:T(8,128)(2,1)}, u32[]{:S(2)}) copy-start(bf16[1,1,512,128]{3,2,1,0:T(8,128)(2,1)} %param.7) | copy-start | bytes 393220
  7.7 0.7 copy-start.3
  8.4 0.7 copy-start.4
  9.1 1.7 %copy-start.5 = (bf16[27,128,128]{2,1,0:T(8,128)(2,1)S(1)}, bf16[27,128,128]{2,1,0:T(8,128)(2,1)}, u32[]{:S(2)}) copy-start(bf16[27,128,128]{2,1,0:T(8,128)(2,1)} %filt.4) | copy-start | bytes 2654212
  12.4 4.8 %collective-permute-start.2 = (bf16[64,128]{1,0:T(8,128)(2,1)S(1)}, bf16[64,128]{1,0:T(8,128)(2,1)S(1)}, u32[]{:S(2)}, u32[]{:S(2)}) collective-permute-start(bf16[64,128]{1,0:T(8,128)(2,1)S(1)} %get-tuple-element.45), channel_id=1, source_target_pairs={{0,4},{4,0},{8,12},{12,8},{16,20},{20,16},{24,28},{28,24},{1,5},{5... | collective-permute-start | bytes 49160 | tf_op jit(solution)/shard_map/ppermute | solution.py:357
  14.0 3.2 %collective-permute-start.3 = (bf16[64,128]{1,0:T(8,128)(2,1)S(1)}, bf16[64,128]{1,0:T(8,128)(2,1)S(1)}, u32[]{:S(2)}, u32[]{:S(2)}) collective-permute-start(bf16[64,128]{1,0:T(8,128)(2,1)S(1)} %get-tuple-element.46), channel_id=1, source_target_pairs={{0,1},{1,0},{4,8},{5,9},{8,4},{9,5},{12,16},{13,17},{16,12},{17,13... | collective-permute-start | bytes 49160 | tf_op jit(solution)/shard_map/ppermute | solution.py:367
  17.1 4.3 %collective-permute-start.5 = (bf16[28,64,128]{2,1,0:T(8,128)(2,1)S(1)}, bf16[28,64,128]{2,1,0:T(8,128)(2,1)S(1)}, u32[]{:S(2)}, u32[]{:S(2)}) collective-permute-start(bf16[28,64,128]{2,1,0:T(8,128)(2,1)S(1)} %get-tuple-element.54), channel_id=1, source_target_pairs={{0,1},{1,0},{2,3},{3,2},{4,5},{5,4},{6,7},{7,6},{8,9},{9,8},{10,11... | collective-permute-start | bytes 1376264 | tf_op jit(solution)/shard_map/ppermute | solution.py:375
  19.4 2.0 %collective-permute-start.4 = (bf16[27,64,128]{2,1,0:T(8,128)(2,1)S(1)}, bf16[27,64,128]{2,1,0:T(8,128)(2,1)S(1)}, u32[]{:S(2)}, u32[]{:S(2)}) collective-permute-start(bf16[27,64,128]{2,1,0:T(8,128)(2,1)S(1)} %get-tuple-element.52), channel_id=1, source_target_pairs={{0,1},{1,0},{2,3},{3,2},{4,5},{5,4},{6,7},{7,6},{8,9},{9,8},{10,11... | collective-permute-start | bytes 1327112 | tf_op jit(solution)/shard_map/ppermute | solution.py:375
  40.7 25.2 %copy-start.1 = (bf16[27,128,128]{2,1,0:T(8,128)(2,1)S(1)}, bf16[27,128,128]{2,1,0:T(8,128)(2,1)}, u32[]{:S(2)}) copy-start(bf16[27,128,128]{2,1,0:T(8,128)(2,1)} %filt.5) | copy-start | bytes 2654212
  40.8 7.6 %collective-permute-start.6 = (bf16[448,128]{1,0:T(8,128)(2,1)S(1)}, bf16[448,128]{1,0:T(8,128)(2,1)S(1)}, u32[]{:S(2)}, u32[]{:S(2)}) collective-permute-start(bf16[448,128]{1,0:T(8,128)(2,1)S(1)} %shard_map.117.mine), channel_id=1, source_target_pairs={{0,16},{16,0},{1,17},{17,1},{2,18},{18,2},{3,19},{19,3},{4,20},{20... | collective-permute-start | bytes 344072 | tf_op jit(solution)/shard_map/ppermute | solution.py:371
  42.1 2.6 %collective-permute-start.7 = (bf16[64,128]{1,0:T(8,128)(2,1)S(1)}, bf16[64,128]{1,0:T(8,128)(2,1)S(1)}, u32[]{:S(2)}, u32[]{:S(2)}) collective-permute-start(bf16[64,128]{1,0:T(8,128)(2,1)S(1)} %get-tuple-element.55), channel_id=1, source_target_pairs={{0,4},{4,0},{8,12},{12,8},{16,20},{20,16},{24,28},{28,24},{1,5},{5... | collective-permute-start | bytes 49160 | tf_op jit(solution)/shard_map/ppermute | solution.py:357
  42.4 3.1 %collective-permute-start.8 = (bf16[64,128]{1,0:T(8,128)(2,1)S(1)}, bf16[64,128]{1,0:T(8,128)(2,1)S(1)}, u32[]{:S(2)}, u32[]{:S(2)}) collective-permute-start(bf16[64,128]{1,0:T(8,128)(2,1)S(1)} %get-tuple-element.56), channel_id=1, source_target_pairs={{0,1},{1,0},{4,8},{5,9},{8,4},{9,5},{12,16},{13,17},{16,12},{17,13... | collective-permute-start | bytes 49160 | tf_op jit(solution)/shard_map/ppermute | solution.py:367
  62.9 5.9 %collective-permute-start.9 = (bf16[2,27,64,128]{3,2,1,0:T(8,128)(2,1)S(1)}, bf16[2,27,64,128]{3,2,1,0:T(8,128)(2,1)S(1)}, u32[]{:S(2)}, u32[]{:S(2)}) collective-permute-start(bf16[2,27,64,128]{3,2,1,0:T(8,128)(2,1)S(1)} %bitcast.14), channel_id=1, source_target_pairs={{0,1},{1,0},{2,3},{3,2},{4,5},{5,4},{6,7},{7,6},{8,9},{9,8},{10,11... | collective-permute-start | bytes 2654216 | tf_op jit(solution)/shard_map/ppermute | solution.py:375
